TPU v7x, 32 devices: a whole 2x2x4 slice. The times are simulated.
32 devices in a mesh: mode: 8 (over y, x, core), elem: 4 (over z).
Axes of the slice: x: 2, y: 2, z: 4, core: 2. Of those that a mesh axis runs over, the one named last changes fastest.
Arguments:
- rhs_phys: float32 [128, 12288], P(None, ('elem', 'mode')), may hold values from -6 to 6
- radial_basis: float32 [12, 128, 128], P('elem'), may hold values from -0.5 to 0.5
- axial_basis: float32 [12, 7, 7], P('elem'), may hold values from -2 to 2
- radial_eig: float32 [12, 128], P('elem'), may hold values from 0.25 to 8
- axial_eig: float32 [12, 7], P('elem'), may hold values from 0.25 to 8
- face_stiff: float32 [12, 128, 128], P('elem'), may hold values from -0.5 to 0.5
- face_mass: float32 [12, 128, 128], P('elem'), may hold values from -0.5 to 0.5
- axial_coupling: float32 [12, 2, 7], P('elem'), may hold values from -3 to 3
- face_numbering: int32 [12, 2, 128], P('elem'), may hold values from 0 to 127, each once within a row
- band_panels: float32 [2, 12, 128, 128], P(None, 'elem'), may hold values from -1 to 1
- inverse_panels: float32 [64, 12, 128, 128], P('mode', 'elem'), may hold values from -2 to 2
Outputs:
- pressure: float32 [128, 12288], P('mode', 'elem')
Inputs may be any that keep to these rules, and one draw needn't show every extreme that they name: Each row of face_numbering is a permutation of 0 to 127.
All inputs are finite; a program needn't handle non-finite values.
Results may differ from a plain program's by a relative error of at most 0.0003.
Values sent between devices are 32-bit elements; how exact they have to be, the bound alone decides.
No kernel may reach another device: no remote copies, remote signals or barrier semaphores. Data moves between devices by JAX's collectives and lax.ppermute only.
A program may use at most 64 MiB of HBM per device.

v0:
```python
import math

import jax
import jax.numpy as jnp
from jax import lax
from jax.sharding import PartitionSpec as P

HIGHEST = lax.Precision.HIGHEST


def shifted(block, axis, distance):
    devices = range(lax.axis_size(axis))
    route = [(i - distance, i) for i in devices if i - distance in devices]
    return lax.ppermute(block, axis, route)


def inverse_interior(values, radial_basis, axial_basis, denominator):
    section_one = jnp.einsum("mcjar,jrs->mcjas", values, radial_basis, precision=HIGHEST)
    section_one = jnp.einsum("mcjas,jab->mcjbs", section_one, axial_basis, precision=HIGHEST)
    section_one = section_one / denominator[:, None]
    section_one = jnp.einsum("mcjbs,jrs->mcjbr", section_one, radial_basis, precision=HIGHEST)
    return jnp.einsum("mcjbr,jab->mcjar", section_one, axial_basis, precision=HIGHEST)


def apply_panel(matrix, vector):
    return jnp.einsum("mrs,mcs->mcr", matrix, vector, precision=HIGHEST)


def apply_transposed(matrix, vector):
    return jnp.einsum("mrs,mcr->mcs", matrix, vector, precision=HIGHEST)


def body(
    rhs_phys,
    radial_basis,
    axial_basis,
    radial_eig,
    axial_eig,
    face_stiff,
    face_mass,
    axial_coupling,
    face_numbering,
    band_panels,
    inverse_panels,
):
    planes = rhs_phys.shape[0]
    mode_dev = inverse_panels.shape[0]
    slab_dev = inverse_panels.shape[1]
    radial = inverse_panels.shape[2]
    inner_count = axial_basis.shape[1]
    mode_total = mode_dev * lax.axis_size("mode")
    row_index = lax.broadcasted_iota(jnp.int32, (planes, planes), 0)
    col_index = lax.broadcasted_iota(jnp.int32, (planes, planes), 1)
    phase_index = row_index // 2 * col_index % planes
    angles = phase_index.astype(jnp.float32) * (2.0 * math.pi / planes)
    dft_table = jnp.where(row_index % 2 == 0, jnp.cos(angles), -jnp.sin(angles)) / math.sqrt(planes)
    spectrum = jnp.dot(dft_table, rhs_phys, precision=HIGHEST, preferred_element_type=jnp.float32)
    spectrum = lax.all_to_all(spectrum, "mode", split_axis=0, concat_axis=1, tiled=True)
    fields = spectrum.reshape(mode_dev, 2, slab_dev, inner_count + 1, radial)
    source_in = fields[:, :, :, :inner_count]
    source_bd = fields[:, :, :, inner_count]
    wavenumber = (lax.axis_index("mode") * mode_dev + jnp.arange(mode_dev, dtype=jnp.int32)).astype(
        jnp.float32
    ) / mode_total
    wavenumber_squared = 4.0 * wavenumber * wavenumber
    denominator = (
        axial_eig[None, :, :, None]
        + radial_eig[None, :, None, :]
        + wavenumber_squared[:, None, None, None]
    )
    solved_values = inverse_interior(source_in, radial_basis, axial_basis, denominator)
    onehot = (face_numbering[..., None] == jnp.arange(radial, dtype=jnp.int32)).astype(jnp.float32)
    wave_five = wavenumber_squared[:, None, None, None, None]
    face_sums = jnp.einsum("mcjar,jsa->mcjsr", solved_values, axial_coupling, precision=HIGHEST)
    pushed = jnp.einsum(
        "mcjsr,jrq->mcjsq", face_sums, face_stiff, precision=HIGHEST
    ) + wave_five * jnp.einsum("mcjsr,jrq->mcjsq", face_sums, face_mass, precision=HIGHEST)
    placed = jnp.einsum("mcjsq,jsqp->mcjsp", pushed, onehot, precision=HIGHEST)
    incoming = shifted(placed[:, :, 0, 0], "elem", -1)
    from_right = jnp.concatenate([placed[:, :, 1:, 0], incoming[:, :, None]], axis=2)
    reduced = source_bd - placed[:, :, :, 1] - from_right
    coupling = band_panels[0][None] + wavenumber_squared[:, None, None, None] * band_panels[1][None]
    zero_vec = jnp.zeros((mode_dev, 2, radial), jnp.float32)
    identity_mat = jnp.broadcast_to(jnp.eye(radial, dtype=jnp.float32), (mode_dev, radial, radial))

    def forward(start_vec):
        output_values = []
        current = start_vec
        for slab_index in range(slab_dev):
            inner_term = reduced[:, :, slab_index] - apply_panel(coupling[:, slab_index], current)
            current = apply_panel(inverse_panels[:, slab_index], inner_term)
            output_values.append(current)
        return output_values

    def backward(start_vec, forward_vals):
        output_values = [None] * slab_dev
        current = start_vec
        for slab_index in reversed(range(slab_dev)):
            solution = forward_vals[slab_index] - apply_panel(
                inverse_panels[:, slab_index], current
            )
            output_values[slab_index] = solution
            current = apply_transposed(coupling[:, slab_index], solution)
        return (output_values, current)

    forward_map = identity_mat
    for slab_index in range(slab_dev):
        banded = jnp.einsum("mrs,mst->mrt", coupling[:, slab_index], forward_map, precision=HIGHEST)
        forward_map = -jnp.einsum(
            "mrs,mst->mrt", inverse_panels[:, slab_index], banded, precision=HIGHEST
        )
    forward_offset = forward(zero_vec)[-1]

    def forward_round(turn_index, carried):
        return shifted(apply_panel(forward_map, carried) + forward_offset, "elem", 1)

    forward_start = lax.fori_loop(0, lax.axis_size("elem") - 1, forward_round, zero_vec)
    forward_vals = forward(forward_start)
    backward_map = identity_mat
    for slab_index in reversed(range(slab_dev)):
        solved_map = jnp.einsum(
            "mrs,mst->mrt", inverse_panels[:, slab_index], backward_map, precision=HIGHEST
        )
        backward_map = -jnp.einsum(
            "mrs,mrt->mst", coupling[:, slab_index], solved_map, precision=HIGHEST
        )
    backward_offset = backward(zero_vec, forward_vals)[1]

    def backward_round(turn_index, carried):
        return shifted(apply_panel(backward_map, carried) + backward_offset, "elem", -1)

    backward_start = lax.fori_loop(0, lax.axis_size("elem") - 1, backward_round, zero_vec)
    back_vals = backward(backward_start, forward_vals)[0]
    interface = jnp.stack(back_vals, axis=2)
    before = shifted(interface[:, :, -1], "elem", 1)
    previous = jnp.concatenate([before[:, :, None], interface[:, :, :-1]], axis=2)
    face_vals = jnp.stack([previous, interface], axis=3)
    local_face = jnp.einsum("mcjsp,jsqp->mcjsq", face_vals, onehot, precision=HIGHEST)
    lifted = jnp.einsum(
        "jrq,mcjsq->mcjsr", face_stiff, local_face, precision=HIGHEST
    ) + wave_five * jnp.einsum("jrq,mcjsq->mcjsr", face_mass, local_face, precision=HIGHEST)
    spread = jnp.einsum("mcjsr,jsa->mcjar", lifted, axial_coupling, precision=HIGHEST)
    interior_values = solved_values - inverse_interior(
        spread, radial_basis, axial_basis, denominator
    )
    assembled = jnp.concatenate([interior_values, interface[:, :, :, None]], axis=3)
    return assembled.reshape(2 * mode_dev, slab_dev * (inner_count + 1) * radial)


def solution(mesh):
    placed = (
        P(None, ("elem", "mode")),
        P("elem", None, None),
        P("elem", None, None),
        P("elem", None),
        P("elem", None),
        P("elem", None, None),
        P("elem", None, None),
        P("elem", None, None),
        P("elem", None, None),
        P(None, "elem", None, None),
        P("mode", "elem", None, None),
    )
    return jax.shard_map(
        body, mesh=mesh, in_specs=placed, out_specs=P("mode", "elem"), check_vma=False
    )
```

profile of v0, /device:TPU:0, one launch (start us, length us, event | category | flops | bytes accessed | tf_op | source)
XLA Modules:
  0.0 123.7 jit_solution(1687513140092601049)
XLA Ops:
  0.0 2.3 %fusion.89 = f32[128,384]{1,0:T(8,128)} fusion(f32[128,384]{1,0:T(8,128)} %param.15, s32[128]{0:T(128)S(1)} %get-tuple-element.77, s32[128]{0:T(128)S(1)} %get-tuple-element.79, s32[128]{0:T(128)S(1)} %get-tuple-element.78, s32[128]{0:T(128)S(1)} %get-tuple-element.80, pred[128]{0:T(512)(128)(4,1)S(1)} %get-tuple-element.75, ...), kind=kOutput, calls=%fused_computation.127 | convolution fusion | flops 75825152 | bytes 395520 | tf_op jit(solution)/shard_map/dot_general | solution.py:57
  2.4 5.2 %all-to-all-start = ((f32[8,16,384]{2,1,0:T(8,128)}), f32[8,16,384]{2,1,0:T(8,128)S(1)}, u32[]{:S(2)}, u32[]{:S(2)}) async-start(f32[8,16,384]{2,1,0:T(8,128)} %bitcast), calls=%async_computation | async-start | bytes 393216 | tf_op jit(solution)/shard_map/all_to_all | solution.py:58
  12.9 2.0 %fusion.39 = f32[8,128,128]{1,2,0:T(8,128)S(1)} fusion(f32[8,3,128,128]{3,2,0,1:T(8,128)S(1)} %multiply_add_fusion, f32[128,128]{0,1:T(8,128)} %fusion.96), kind=kOutput, calls=%fused_computation.71 | convolution fusion | flops 201326592 | bytes 1114112 | tf_op jit(solution)/shard_map/mrs,mst->mrt/dot_general | solution.py:108
  15.0 2.0 %fusion.11 = f32[8,128,128]{2,1,0:T(8,128)} fusion(f32[8,3,128,128]{3,2,1,0:T(8,128)S(1)} %copy-done.1, f32[128,128]{0,1:T(8,128)S(1)} %copy-done.7), kind=kOutput, calls=%fused_computation.43 | convolution fusion | flops 201326592 | bytes 1114112 | tf_op jit(solution)/shard_map/mrs,mst->mrt/dot_general | solution.py:121
  21.9 2.0 %fusion = f32[8,128,128]{1,2,0:T(8,128)} fusion(f32[8,128,128]{1,2,0:T(8,128)S(1)} %fusion.47, f32[8,3,128,128]{3,2,1,0:T(8,128)S(1)} %copy-done.1), kind=kOutput, calls=%fused_computation.7 | convolution fusion | flops 201457664 | bytes 1572864 | tf_op jit(solution)/shard_map/mrs,mst->mrt/dot_general | solution.py:109
  23.9 2.1 %copy.51 = f32[8,128,128]{2,1,0:T(8,128)} copy(f32[8,128,128]{1,2,0:T(8,128)} %fusion) | data formatting | bytes 1048576 | tf_op jit(solution)/shard_map/while | solution.py:117
  25.9 2.0 %convolution_negate_fusion.2 = f32[8,128,128]{2,1,0:T(8,128)S(1)} fusion(f32[8,128,128]{2,1,0:T(8,128)} %fusion.11, f32[8,3,128,128]{3,2,0,1:T(8,128)S(1)} %multiply_add_fusion), kind=kOutput, calls=%fused_computation.5 | convolution fusion | flops 201457664 | bytes 1572864 | tf_op jit(solution)/shard_map/mrs,mrt->mst/dot_general | solution.py:124
  31.1 1.8 %convolution_negate_fusion = f32[8,128,128]{2,1,0:T(8,128)} fusion(f32[8,128,128]{2,1,0:T(8,128)S(1)} %fusion.29, f32[8,3,128,128]{3,2,0,1:T(8,128)S(1)} %multiply_add_fusion), kind=kOutput, calls=%fused_computation.3 | convolution fusion | flops 201457664 | bytes 1572864 | tf_op jit(solution)/shard_map/mrs,mrt->mst/dot_general | solution.py:124
  41.8 3.3 %collective-permute-done.2 = f32[8,2,128]{2,0,1:T(8,128)S(1)} collective-permute-done((f32[8,2,128]{2,0,1:T(8,128)S(1)}, f32[8,2,128]{2,0,1:T(8,128)S(1)}, u32[]{:S(2)}, u32[]{:S(2)}) %collective-permute-start.2) | collective-permute-done | bytes 8224 | tf_op jit(solution)/shard_map/ppermute | solution.py:14
  49.8 24.2 %while.20 = (s32[]{:T(128)}, f32[8,2,128]{2,1,0:T(2,128)S(1)}, f32[8,128,128]{2,1,0:T(8,128)}, f32[8,2,128]{2,1,0:T(2,128)S(1)}, s32[]{:T(128)}) while((s32[]{:T(128)}, f32[8,2,128]{2,1,0:T(2,128)S(1)}, f32[8,128,128]{2,1,0:T(8,128)}, f32[8,2,128]{2,1,0:T(2,128)S(1)}, s32[]{:T(128)}) %tuple.37), condition=%wide.region_1.2_spmd, body=%wide.region_0.1_spmd.sunk | while | flops 3147778 | bytes 581733 | solution.py:117
  49.8 2.6 %convolution_add_fusion.4 = f32[8,2,128]{2,1,0:T(2,128)} fusion(f32[8,2,128]{2,1,0:T(2,128)S(1)} %get-tuple-element.144, f32[8,2,128]{2,1,0:T(2,128)S(1)} %get-tuple-element.137, f32[8,128,128]{2,1,0:T(8,128)} %get-tuple-element.143), kind=kOutput, calls=%fused_computation.clone.1 | convolution fusion | flops 3147776 | bytes 548864 | tf_op jit(solution)/shard_map/while/body/eval_jaxpr/mrs,mcs->mcr/dot_general | solution.py:26
  52.4 3.5 %collective-permute-start = (f32[8,2,128]{2,1,0:T(2,128)}, f32[8,2,128]{2,1,0:T(2,128)S(1)}, u32[]{:S(2)}, u32[]{:S(2)}) collective-permute-start(f32[8,2,128]{2,1,0:T(2,128)} %convolution_add_fusion.4), channel_id=1, source_target_pairs={{0,1},{1,2},{2,3},{4,5},{5,6},{6,7},{8,9},{9,10},{10,11},{12,13},{... | collective-permute-start | bytes 24584 | tf_op jit(solution)/shard_map/while/body/eval_jaxpr/ppermute | solution.py:14
  57.4 2.6 %convolution_add_fusion.4 = f32[8,2,128]{2,1,0:T(2,128)} fusion(f32[8,2,128]{2,1,0:T(2,128)S(1)} %get-tuple-element.144, f32[8,2,128]{2,1,0:T(2,128)S(1)} %get-tuple-element.137, f32[8,128,128]{2,1,0:T(8,128)} %get-tuple-element.143), kind=kOutput, calls=%fused_computation.clone.1 | convolution fusion | flops 3147776 | bytes 548864 | tf_op jit(solution)/shard_map/while/body/eval_jaxpr/mrs,mcs->mcr/dot_general | solution.py:26
  60.0 4.2 %collective-permute-start = (f32[8,2,128]{2,1,0:T(2,128)}, f32[8,2,128]{2,1,0:T(2,128)S(1)}, u32[]{:S(2)}, u32[]{:S(2)}) collective-permute-start(f32[8,2,128]{2,1,0:T(2,128)} %convolution_add_fusion.4), channel_id=1, source_target_pairs={{0,1},{1,2},{2,3},{4,5},{5,6},{6,7},{8,9},{9,10},{10,11},{12,13},{... | collective-permute-start | bytes 24584 | tf_op jit(solution)/shard_map/while/body/eval_jaxpr/ppermute | solution.py:14
  65.7 2.6 %convolution_add_fusion.4 = f32[8,2,128]{2,1,0:T(2,128)} fusion(f32[8,2,128]{2,1,0:T(2,128)S(1)} %get-tuple-element.144, f32[8,2,128]{2,1,0:T(2,128)S(1)} %get-tuple-element.137, f32[8,128,128]{2,1,0:T(8,128)} %get-tuple-element.143), kind=kOutput, calls=%fused_computation.clone.1 | convolution fusion | flops 3147776 | bytes 548864 | tf_op jit(solution)/shard_map/while/body/eval_jaxpr/mrs,mcs->mcr/dot_general | solution.py:26
  68.3 4.2 %collective-permute-start = (f32[8,2,128]{2,1,0:T(2,128)}, f32[8,2,128]{2,1,0:T(2,128)S(1)}, u32[]{:S(2)}, u32[]{:S(2)}) collective-permute-start(f32[8,2,128]{2,1,0:T(2,128)} %convolution_add_fusion.4), channel_id=1, source_target_pairs={{0,1},{1,2},{2,3},{4,5},{5,6},{6,7},{8,9},{9,10},{10,11},{12,13},{... | collective-permute-start | bytes 24584 | tf_op jit(solution)/shard_map/while/body/eval_jaxpr/ppermute | solution.py:14
  84.8 25.2 %while.21 = (s32[]{:T(128)}, f32[8,2,128]{2,1,0:T(2,128)S(1)}, f32[8,128,128]{2,1,0:T(8,128)}, f32[8,2,128]{2,1,0:T(2,128)S(1)}, s32[]{:T(128)}) while((s32[]{:T(128)}, f32[8,2,128]{2,1,0:T(2,128)S(1)}, f32[8,128,128]{2,1,0:T(8,128)}, f32[8,2,128]{2,1,0:T(2,128)S(1)}, s32[]{:T(128)}) %tuple.40), condition=%wide.region_3.4_spmd, body=%wide.region_2.3_spmd.sunk | while | flops 3147778 | bytes 581733 | solution.py:132
  84.8 2.6 %convolution_add_fusion.5 = f32[8,2,128]{2,1,0:T(2,128)} fusion(f32[8,2,128]{2,1,0:T(2,128)S(1)} %get-tuple-element.159, f32[8,2,128]{2,1,0:T(2,128)S(1)} %get-tuple-element.152, f32[8,128,128]{2,1,0:T(8,128)} %get-tuple-element.158), kind=kOutput, calls=%fused_computation.1.clone.1 | convolution fusion | flops 3147776 | bytes 548864 | tf_op jit(solution)/shard_map/while/body/eval_jaxpr/mrs,mcs->mcr/dot_general | solution.py:26
  88.7 4.7 %collective-permute-done.1 = f32[8,2,128]{2,1,0:T(2,128)S(1)} collective-permute-done((f32[8,2,128]{2,1,0:T(2,128)}, f32[8,2,128]{2,1,0:T(2,128)S(1)}, u32[]{:S(2)}, u32[]{:S(2)}) %collective-permute-start.1) | collective-permute-done | bytes 8224 | tf_op jit(solution)/shard_map/while/body/eval_jaxpr/ppermute | solution.py:14
  93.4 2.6 %convolution_add_fusion.5 = f32[8,2,128]{2,1,0:T(2,128)} fusion(f32[8,2,128]{2,1,0:T(2,128)S(1)} %get-tuple-element.159, f32[8,2,128]{2,1,0:T(2,128)S(1)} %get-tuple-element.152, f32[8,128,128]{2,1,0:T(8,128)} %get-tuple-element.158), kind=kOutput, calls=%fused_computation.1.clone.1 | convolution fusion | flops 3147776 | bytes 548864 | tf_op jit(solution)/shard_map/while/body/eval_jaxpr/mrs,mcs->mcr/dot_general | solution.py:26
  97.2 4.5 %collective-permute-done.1 = f32[8,2,128]{2,1,0:T(2,128)S(1)} collective-permute-done((f32[8,2,128]{2,1,0:T(2,128)}, f32[8,2,128]{2,1,0:T(2,128)S(1)}, u32[]{:S(2)}, u32[]{:S(2)}) %collective-permute-start.1) | collective-permute-done | bytes 8224 | tf_op jit(solution)/shard_map/while/body/eval_jaxpr/ppermute | solution.py:14
  101.7 2.6 %convolution_add_fusion.5 = f32[8,2,128]{2,1,0:T(2,128)} fusion(f32[8,2,128]{2,1,0:T(2,128)S(1)} %get-tuple-element.159, f32[8,2,128]{2,1,0:T(2,128)S(1)} %get-tuple-element.152, f32[8,128,128]{2,1,0:T(8,128)} %get-tuple-element.158), kind=kOutput, calls=%fused_computation.1.clone.1 | convolution fusion | flops 3147776 | bytes 548864 | tf_op jit(solution)/shard_map/while/body/eval_jaxpr/mrs,mcs->mcr/dot_general | solution.py:26
  105.5 4.5 %collective-permute-done.1 = f32[8,2,128]{2,1,0:T(2,128)S(1)} collective-permute-done((f32[8,2,128]{2,1,0:T(2,128)}, f32[8,2,128]{2,1,0:T(2,128)S(1)}, u32[]{:S(2)}, u32[]{:S(2)}) %collective-permute-start.1) | collective-permute-done | bytes 8224 | tf_op jit(solution)/shard_map/while/body/eval_jaxpr/ppermute | solution.py:14
  112.2 4.1 %collective-permute-start.3 = (f32[8,2,128]{2,1,0:T(2,128)S(1)}, f32[8,2,128]{2,1,0:T(2,128)S(1)}, u32[]{:S(2)}, u32[]{:S(2)}) collective-permute-start(f32[8,2,128]{2,1,0:T(2,128)S(1)} %convolution_subtract_fusion.2), channel_id=1, source_target_pairs={{0,1},{1,2},{2,3},{4,5},{5,6},{6,7},{8,9},{9,10},{10,11},{12,13},{... | collective-permute-start | bytes 24584 | tf_op jit(solution)/shard_map/ppermute | solution.py:14
  (139 shorter events, 55.3 us)
Async XLA Ops:
  0.0 35.5 %copy-start = (f32[3,128,128]{2,1,0:T(8,128)S(1)}, f32[3,128,128]{2,1,0:T(8,128)}, u32[]{:S(2)}) copy-start(f32[3,128,128]{2,1,0:T(8,128)} %param.16) | copy-start | bytes 589828
  2.4 31.4 %all-to-all-start = ((f32[8,16,384]{2,1,0:T(8,128)}), f32[8,16,384]{2,1,0:T(8,128)S(1)}, u32[]{:S(2)}, u32[]{:S(2)}) async-start(f32[8,16,384]{2,1,0:T(8,128)} %bitcast), calls=%async_computation | async-start | bytes 393216 | tf_op jit(solution)/shard_map/all_to_all | solution.py:58
  10.0 5.0 %copy-start.20 = (f32[8]{0:T(128)}, f32[8]{0:T(128)S(1)}, u32[]{:S(2)}) copy-start(f32[8]{0:T(128)S(1)} %multiply_multiply_fusion) | copy-start | bytes 100
  10.0 5.0 %copy-start.1 = (f32[8,3,128,128]{3,2,1,0:T(8,128)S(1)}, f32[8,3,128,128]{3,2,1,0:T(8,128)}, u32[]{:S(2)}) copy-start(f32[8,3,128,128]{3,2,1,0:T(8,128)} %param.25) | copy-start | bytes 4718596
  10.0 5.0 %copy-start.7 = (f32[128,128]{0,1:T(8,128)S(1)}, f32[128,128]{0,1:T(8,128)}, u32[]{:S(2)}) copy-start(f32[128,128]{0,1:T(8,128)} %fusion.96) | copy-start | bytes 196612
  31.1 4.8 %copy-start.15 = (f32[3,7,7]{2,1,0:T(8,128)S(1)}, f32[3,7,7]{2,1,0:T(8,128)}, u32[]{:S(2)}) copy-start(f32[3,7,7]{2,1,0:T(8,128)} %param.17) | copy-start | bytes 1768
  33.1 5.2 %copy-start.18 = (f32[3,2,7]{2,1,0:T(2,128)S(1)}, f32[3,2,7]{2,1,0:T(2,128)}, u32[]{:S(2)}) copy-start(f32[3,2,7]{2,1,0:T(2,128)} %param.22) | copy-start | bytes 508
  35.9 9.2 %copy-start.17 = (f32[8,2,128]{2,1,0:T(2,128)S(1)}, f32[8,2,128]{2,1,0:T(2,128)}, u32[]{:S(2)}) copy-start(f32[8,2,128]{2,1,0:T(2,128)} %fusion.38) | copy-start | bytes 24580
  39.5 5.5 %collective-permute-start.2 = (f32[8,2,128]{2,0,1:T(8,128)S(1)}, f32[8,2,128]{2,0,1:T(8,128)S(1)}, u32[]{:S(2)}, u32[]{:S(2)}) collective-permute-start(f32[8,2,128]{2,0,1:T(8,128)S(1)} %slice_bitcast_fusion.27), channel_id=1, source_target_pairs={{1,0},{2,1},{3,2},{5,4},{6,5},{7,6},{9,8},{10,9},{11,10},{13,12},{... | collective-permute-start | bytes 24584 | tf_op jit(solution)/shard_map/ppermute | solution.py:14
  52.4 5.0 %collective-permute-start = (f32[8,2,128]{2,1,0:T(2,128)}, f32[8,2,128]{2,1,0:T(2,128)S(1)}, u32[]{:S(2)}, u32[]{:S(2)}) collective-permute-start(f32[8,2,128]{2,1,0:T(2,128)} %convolution_add_fusion.4), channel_id=1, source_target_pairs={{0,1},{1,2},{2,3},{4,5},{5,6},{6,7},{8,9},{9,10},{10,11},{12,13},{... | collective-permute-start | bytes 24584 | tf_op jit(solution)/shard_map/while/body/eval_jaxpr/ppermute | solution.py:14
  60.0 5.7 %collective-permute-start = (f32[8,2,128]{2,1,0:T(2,128)}, f32[8,2,128]{2,1,0:T(2,128)S(1)}, u32[]{:S(2)}, u32[]{:S(2)}) collective-permute-start(f32[8,2,128]{2,1,0:T(2,128)} %convolution_add_fusion.4), channel_id=1, source_target_pairs={{0,1},{1,2},{2,3},{4,5},{5,6},{6,7},{8,9},{9,10},{10,11},{12,13},{... | collective-permute-start | bytes 24584 | tf_op jit(solution)/shard_map/while/body/eval_jaxpr/ppermute | solution.py:14
  68.3 5.7 %collective-permute-start = (f32[8,2,128]{2,1,0:T(2,128)}, f32[8,2,128]{2,1,0:T(2,128)S(1)}, u32[]{:S(2)}, u32[]{:S(2)}) collective-permute-start(f32[8,2,128]{2,1,0:T(2,128)} %convolution_add_fusion.4), channel_id=1, source_target_pairs={{0,1},{1,2},{2,3},{4,5},{5,6},{6,7},{8,9},{9,10},{10,11},{12,13},{... | collective-permute-start | bytes 24584 | tf_op jit(solution)/shard_map/while/body/eval_jaxpr/ppermute | solution.py:14
  76.6 6.7 %copy-start.10 = (f32[8,2,128]{2,1,0:T(2,128)}, f32[8,2,128]{2,1,0:T(2,128)S(1)}, u32[]{:S(2)}) copy-start(f32[8,2,128]{2,1,0:T(2,128)S(1)} %fusion.31) | copy-start | bytes 24580
  78.5 4.8 %copy-start.12 = (f32[8,2,128]{2,1,0:T(2,128)}, f32[8,2,128]{2,1,0:T(2,128)S(1)}, u32[]{:S(2)}) copy-start(f32[8,2,128]{2,1,0:T(2,128)S(1)} %fusion.22) | copy-start | bytes 24580
  87.4 6.0 %collective-permute-start.1 = (f32[8,2,128]{2,1,0:T(2,128)}, f32[8,2,128]{2,1,0:T(2,128)S(1)}, u32[]{:S(2)}, u32[]{:S(2)}) collective-permute-start(f32[8,2,128]{2,1,0:T(2,128)} %convolution_add_fusion.5), channel_id=1, source_target_pairs={{1,0},{2,1},{3,2},{5,4},{6,5},{7,6},{9,8},{10,9},{11,10},{13,12},{... | collective-permute-start | bytes 24584 | tf_op jit(solution)/shard_map/while/body/eval_jaxpr/ppermute | solution.py:14
  95.9 5.7 %collective-permute-start.1 = (f32[8,2,128]{2,1,0:T(2,128)}, f32[8,2,128]{2,1,0:T(2,128)S(1)}, u32[]{:S(2)}, u32[]{:S(2)}) collective-permute-start(f32[8,2,128]{2,1,0:T(2,128)} %convolution_add_fusion.5), channel_id=1, source_target_pairs={{1,0},{2,1},{3,2},{5,4},{6,5},{7,6},{9,8},{10,9},{11,10},{13,12},{... | collective-permute-start | bytes 24584 | tf_op jit(solution)/shard_map/while/body/eval_jaxpr/ppermute | solution.py:14
  104.2 5.7 %collective-permute-start.1 = (f32[8,2,128]{2,1,0:T(2,128)}, f32[8,2,128]{2,1,0:T(2,128)S(1)}, u32[]{:S(2)}, u32[]{:S(2)}) collective-permute-start(f32[8,2,128]{2,1,0:T(2,128)} %convolution_add_fusion.5), channel_id=1, source_target_pairs={{1,0},{2,1},{3,2},{5,4},{6,5},{7,6},{9,8},{10,9},{11,10},{13,12},{... | collective-permute-start | bytes 24584 | tf_op jit(solution)/shard_map/while/body/eval_jaxpr/ppermute | solution.py:14
  110.0 8.5 %copy-start.11 = (f32[8,2,128]{2,1,0:T(2,128)S(1)}, f32[8,2,128]{2,1,0:T(2,128)}, u32[]{:S(2)}) copy-start(f32[8,2,128]{2,1,0:T(2,128)} %copy-done.10) | copy-start | bytes 24580
  110.0 9.6 %copy-start.27 = (s32[3,2,128]{2,1,0:T(2,128)S(1)}, s32[3,2,128]{2,1,0:T(2,128)}, u32[]{:S(2)}) copy-start(s32[3,2,128]{2,1,0:T(2,128)} %param.23) | copy-start | bytes 9220
  110.0 10.0 %copy-start.4 = (f32[3,128,128]{2,1,0:T(8,128)S(1)}, f32[3,128,128]{2,1,0:T(8,128)}, u32[]{:S(2)}) copy-start(f32[3,128,128]{2,1,0:T(8,128)} %param.20) | copy-start | bytes 589828
  111.7 8.8 %copy-start.6 = (f32[3,128,128]{2,1,0:T(8,128)S(1)}, f32[3,128,128]{2,1,0:T(8,128)}, u32[]{:S(2)}) copy-start(f32[3,128,128]{2,1,0:T(8,128)} %param.21) | copy-start | bytes 589828
  111.7 8.8 %copy-start.23 = (f32[8]{0:T(128)S(1)}, f32[8]{0:T(128)}, u32[]{:S(2)}) copy-start(f32[8]{0:T(128)} %copy-done.20) | copy-start | bytes 100
  111.7 9.3 %copy-start.19 = (f32[3,2,7]{2,1,0:T(2,128)S(1)}, f32[3,2,7]{2,1,0:T(2,128)}, u32[]{:S(2)}) copy-start(f32[3,2,7]{2,1,0:T(2,128)} %param.22) | copy-start | bytes 508
  112.2 7.2 %collective-permute-start.3 = (f32[8,2,128]{2,1,0:T(2,128)S(1)}, f32[8,2,128]{2,1,0:T(2,128)S(1)}, u32[]{:S(2)}, u32[]{:S(2)}) collective-permute-start(f32[8,2,128]{2,1,0:T(2,128)S(1)} %convolution_subtract_fusion.2), channel_id=1, source_target_pairs={{0,1},{1,2},{2,3},{4,5},{5,6},{6,7},{8,9},{9,10},{10,11},{12,13},{... | collective-permute-start | bytes 24584 | tf_op jit(solution)/shard_map/ppermute | solution.py:14
  (13 other events, 43.0 us)
where the time goes:
time: 125 us; the launch traced here: 124 us
  matrix products  64.1 us (51%)
  starting transfers between devices  26.3 us (21%)
  waiting for transfers between devices  21.6 us (17%)
  local copies, waits for them, and re-layouts  7.38 us (6%)
  other arithmetic  3.71 us (3%)
    dot_general x24, matrix products, apply_panel(): return jnp.einsum('mrs,mcs->mcr', matrix, vector, precision=HIGHEST)  34.2 us
    ppermute x8, waiting for transfers between devices, shifted(): return lax.ppermute(block, axis, route)  21.6 us
    ppermute x8, starting transfers between devices, shifted(): return lax.ppermute(block, axis, route)  21.1 us
    all_to_all x1, starting transfers between devices, body(): lax.all_to_all(spectrum, 'mode', split_axis=0, concat_axis=1, tiled=True)  5.19 us
    dot_general x3, matrix products, body(): jnp.einsum('mrs,mrt->mst', coupling[:, slab_index], solved_map, precision...  4.92 us
    dot_general x3, matrix products, body(): jnp.einsum('mrs,mst->mrt', coupling[:, slab_index], forward_map, precisio...  4.46 us
    dot_general x3, matrix products, body(): jnp.einsum('mrs,mst->mrt', inverse_panels[:, slab_index], banded, precisi...  4.42 us
    dot_general x3, matrix products, body(): jnp.einsum('mrs,mst->mrt', inverse_panels[:, slab_index], backward_map, p...  4.07 us
  transfers between devices with their start and end apart: 9, of which 7 were waited for; matrix products, arithmetic and copies ran while one was open for 24% of the time, Pallas kernels for 0%

commit v1 on v0

v1 whole, which is shorter than its diff:
```python
import functools
import math

import jax
import jax.numpy as jnp
import numpy as np
from jax import lax
from jax.experimental import pallas as pl
from jax.experimental.pallas import tpu as pltpu
from jax.sharding import PartitionSpec as P

F32 = jnp.float32
BF16 = jnp.bfloat16
VMEM = pl.BlockSpec(memory_space=pltpu.VMEM)
SMEM = pl.BlockSpec(memory_space=pltpu.SMEM)
NN = (((1,), (0,)), ((), ()))
NT = (((1,), (1,)), ((), ()))


def call(kernel, outs, args, smem=0, aliases=None):
    return pl.pallas_call(
        kernel,
        out_shape=outs,
        in_specs=[VMEM] * (len(args) - smem) + [SMEM] * smem,
        out_specs=[VMEM] * len(outs),
        input_output_aliases=aliases or {},
        compiler_params=pltpu.CompilerParams(vmem_limit_bytes=56 * 2**20),
    )(*args)


def split(x):
    high = x.astype(BF16)
    return high, (x - high.astype(F32)).astype(BF16)


def dot(a, b, dims=NN):
    return lax.dot_general(a, b, dims, preferred_element_type=F32)


def wide(x):
    return jnp.concatenate(split(x), axis=1)


def tall(x):
    return jnp.concatenate(split(x), axis=0)


def product(left, right):
    size = right.shape[1] // 2
    high, low = split(left)
    upper, lower = right[:, :size], right[:, size:]
    return dot(
        jnp.concatenate([high, low, high], axis=1), jnp.concatenate([upper, upper, lower], axis=0)
    )


def by_mode(x, modes):
    mode_of = lax.broadcasted_iota(jnp.int32, x.shape, 0) // 2
    spread = jnp.concatenate([jnp.where(mode_of == k, x, 0.0) for k in range(modes)], axis=1)
    return tall(spread)


def folded(out, rows):
    size = out.shape[1] // 2
    return out[:rows, :size] + out[:rows, size:] + out[rows:, :size]


def apply(x, weight, modes):
    return folded(dot(by_mode(x, modes), weight), x.shape[0])


def wave(mode_total, shape, modes, axis=0):
    first = lax.axis_index("mode") * modes
    index = first + lax.broadcasted_iota(jnp.int32, shape, axis) // 2
    number = index.astype(F32) / mode_total
    return 4.0 * number * number


def wave_of(k, mode_total, modes):
    number = (jnp.full((1, 1), lax.axis_index("mode") * modes + k, jnp.int32)).astype(F32) / mode_total
    return 4.0 * number * number


def dft_kernel(table_ref, rhs_ref, out_ref):
    high, low = split(rhs_ref[...])
    out_ref[...] = dot(table_ref[...], jnp.concatenate([high, high, low], axis=0))


def maps_kernel(
    modes,
    mode_total,
    panels_ref,
    band_ref,
    radial_ref,
    stiff_ref,
    mass_ref,
    number_ref,
    wp_ref,
    wg_ref,
    wh_ref,
    we_ref,
    rad_ref,
    radt_ref,
    face_ref,
    ship_ref,
):
    slabs = panels_ref.shape[1]
    size = panels_ref.shape[2]
    elem, last = lax.axis_index("elem"), lax.axis_size("elem") - 1
    band_t = [(band_ref[0, j].T, band_ref[1, j].T) for j in range(slabs)]
    for j in range(slabs):
        for k in range(modes):
            rows = pl.ds(k * size, size)
            weight = wide(panels_ref[k, j].T)
            wp_ref[j, rows] = weight
            lam = wave_of(k, mode_total, modes)
            wg_ref[j, rows] = wide(product(band_t[j][0] + lam * band_t[j][1], weight))
            if j + 1 < slabs:
                wh_ref[j, rows] = wide(
                    product(band_ref[0, j + 1] + lam * band_ref[1, j + 1], weight)
                )
    stiff_high, stiff_low = split(band_ref[0, 0])
    mass_high, mass_low = split(band_ref[1, 0])
    we_ref[...] = jnp.concatenate([stiff_high, mass_high, stiff_low, mass_low], axis=1)
    for j in range(slabs):
        radial = wide(radial_ref[j])
        rad_ref[j] = radial
        radt_ref[j] = wide(radial_ref[j].T)
        parts = [wide(product(ref[j].T, radial)) for ref in (stiff_ref, mass_ref)]
        both = jnp.concatenate(
            [parts[0][:, :size], parts[1][:, :size], parts[0][:, size:], parts[1][:, size:]], axis=1
        )
        for side in range(2):
            place = lax.broadcasted_iota(jnp.int32, (size, size), 0)
            onehot = jnp.where(number_ref[j, side : side + 1] == place, 1.0, 0.0).astype(BF16)
            face_ref[j, side] = dot(onehot, both).astype(BF16)

    @pl.when(elem == last)
    def _():
        for k in range(modes):
            rows = pl.ds(k * size, size)
            lam = wave_of(k, mode_total, modes)
            forward = []
            current = None
            for j in range(slabs):
                if current is None:
                    weight = wg_ref[j, rows].astype(F32)
                    current = -(weight[:, :size] + weight[:, size:])
                else:
                    current = -product(current, wg_ref[j, rows])
                forward.append(current)
            for j in range(slabs - 2, -1, -1):
                current = forward[j] - product(current, wh_ref[j, rows])
            ship_ref[k] = product(current, wide(band_ref[0, 0] + lam * band_ref[1, 0]))

    @pl.when(elem != last)
    def _():
        for k in range(modes):
            ship_ref[k] = panels_ref[k, slabs - 1]


def face_push(values, weight, lam):
    rows, size = values.shape
    high, low = split(values)
    blocks = [weight[:, i * size : (i + 1) * size] for i in range(4)]
    out = dot(
        jnp.concatenate([high, low], axis=0), jnp.concatenate(blocks, axis=0), NT
    )
    out = out[:rows, : 2 * size] + out[:rows, 2 * size :] + out[rows:, : 2 * size]
    return out[:, :size] + lam * out[:, size:]


def face_lift(values, weight, lam):
    rows, size = values.shape
    out = folded(dot(tall(values), weight), rows)
    return out[:, :size] + lam * out[:, size:]


def block_of(spec_ref, index, size):
    per = spec_ref.shape[2] // size
    at = index % per * size
    return spec_ref[index // per, :, at : at + size]


def inner_kernel(
    modes,
    mode_total,
    spec_ref,
    rad_ref,
    face_ref,
    wp_ref,
    wg_ref,
    wh_ref,
    we_ref,
    reig_ref,
    axial_ref,
    aeig_ref,
    coup_ref,
    zsrc_ref,
    solved_ref,
    y_ref,
    msg_ref,
):
    slabs, inner = aeig_ref.shape
    size = rad_ref.shape[1]
    rows = 2 * modes
    lam = wave(mode_total, (rows, size), modes)
    elem, last = lax.axis_index("elem"), lax.axis_size("elem") - 1
    pushed = []
    for j in range(slabs):
        source = jnp.concatenate(
            [block_of(spec_ref, j * (inner + 1) + a, size) for a in range(inner)], axis=0
        )
        first = folded(dot(tall(source), rad_ref[j]), inner * rows)
        first = [first[a * rows : (a + 1) * rows] for a in range(inner)]
        sums = [None, None]
        for b in range(inner):
            value = first[0] * axial_ref[j, 0, b]
            for a in range(1, inner):
                value = value + first[a] * axial_ref[j, a, b]
            value = value / (aeig_ref[j, b] + reig_ref[j : j + 1] + lam)
            zsrc_ref[j, b] = value
            for side in range(2):
                weight = coup_ref[j, side, 0] * axial_ref[j, 0, b]
                for a in range(1, inner):
                    weight = weight + coup_ref[j, side, a] * axial_ref[j, a, b]
                term = value * weight
                sums[side] = term if sums[side] is None else sums[side] + term
        pushed.append([face_push(sums[side], face_ref[j, side], lam) for side in range(2)])
    solved = []
    for j in range(slabs):
        reduced = block_of(spec_ref, j * (inner + 1) + inner, size) - pushed[j][1]
        if j + 1 < slabs:
            reduced = reduced - pushed[j + 1][0]
        solved.append(apply(reduced, wp_ref[j], modes))
        solved_ref[j] = solved[j]
    values = [solved[0]]
    for j in range(1, slabs):
        values.append(solved[j] - apply(values[-1], wg_ref[j], modes))
    for j in range(slabs):
        y_ref[j] = values[j]
    load = pushed[0][0]
    msg_ref[1] = load

    @pl.when(elem != last)
    def _():
        msg_ref[0] = values[slabs - 1]

    @pl.when(elem == last)
    def _():
        current = values[slabs - 1]
        for j in range(slabs - 2, -1, -1):
            current = values[j] - apply(current, wh_ref[j], modes)
        msg_ref[0] = load + face_lift(current, we_ref[...], lam)


def previous_weight(panel_ref, modes):
    parts = [split(panel_ref[k]) for k in range(modes)]
    return jnp.concatenate(
        [jnp.concatenate([p[i] for p in parts], axis=1) for i in range(2)], axis=0
    )


def apply_nt(x, weight, modes):
    return folded(dot(by_mode(x, modes), weight, NT), x.shape[0])


def forward_values(before, solved_ref, wg_ref, modes):
    values = []
    for j in range(solved_ref.shape[0]):
        before = solved_ref[j] - apply(before, wg_ref[j], modes)
        values.append(before)
    return values


def backward_values(values, after, wp_ref, wh_ref, modes):
    slabs = len(values)
    out = [None] * slabs
    out[-1] = values[-1] - apply(after, wp_ref[slabs - 1], modes)
    for j in range(slabs - 2, -1, -1):
        out[j] = values[j] - apply(out[j + 1], wh_ref[j], modes)
    return out


def forward_kernel(
    modes, mode_total, at, hub, got_ref, far_ref, msg_ref, pprev_ref, ship_ref, solved_ref, y_ref, wp_ref, wg_ref, wh_ref, we_ref,
    before_ref, values_ref, out_ref,
):
    rows, size = solved_ref.shape[1:]
    slabs = solved_ref.shape[0]
    lam = wave(mode_total, (rows, size), modes)

    @pl.when(lax.axis_index("elem") == at)
    def _():
        if at > 0:
            weight = previous_weight(pprev_ref, modes)
            before = got_ref[0] - apply_nt(msg_ref[1], weight, modes)
            before_ref[...] = before
            values = forward_values(before, solved_ref, wg_ref, modes)
        else:
            before_ref[...] = jnp.zeros((rows, size), F32)
            values = [y_ref[j] for j in range(slabs)]
        for j in range(slabs):
            values_ref[j] = values[j]
        if not hub:
            out_ref[0] = values[-1]
        else:
            final = values[-1] - apply(far_ref[1], wp_ref[slabs - 1], modes)
            weight = jnp.concatenate([wide(ship_ref[k]) for k in range(modes)], axis=0)
            back = far_ref[0] + apply(final, weight, modes)
            found = backward_values(values, back, wp_ref, wh_ref, modes)
            out_ref[0] = msg_ref[1] + face_lift(found[0], we_ref[...], lam)
            out_ref[1] = final
            out_ref[2] = back


def backward_kernel(modes, mode_total, at, got_ref, msg_ref, y_ref, wp_ref, wh_ref, we_ref, out_ref):
    rows, size = y_ref.shape[1:]
    lam = wave(mode_total, (rows, size), modes)

    @pl.when(lax.axis_index("elem") == at)
    def _():
        values = [y_ref[j] for j in range(y_ref.shape[0])]
        found = backward_values(values, got_ref[0], wp_ref, wh_ref, modes)
        out_ref[0] = msg_ref[1] + face_lift(found[0], we_ref[...], lam)


def final_kernel(
    modes, mode_total,
    zsrc_ref, before_ref, y_ref, after_ref, solved_ref, pprev_ref, wp_ref, wg_ref, wh_ref, we_ref, face_ref, radt_ref, reig_ref,
    axial_ref, aeig_ref, coup_ref,
    out_ref, x_ref,
):
    slabs, inner = aeig_ref.shape
    rows, size = before_ref.shape
    lam = wave(mode_total, (rows, size), modes)
    elem, last = lax.axis_index("elem"), lax.axis_size("elem") - 1

    def finish(before, found):
        for j in range(slabs):
            x_ref[j + 1] = found[j]
        weight = previous_weight(pprev_ref, modes)
        back = face_lift(found[0], we_ref[...], lam)
        x_ref[0] = before - apply_nt(back, weight, modes)

    @pl.when(elem == last)
    def _():
        before = before_ref[...]
        values = forward_values(before, solved_ref, wg_ref, modes)
        found = [None] * slabs
        found[-1] = values[-1]
        for j in range(slabs - 2, -1, -1):
            found[j] = values[j] - apply(found[j + 1], wh_ref[j], modes)
        finish(before, found)

    @pl.when(elem != last)
    def _():
        values = [y_ref[j] for j in range(slabs)]
        found = backward_values(values, after_ref[...], wp_ref, wh_ref, modes)
        finish(before_ref[...], found)

    @pl.when(elem == 0)
    def _():
        x_ref[0] = jnp.zeros((rows, size), F32)

    for j in range(slabs):
        lifted = [face_lift(x_ref[j + side], face_ref[j, side], lam) for side in range(2)]
        kept = []
        for b in range(inner):
            total = None
            for side in range(2):
                weight = coup_ref[j, side, 0] * axial_ref[j, 0, b]
                for a in range(1, inner):
                    weight = weight + coup_ref[j, side, a] * axial_ref[j, a, b]
                term = lifted[side] * weight
                total = term if total is None else total + term
            kept.append(zsrc_ref[j, b] - total / (aeig_ref[j, b] + reig_ref[j : j + 1] + lam))
        values = []
        for a in range(inner):
            value = kept[0] * axial_ref[j, a, 0]
            for b in range(1, inner):
                value = value + kept[b] * axial_ref[j, a, b]
            values.append(value)
        result = folded(dot(tall(jnp.concatenate(values, axis=0)), radt_ref[j]), inner * rows)
        for a in range(inner):
            at = (j * (inner + 1) + a) * size
            out_ref[:, at : at + size] = result[a * rows : (a + 1) * rows]
        at = (j * (inner + 1) + inner) * size
        out_ref[:, at : at + size] = x_ref[j + 1]


def dft_table(planes):
    row, col = np.arange(planes)[:, None], np.arange(planes)[None]
    angle = row // 2 * col % planes * (2.0 * math.pi / planes)
    table = np.where(row % 2 == 0, np.cos(angle), -np.sin(angle)) / math.sqrt(planes)
    table = jnp.asarray(table, F32)
    high, low = split(table)
    return jnp.concatenate([high, low, high], axis=1)


def body(
    rhs_phys, radial_basis, axial_basis, radial_eig, axial_eig, face_stiff, face_mass, axial_coupling, face_numbering,
    band_panels, inverse_panels,
):
    planes, nodes = rhs_phys.shape
    modes, slabs, size, _ = inverse_panels.shape
    inner = axial_basis.shape[1]
    devices = lax.axis_size("mode")
    elems = lax.axis_size("elem")
    mode_total = modes * devices
    rows = 2 * modes
    hub = elems - 2
    here = lax.axis_index("elem")

    def shape(*dims):
        return jax.ShapeDtypeStruct(dims, F32)

    def half(*dims):
        return jax.ShapeDtypeStruct(dims, BF16)

    spectrum = call(dft_kernel, [shape(planes, nodes)], [dft_table(planes), rhs_phys])[0]
    spectrum = lax.all_to_all(spectrum.reshape(devices, rows, nodes), "mode", 0, 0, tiled=False)
    if nodes % size:
        spectrum = jnp.swapaxes(spectrum, 0, 1).reshape(1, rows, devices * nodes)
    wp, wg, wh, we, rad, radt, face, ship = call(
        functools.partial(maps_kernel, modes, mode_total),
        [
            half(slabs, modes * size, 2 * size),
            half(slabs, modes * size, 2 * size),
            half(slabs - 1, modes * size, 2 * size),
            half(size, 4 * size),
            half(slabs, size, 2 * size),
            half(slabs, size, 2 * size),
            half(slabs, 2, size, 4 * size),
            shape(modes, size, size),
        ],
        [inverse_panels, band_panels, radial_basis, face_stiff, face_mass, face_numbering],
    )
    pprev = lax.ppermute(ship, "elem", [(i, i + 1) for i in range(elems - 1)])
    far_map = lax.ppermute(ship, "elem", [(elems - 1, hub)])
    zsrc, solved, y, msg = call(
        functools.partial(inner_kernel, modes, mode_total),
        [shape(slabs, inner, rows, size), shape(slabs, rows, size), shape(slabs, rows, size), shape(2, rows, size)],
        [spectrum, rad, face, wp, wg, wh, we, radial_eig, axial_basis, axial_eig, axial_coupling],
        smem=3,
    )
    far = lax.ppermute(msg, "elem", [(elems - 1, hub)])
    before = jnp.zeros((rows, size), F32)
    send = msg[:1]
    values = y
    for at in range(hub + 1):
        got = lax.ppermute(send, "elem", [(at - 1, at)]) if at > 0 else send
        if at == 0 and hub > 0:
            continue
        before_new, values_new, out = call(
            functools.partial(forward_kernel, modes, mode_total, at, at == hub),
            [shape(rows, size), shape(slabs, rows, size), shape(3 if at == hub else 1, rows, size)],
            [got, far, msg, pprev, far_map, solved, y, wp, wg, wh, we],
        )
        before = jnp.where(here == at, before_new, before)
        values = jnp.where(here == at, values_new, values)
        send = out
    after = jnp.where(here == hub, out[2], 0.0)
    final = lax.ppermute(out[1], "elem", [(hub, elems - 1)])
    before = jnp.where(here == elems - 1, final, before)
    send = out[:1]
    for at in range(hub - 1, -1, -1):
        got = lax.ppermute(send, "elem", [(at + 1, at)])
        after = jnp.where(here == at, got[0], after)
        if at > 0:
            send = call(
                functools.partial(backward_kernel, modes, mode_total, at),
                [shape(1, rows, size)],
                [got, msg, values, wp, wh, we],
            )[0]
    return call(
        functools.partial(final_kernel, modes, mode_total),
        [shape(rows, slabs * (inner + 1) * size), shape(slabs + 1, rows, size)],
        [zsrc, before, values, after, solved, pprev, wp, wg, wh, we, face, radt, radial_eig, axial_basis, axial_eig, axial_coupling],
        smem=3,
    )[0]


def solution(mesh):
    placed = (
        P(None, ("elem", "mode")),
        P("elem", None, None),
        P("elem", None, None),
        P("elem", None),
        P("elem", None),
        P("elem", None, None),
        P("elem", None, None),
        P("elem", None, None),
        P("elem", None, None),
        P(None, "elem", None, None),
        P("mode", "elem", None, None),
    )
    return jax.shard_map(
        body, mesh=mesh, in_specs=placed, out_specs=P("mode", "elem"), check_vma=False
    )
```

time: 125 us -> 77.9 us (0.62)
  matrix products: 64.1 us -> 0 us
  Pallas kernels: 0 us -> 27.3 us
  starting transfers between devices: 26.3 us -> 13 us
  blocking collectives: 0 us -> 10.3 us
  local copies, waits for them, and re-layouts: 7.38 us -> 3.65 us
  other arithmetic: 3.71 us -> 1.8 us
    dot_general x58 -> x0, matrix products: 64.1 us -> none  [the longest x24 34.2 us: apply_panel(): return jnp.einsum('mrs,mcs->mcr', matrix, vector, precision=HIGHEST)]
    pallas_call x0 -> x7, Pallas kernels: none -> 27.3 us  [call(): pl.pallas_call(kernel, out_shape=outs, in_specs=[VMEM] * (len(args) - sme...]
    all_to_all x0 -> x1, blocking collectives: none -> 10.3 us  [body(): lax.all_to_all(spectrum.reshape(devices, rows, nodes), 'mode', 0, 0, tile...]
    ppermute x8, starting transfers between devices: 21.1 us -> 13 us  [the longest x1 4.95 us: body(): pprev = lax.ppermute(ship, 'elem', [(i, i + 1) for i in range(elems - 1)])]
    all_to_all x1 -> x0, starting transfers between devices: 5.19 us -> none  [body(): lax.all_to_all(spectrum, 'mode', split_axis=0, concat_axis=1, tiled=True)]
    add x3 -> x0, other arithmetic: 2.18 us -> none  [the longest x1 1.38 us: body(): band_panels[0][None]]
    while x1 -> x0, local copies, waits for them, and re-layouts: 2.05 us -> none  [body(): lax.fori_loop(0, lax.axis_size('elem') - 1, forward_round, zero_vec)]
    unnamed x56 -> x22, local copies, waits for them, and re-layouts: 0.17 us -> 2.19 us
  transfers between devices with their start and end apart: 9 -> 8, of which waited for: 7 -> 2; matrix products, arithmetic and copies ran while one was open for 24% -> 2% of each run, Pallas kernels for 0% -> 9%
where the time goes in v1:
time: 77.9 us; the launch traced here: 77.3 us
  Pallas kernels  27.3 us (35%)
  waiting for transfers between devices  21.2 us (27%)
  starting transfers between devices  13 us (17%)
  blocking collectives  10.3 us (13%)
  local copies, waits for them, and re-layouts  3.65 us (5%)
  other arithmetic  1.8 us (2%)
    pallas_call x7, Pallas kernels, call(): pl.pallas_call(kernel, out_shape=outs, in_specs=[VMEM] * (len(args) - sme...  27.3 us
    ppermute x2, waiting for transfers between devices, body(): got = lax.ppermute(send, 'elem', [(at + 1, at)])  19.8 us
    all_to_all x1, blocking collectives, body(): lax.all_to_all(spectrum.reshape(devices, rows, nodes), 'mode', 0, 0, tile...  10.3 us
    ppermute x1, starting transfers between devices, body(): pprev = lax.ppermute(ship, 'elem', [(i, i + 1) for i in range(elems - 1)])  4.95 us
    ppermute x2, starting transfers between devices, body(): got = lax.ppermute(send, 'elem', [(at - 1, at)]) if at > 0 else send  4.09 us
    unnamed x22, local copies, waits for them, and re-layouts  2.19 us
    ppermute x2, starting transfers between devices, body(): got = lax.ppermute(send, 'elem', [(at + 1, at)])  1.93 us
  transfers between devices with their start and end apart: 8, of which 2 were waited for; matrix products, arithmetic and copies ran while one was open for 2% of the time, Pallas kernels for 9%

profile of v1, /device:TPU:0, one launch (start us, length us, event | category | flops | bytes accessed | tf_op | source)
XLA Modules:
  0.0 77.3 jit_solution(17648214408405302476)
XLA Ops:
  0.0 6.5 %shard_map.119 = (bf16[3,1024,256]{2,1,0:T(8,128)(2,1)}, bf16[3,1024,256]{2,1,0:T(8,128)(2,1)}, bf16[2,1024,256]{2,1,0:T(8,128)(2,1)}, bf16[128,512]{1,0:T(8,128...) custom-call(f32[8,3,128,128]{3,2,1,0:T(8,128)} %panels_ref.1, ...), custom_call_target="tpu_custom_call" | custom-call | tf_op jit(solution)/shard_map/pallas_call | solution.py:21
  6.5 4.9 %collective-permute-start.2 = (f32[8,128,128]{2,1,0:T(8,128)}, f32[8,128,128]{2,1,0:T(8,128)S(1)}, u32[]{:S(2)}, u32[]{:S(2)}) collective-permute-start(f32[8,128,128]{2,1,0:T(8,128)} %get-tuple-element.32), channel_id=1, source_target_pairs={{0,1},{1,2},{2,3},{4,5},{5,6},{6,7},{8,9},{9,10},{10,11},{12,13},{... | collective-permute-start | bytes 1572872 | tf_op jit(solution)/shard_map/ppermute | solution.py:439
  11.4 0.7 collective-permute-start.3
  12.1 1.9 %shard_map.118 = f32[128,384]{1,0:T(8,128)} custom-call(bf16[128,384]{1,0:T(8,128)(2,1)} %constant.32.table_ref, f32[128,384]{1,0:T(8,128)} %rhs_ref.1), custom_call_target="tpu_custom_call" | custom-call | tf_op jit(solution)/shard_map/pallas_call | solution.py:21
  14.0 10.3 %all_to_all.5.spec_ref = f32[8,16,384]{2,1,0:T(8,128)} all-to-all(f32[8,16,384]{2,1,0:T(8,128)} %bitcast.5), channel_id=1, replica_groups=mesh['mode'=8,'elem'=4] {'mode'}, dimensions={0} | all-to-all | bytes 393216 | tf_op jit(solution)/shard_map/all_to_all | solution.py:422
  24.2 4.8 %shard_map.120 = (f32[3,7,16,128]{3,2,1,0:T(8,128)}, f32[3,16,128]{2,1,0:T(8,128)}, f32[3,16,128]{2,1,0:T(8,128)}, f32[2,16,128]{2,1,0:T(8,128)}) custom-call(f32[8,16,384]{2,1,0:T(8,128)} %all_to_all.5.spec_ref, bf16[3,128,256]{2,1,0:T(8,128)(2,1)} %get-tuple-element.24.rad_ref, bf16[3,2,128,512]{3,2,1,0:T(8,128)(2,1)} %get-tuple-element.25.face_ref, ...), custom_call_target="tpu_custom_call" | custom-call | tf_op jit(solution)/shard_map/pallas_call | solution.py:21
  29.1 0.7 collective-permute-start.1
  29.7 0.7 slice.12
  30.4 3.4 %collective-permute-start = (f32[1,16,128]{2,1,0:T(8,128)S(1)}, f32[1,16,128]{2,1,0:T(8,128)S(1)}, u32[]{:S(2)}, u32[]{:S(2)}) collective-permute-start(f32[1,16,128]{2,1,0:T(8,128)S(1)} %slice.12), channel_id=1, source_target_pairs={{0,1},{4,5},{8,9},{12,13},{16,17},{20,21},{24,25},{28,29}} | collective-permute-start | bytes 24584 | tf_op jit(solution)/shard_map/ppermute | solution.py:452
  33.9 1.3 %collective-permute-done.got_ref = f32[1,16,128]{2,1,0:T(8,128)S(1)} collective-permute-done((f32[1,16,128]{2,1,0:T(8,128)S(1)}, f32[1,16,128]{2,1,0:T(8,128)S(1)}, u32[]{:S(2)}, u32[]{:S(2)}) %collective-permute-start) | collective-permute-done | bytes 8224 | tf_op jit(solution)/shard_map/ppermute | solution.py:452
  36.3 3.2 %shard_map.121 = (f32[16,128]{1,0:T(8,128)}, f32[3,16,128]{2,1,0:T(8,128)}, f32[1,16,128]{2,1,0:T(8,128)}) custom-call(f32[1,16,128]{2,1,0:T(8,128)} %copy-done.8, f32[2,16,128]{2,1,0:T(8,128)} %copy-done.3, f32[2,16,128]{2,1,0:T(8,128)} %get-tuple-element.31.msg_ref, f32[8,128,128]{2,1,0:T(8,128)} %copy-done, f32[8,128,128]{2,1,0:T(8,128)} %copy-done.1, ...), custom_call_target="tpu_custom_call" | custom-call | tf_op jit(solution)/shard_map/pallas_call | solution.py:21
  39.5 0.7 collective-permute-start.4
  40.2 0.6 copy-done.7
  40.8 3.2 %shard_map.122 = (f32[16,128]{1,0:T(8,128)}, f32[3,16,128]{2,1,0:T(8,128)}, f32[3,16,128]{2,1,0:T(8,128)}) custom-call(f32[1,16,128]{2,1,0:T(8,128)} %copy-done.7, f32[2,16,128]{2,1,0:T(8,128)} %copy-done.3, f32[2,16,128]{2,1,0:T(8,128)} %get-tuple-element.31.msg_ref, f32[8,128,128]{2,1,0:T(8,128)} %copy-done, f32[8,128,128]{2,1,0:T(8,128)} %copy-done.1, ...), custom_call_target="tpu_custom_call" | custom-call | tf_op jit(solution)/shard_map/pallas_call | solution.py:21
  44.0 0.8 slice.14
  44.8 0.6 collective-permute-start.6
  45.5 0.6 select_select_fusion.y_ref
  46.1 0.6 copy-done.4
  46.7 2.4 %shard_map.123 = f32[1,16,128]{2,1,0:T(8,128)} custom-call(f32[1,16,128]{2,1,0:T(8,128)} %copy-done.4, f32[2,16,128]{2,1,0:T(8,128)} %get-tuple-element.31.msg_ref, f32[3,16,128]{2,1,0:T(8,128)} %select_select_fusion.y_ref, bf16[3,1024,256]{2,1,0:T(8,128)(2,1)} %get-tuple-element.26.wp_ref, bf16[2,1024,256]{2,1,0:T(8,128)(2,1)} %get-tuple-element.28.wh_ref, ...), custom_call_target="tpu_custom_call" | custom-call | tf_op jit(solution)/shard_map/pallas_call | solution.py:21
  49.0 1.3 %collective-permute-start.7 = (f32[1,16,128]{2,1,0:T(8,128)}, f32[1,16,128]{2,1,0:T(8,128)S(1)}, u32[]{:S(2)}, u32[]{:S(2)}) collective-permute-start(f32[1,16,128]{2,1,0:T(8,128)} %shard_map.123), channel_id=1, source_target_pairs={{1,0},{5,4},{9,8},{13,12},{17,16},{21,20},{25,24},{29,28}} | collective-permute-start | bytes 24584 | tf_op jit(solution)/shard_map/ppermute | solution.py:468
  50.3 19.8 %collective-permute-done.7 = f32[1,16,128]{2,1,0:T(8,128)S(1)} collective-permute-done((f32[1,16,128]{2,1,0:T(8,128)}, f32[1,16,128]{2,1,0:T(8,128)S(1)}, u32[]{:S(2)}, u32[]{:S(2)}) %collective-permute-start.7) | collective-permute-done | bytes 8224 | tf_op jit(solution)/shard_map/ppermute | solution.py:468
  70.2 0.6 select_bitcast_fusion
  70.8 0.6 collective-permute-start.5
  72.1 5.3 %shard_map.124 = (f32[16,3072]{1,0:T(8,128)}, f32[4,16,128]{2,1,0:T(8,128)}) custom-call(f32[3,7,16,128]{3,2,1,0:T(8,128)} %get-tuple-element.30.zsrc_ref, f32[16,128]{1,0:T(8,128)} %select_select_fusion.1.before_ref, f32[3,16,128]{2,1,0:T(8,128)} %select_select_fusion.y_ref, f32[16,128]{1,0:T(8,128)} %get-tuple-element.43.after_ref, ...), custom_call_target="tpu_custom_call" | custom-call | tf_op jit(solution)/shard_map/pallas_call | solution.py:21
  (27 shorter events, 1.6 us)
Async XLA Ops:
  6.5 28.8 %collective-permute-start.2 = (f32[8,128,128]{2,1,0:T(8,128)}, f32[8,128,128]{2,1,0:T(8,128)S(1)}, u32[]{:S(2)}, u32[]{:S(2)}) collective-permute-start(f32[8,128,128]{2,1,0:T(8,128)} %get-tuple-element.32), channel_id=1, source_target_pairs={{0,1},{1,2},{2,3},{4,5},{5,6},{6,7},{8,9},{9,10},{10,11},{12,13},{... | collective-permute-start | bytes 1572872 | tf_op jit(solution)/shard_map/ppermute | solution.py:439
  11.4 23.9 %collective-permute-start.3 = (f32[8,128,128]{2,1,0:T(8,128)}, f32[8,128,128]{2,1,0:T(8,128)S(1)}, u32[]{:S(2)}, u32[]{:S(2)}) collective-permute-start(f32[8,128,128]{2,1,0:T(8,128)} %get-tuple-element.32), channel_id=1, source_target_pairs={{3,2},{7,6},{11,10},{15,14},{19,18},{23,22},{27,26},{31,30}} | collective-permute-start | bytes 1572872 | tf_op jit(solution)/shard_map/ppermute | solution.py:440
  29.1 6.2 %collective-permute-start.1 = (f32[2,16,128]{2,1,0:T(8,128)}, f32[2,16,128]{2,1,0:T(8,128)S(1)}, u32[]{:S(2)}, u32[]{:S(2)}) collective-permute-start(f32[2,16,128]{2,1,0:T(8,128)} %get-tuple-element.31.msg_ref), channel_id=1, source_target_pairs={{3,2},{7,6},{11,10},{15,14},{19,18},{23,22},{27,26},{31,30}} | collective-permute-start | bytes 49160 | tf_op jit(solution)/shard_map/ppermute | solution.py:447
  30.4 4.8 %collective-permute-start = (f32[1,16,128]{2,1,0:T(8,128)S(1)}, f32[1,16,128]{2,1,0:T(8,128)S(1)}, u32[]{:S(2)}, u32[]{:S(2)}) collective-permute-start(f32[1,16,128]{2,1,0:T(8,128)S(1)} %slice.12), channel_id=1, source_target_pairs={{0,1},{4,5},{8,9},{12,13},{16,17},{20,21},{24,25},{28,29}} | collective-permute-start | bytes 24584 | tf_op jit(solution)/shard_map/ppermute | solution.py:452
  35.2 0.6 copy-start.8
  35.2 0.6 copy-start.3
  35.2 0.8 %copy-start = (f32[8,128,128]{2,1,0:T(8,128)}, f32[8,128,128]{2,1,0:T(8,128)S(1)}, u32[]{:S(2)}) copy-start(f32[8,128,128]{2,1,0:T(8,128)S(1)} %collective-permute-done.2.pprev_ref) | copy-start | bytes 1572868
  35.3 1.0 %copy-start.1 = (f32[8,128,128]{2,1,0:T(8,128)}, f32[8,128,128]{2,1,0:T(8,128)S(1)}, u32[]{:S(2)}) copy-start(f32[8,128,128]{2,1,0:T(8,128)S(1)} %collective-permute-done.3.ship_ref) | copy-start | bytes 1572868
  39.5 0.7 collective-permute-start.4
  40.1 5.3 %copy-start.2 = (f32[3,16,128]{2,1,0:T(8,128)S(1)}, f32[3,16,128]{2,1,0:T(8,128)}, u32[]{:S(2)}) copy-start(f32[3,16,128]{2,1,0:T(8,128)} %get-tuple-element.34.y_ref) | copy-start | bytes 73732
  40.2 5.3 %copy-start.6 = (f32[3,16,128]{2,1,0:T(8,128)S(1)}, f32[3,16,128]{2,1,0:T(8,128)}, u32[]{:S(2)}) copy-start(f32[3,16,128]{2,1,0:T(8,128)} %get-tuple-element.40) | copy-start | bytes 73732
  40.2 0.6 copy-start.7
  44.0 26.2 %copy-start.5 = (f32[3,16,128]{2,1,0:T(8,128)S(1)}, f32[3,16,128]{2,1,0:T(8,128)}, u32[]{:S(2)}) copy-start(f32[3,16,128]{2,1,0:T(8,128)} %get-tuple-element.36) | copy-start | bytes 73732
  44.0 27.4 %copy-start.9 = (f32[16,128]{1,0:T(8,128)S(1)}, f32[16,128]{1,0:T(8,128)}, u32[]{:S(2)}) copy-start(f32[16,128]{1,0:T(8,128)} %get-tuple-element.38) | copy-start | bytes 24580
  44.0 27.4 %copy-start.10 = (f32[16,128]{1,0:T(8,128)S(1)}, f32[16,128]{1,0:T(8,128)}, u32[]{:S(2)}) copy-start(f32[16,128]{1,0:T(8,128)} %get-tuple-element.37) | copy-start | bytes 24580
  44.8 1.3 %collective-permute-start.6 = (f32[1,16,128]{2,1,0:T(8,128)S(1)}, f32[1,16,128]{2,1,0:T(8,128)S(1)}, u32[]{:S(2)}, u32[]{:S(2)}) collective-permute-start(f32[1,16,128]{2,1,0:T(8,128)S(1)} %slice.14), channel_id=1, source_target_pairs={{2,1},{6,5},{10,9},{14,13},{18,17},{22,21},{26,25},{30,29}} | collective-permute-start | bytes 24584 | tf_op jit(solution)/shard_map/ppermute | solution.py:468
  46.1 0.6 copy-start.4
  49.0 21.1 %collective-permute-start.7 = (f32[1,16,128]{2,1,0:T(8,128)}, f32[1,16,128]{2,1,0:T(8,128)S(1)}, u32[]{:S(2)}, u32[]{:S(2)}) collective-permute-start(f32[1,16,128]{2,1,0:T(8,128)} %shard_map.123), channel_id=1, source_target_pairs={{1,0},{5,4},{9,8},{13,12},{17,16},{21,20},{25,24},{29,28}} | collective-permute-start | bytes 24584 | tf_op jit(solution)/shard_map/ppermute | solution.py:468
  70.8 0.7 collective-permute-start.5

commit v2 on v1

v2 whole, which is shorter than its diff:
```python
import functools
import math

import jax
import jax.numpy as jnp
import numpy as np
from jax import lax
from jax.experimental import pallas as pl
from jax.experimental.pallas import tpu as pltpu
from jax.sharding import PartitionSpec as P

F32 = jnp.float32
BF16 = jnp.bfloat16
VMEM = pl.BlockSpec(memory_space=pltpu.VMEM)
SMEM = pl.BlockSpec(memory_space=pltpu.SMEM)
HBM = pl.BlockSpec(memory_space=pltpu.HBM)
COST_INNER = 2**24
NN = (((1,), (0,)), ((), ()))
NT = (((1,), (1,)), ((), ()))


def call(kernel, outs, args, smem=0, anywhere=0, outside=0, scratch=(), aliases=None, cost=0):
    inside = len(args) - smem - anywhere
    spaces = [pltpu.HBM] * anywhere + [pltpu.VMEM] * inside + [pltpu.SMEM] * smem
    args = [pltpu.with_memory_space_constraint(arg, space) for arg, space in zip(args, spaces)]
    return pl.pallas_call(
        kernel,
        out_shape=outs,
        in_specs=[HBM] * anywhere + [VMEM] * inside + [SMEM] * smem,
        out_specs=[HBM if getattr(out, "memory_space", None) is pltpu.HBM else VMEM for out in outs[: len(outs) - outside]]
        + [SMEM] * outside,
        scratch_shapes=scratch,
        input_output_aliases=aliases or {},
        cost_estimate=pl.CostEstimate(flops=0, bytes_accessed=cost, transcendentals=0),
        compiler_params=pltpu.CompilerParams(vmem_limit_bytes=16 * 2**20),
    )(*args)


def split(x):
    high = x.astype(BF16)
    return high, (x - high.astype(F32)).astype(BF16)


def dot(a, b, dims=NN):
    return lax.dot_general(a, b, dims, preferred_element_type=F32)


def wide(x):
    return jnp.concatenate(split(x), axis=1)


def tall(x):
    return jnp.concatenate(split(x), axis=0)


def product(left, right):
    size = right.shape[1] // 2
    high, low = split(left)
    upper, lower = right[:, :size], right[:, size:]
    return dot(
        jnp.concatenate([high, low, high], axis=1), jnp.concatenate([upper, upper, lower], axis=0)
    )


def by_mode(x, modes):
    mode_of = lax.broadcasted_iota(jnp.int32, x.shape, 0) // 2
    spread = jnp.concatenate([jnp.where(mode_of == k, x, 0.0) for k in range(modes)], axis=1)
    return tall(spread)


def folded(out, rows):
    size = out.shape[1] // 2
    return out[:rows, :size] + out[:rows, size:] + out[rows:, :size]


def apply(x, weight, modes):
    return folded(dot(by_mode(x, modes), weight), x.shape[0])


def wave(mode_total, shape, modes, axis=0):
    first = lax.axis_index("mode") * modes
    index = first + lax.broadcasted_iota(jnp.int32, shape, axis) // 2
    number = index.astype(F32) / mode_total
    return 4.0 * number * number


def wave_of(k, mode_total, modes):
    number = (jnp.full((1, 1), lax.axis_index("mode") * modes + k, jnp.int32)).astype(F32) / mode_total
    return 4.0 * number * number


class Weights:
    def __init__(self, size, *entries):
        self.size, self.rows = size, {}
        self.total = 0
        for name, count, rows in entries:
            self.rows[name] = (self.total, rows)
            self.total += count * rows

    def at(self, name, index, mode=None):
        start, rows = self.rows[name]
        if mode is None:
            return pl.ds(start + index * rows, rows)
        return pl.ds(start + index * rows + mode * self.size, self.size)

    def pair(self, ref, name, index):
        return jnp.concatenate([ref[self.at(name, index)], ref[self.at(name, index + 1)]], axis=1)

    def face(self, ref, slab, side):
        return self.pair(ref, "face", 4 * slab + 2 * side)


def band_of(ref, slab):
    return jnp.concatenate([ref[2 * slab], ref[2 * slab + 1]], axis=1)


def whole(weight):
    size = weight.shape[1] // 2
    value = weight.astype(F32)
    return value[:, :size] + value[:, size:]


def start_copies(pairs, sems):
    copies = [pltpu.make_async_copy(src, dst, sems.at[i]) for i, (src, dst) in enumerate(pairs)]
    for copy in copies:
        copy.start()
    return copies


def transform(rhs_ref, table_ref, out_ref, rhs_buf, table_buf, sems):
    for copy in start_copies([(rhs_ref, rhs_buf), (table_ref, table_buf)], sems):
        copy.wait()
    high, low = split(rhs_buf[...])
    rhs_buf[...] = dot(table_buf[...], jnp.concatenate([high, high, low], axis=0))
    for copy in start_copies([(rhs_buf, out_ref)], sems):
        copy.wait()


def dft_kernel(rhs_ref, table_ref, old_ref, out_ref, rhs_buf, table_buf, sems):
    @pl.when(lax.axis_index("elem") != 0)
    def _():
        transform(rhs_ref, table_ref, out_ref, rhs_buf, table_buf, sems)


def far_kernel(
    modes, mode_total, panels_ref, band_ref, rhs_ref, table_ref, ship_ref, out_ref, panels_buf, band_buf, rhs_buf, table_buf, sems
):
    slabs, size = panels_ref.shape[1:3]
    elem, last = lax.axis_index("elem"), lax.axis_size("elem") - 1
    line = (panels_ref.at[:, slabs - 1], ship_ref)
    parts = sems.at[pl.ds(2, slabs + 1)]

    @pl.when(elem != last)
    def _():
        start_copies([line], parts)

    @pl.when(elem == 0)
    def _():
        transform(rhs_ref, table_ref, out_ref, rhs_buf, table_buf, sems)

    @pl.when(elem != last)
    def _():
        pltpu.make_async_copy(*line, sems.at[2]).wait()

    @pl.when(elem == last)
    def _():
        copies = start_copies(
            [(band_ref, band_buf)] + [(panels_ref.at[:, j], panels_buf.at[j]) for j in range(slabs)], parts
        )
        copies[0].wait()
        band_t = [(band_buf[0, j].T, band_buf[1, j].T) for j in range(slabs)]
        lam = [wave_of(k, mode_total, modes) for k in range(modes)]
        forward, weights = [], []
        for j in range(slabs):
            copies[1 + j].wait()
            weights.append([wide(panels_buf[j, k].T) for k in range(modes)])
            steps = [product(band_t[j][0] + lam[k] * band_t[j][1], weights[j][k]) for k in range(modes)]
            if j == 0:
                forward.append([-step for step in steps])
            else:
                forward.append([-product(forward[-1][k], wide(steps[k])) for k in range(modes)])
        current = forward[-1]
        for j in range(slabs - 2, -1, -1):
            steps = [
                product(band_buf[0, j + 1] + lam[k] * band_buf[1, j + 1], weights[j][k]) for k in range(modes)
            ]
            current = [forward[j][k] - product(current[k], wide(steps[k])) for k in range(modes)]
        for k in range(modes):
            ship_ref[k] = product(current[k], wide(band_buf[0, 0] + lam[k] * band_buf[1, 0]))


def maps_kernel(
    modes, mode_total, hub, place, panels_ref, band_ref, radial_ref, stiff_ref, mass_ref, number_ref, reig_ref, axial_ref, aeig_ref,
    coup_ref, bands_ref, front_ref, w_ref, reig_out, axial_out, weight_out, aeig_out,
    panels_buf, band_buf, radial_buf, stiff_buf, mass_buf, number_buf, axial_buf, coup_buf, bands_buf, front_buf, sems,
):
    slabs, size = panels_ref.shape[1:3]
    inner = aeig_ref.shape[1]
    copies = start_copies(
        [(radial_ref, radial_buf), (stiff_ref, stiff_buf), (mass_ref, mass_buf), (number_ref, number_buf), (band_ref, band_buf)]
        + [(panels_ref.at[:, j], panels_buf.at[j]) for j in range(slabs)]
        + [(axial_ref, axial_buf), (coup_ref, coup_buf), (aeig_ref, aeig_out), (reig_ref, reig_out)],
        sems,
    )
    for copy in copies[:4]:
        copy.wait()
    for j in range(slabs):
        radial = wide(radial_buf[j])
        w_ref[place.at("radial", j)] = radial
        parts = [wide(product(ref[j].T, radial)) for ref in (stiff_buf, mass_buf)]
        for side in range(2):
            spot = lax.broadcasted_iota(jnp.int32, (size, size), 0)
            onehot = jnp.where(number_buf[j, side : side + 1] == spot, 1.0, 0.0).astype(BF16)
            for i in range(2):
                both = jnp.concatenate([p[:, i * size : (i + 1) * size] for p in parts], axis=1)
                w_ref[place.at("face", 4 * j + 2 * side + i)] = dot(onehot, both).astype(BF16)
    copies[4].wait()
    for j in range(slabs):
        bands = wide(jnp.concatenate([band_buf[0, j], band_buf[1, j]], axis=1))
        for i in range(2):
            bands_buf[2 * j + i] = bands[:, 2 * i * size : 2 * (i + 1) * size]
    bands_copy = start_copies([(bands_buf, bands_ref)], sems)[0]
    for j in range(slabs):
        copies[5 + j].wait()
        for k in range(modes):
            w_ref[place.at("panel", j, k)] = wide(panels_buf[j, k].T)
    for copy in copies[5 + slabs :]:
        copy.wait()
    for j in range(slabs):
        for b in range(inner):
            for a in range(inner):
                axial_out[j, a, b] = axial_buf[j, a, b]
            for side in range(2):
                weight = coup_buf[j, side, 0] * axial_buf[j, 0, b]
                for a in range(1, inner):
                    weight = weight + coup_buf[j, side, a] * axial_buf[j, a, b]
                weight_out[j, side, b] = weight

    @pl.when((lax.axis_index("elem") > 0) & (lax.axis_index("elem") <= hub))
    def _():
        lam = [wave_of(k, mode_total, modes) for k in range(modes)]
        current = None
        for j in range(slabs):
            first, second = band_buf[0, j].T, band_buf[1, j].T
            steps = [product(first + lam[k] * second, w_ref[place.at("panel", j, k)]) for k in range(modes)]
            if current is None:
                current = [-step for step in steps]
            else:
                current = [-product(current[k], wide(steps[k])) for k in range(modes)]
        for k in range(modes):
            front_buf[pl.ds(k * size, size)] = wide(current[k])
        for copy in start_copies([(front_buf, front_ref)], sems.at[pl.ds(1, 1)]):
            copy.wait()

    bands_copy.wait()


def face_push(values, weight, lam):
    rows, size = values.shape
    high, low = split(values)
    blocks = [weight[:, i * size : (i + 1) * size] for i in range(4)]
    out = dot(
        jnp.concatenate([high, low], axis=0), jnp.concatenate(blocks, axis=0), NT
    )
    out = out[:rows, : 2 * size] + out[:rows, 2 * size :] + out[rows:, : 2 * size]
    return out[:, :size] + lam * out[:, size:]


def face_lift(values, weight, lam):
    rows, size = values.shape
    out = folded(dot(tall(values), weight), rows)
    return out[:, :size] + lam * out[:, size:]


def block_of(spec_ref, index, size):
    per = spec_ref.shape[2] // size
    at = index % per * size
    return spec_ref[index // per, :, at : at + size]


def band_step(values, weight, lam):
    return face_push(values, weight, lam)


def inner_kernel(
    modes, mode_total, place, first_call, bands_ref, spec_ref, w_ref, reig_ref, *refs
):
    axial_ref, weight_ref, aeig_ref, bands_out, zsrc_ref, inv_ref, reduced_ref, y_ref, out_ref, sems = refs[-10:]

    @pl.when((lax.axis_index("elem") == 0) == first_call)
    def _():
        inner_part(
            modes, mode_total, place, first_call, bands_ref, spec_ref, w_ref, reig_ref, axial_ref, weight_ref, aeig_ref,
            bands_out, zsrc_ref, inv_ref, reduced_ref, y_ref, out_ref, sems,
        )


def inner_part(
    modes, mode_total, place, first_call, bands_ref, spec_ref, w_ref, reig_ref, axial_ref, weight_ref, aeig_ref,
    bands_out, zsrc_ref, inv_ref, solved_ref, y_ref, out_ref, sems,
):
    slabs, inner, rows, size = zsrc_ref.shape
    lam = wave(mode_total, (rows, size), modes)
    elem, last = lax.axis_index("elem"), lax.axis_size("elem") - 1
    bands_copy = start_copies([(bands_ref, bands_out)], sems)[0]
    pushed = []
    for j in range(slabs):
        source = jnp.concatenate(
            [block_of(spec_ref, j * (inner + 1) + a, size) for a in range(inner)], axis=0
        )
        first = folded(dot(tall(source), w_ref[place.at("radial", j)]), inner * rows)
        first = [first[a * rows : (a + 1) * rows] for a in range(inner)]
        sums = [None, None]
        for b in range(inner):
            value = first[0] * axial_ref[j, 0, b]
            for a in range(1, inner):
                value = value + first[a] * axial_ref[j, a, b]
            inverse = 1.0 / (aeig_ref[j, b] + reig_ref[j : j + 1] + lam)
            inv_ref[j, b] = inverse
            value = value * inverse
            zsrc_ref[j, b] = value
            for side in range(2):
                term = value * weight_ref[j, side, b]
                sums[side] = term if sums[side] is None else sums[side] + term
        pushed.append([face_push(sums[side], place.face(w_ref, j, side), lam) for side in range(2)])
    load = pushed[0][0]
    bands_copy.wait()
    values = []
    for j in range(slabs):
        reduced = block_of(spec_ref, j * (inner + 1) + inner, size) - pushed[j][1]
        if j + 1 < slabs:
            reduced = reduced - pushed[j + 1][0]
        panel = w_ref[place.at("panel", j)]
        solved_ref[j] = reduced
        if j > 0:
            reduced = reduced - band_step(values[-1], band_of(bands_out, j), lam)
        values.append(apply(reduced, panel, modes))
        y_ref[j] = values[j]
    if first_call:
        out_ref[...] = values[slabs - 1]
        return
    out_ref[1] = load

    @pl.when(elem == last)
    def _():
        current = values[slabs - 1]
        for j in range(slabs - 2, -1, -1):
            step = face_lift(current, band_of(bands_out, j + 1), lam)
            current = values[j] - apply(step, w_ref[place.at("panel", j)], modes)
        out_ref[0] = load + face_lift(current, band_of(bands_out, 0), lam)


def previous_weight(panel_ref, modes):
    parts = [split(panel_ref[k]) for k in range(modes)]
    return jnp.concatenate(
        [jnp.concatenate([p[i] for p in parts], axis=1) for i in range(2)], axis=0
    )


def apply_nt(x, weight, modes):
    return folded(dot(by_mode(x, modes), weight, NT), x.shape[0])


def forward_values(before, solved_ref, ahead_ref, modes):
    values = []
    for j in range(solved_ref.shape[0]):
        before = solved_ref[j] - apply(before, ahead_ref[j], modes)
        values.append(before)
    return values


def backward_values(values, after, panel, behind_ref, modes):
    slabs = len(values)
    out = [None] * slabs
    out[-1] = values[-1]
    if after is not None:
        out[-1] = out[-1] - apply(after, panel, modes)
    for j in range(slabs - 2, -1, -1):
        out[j] = values[j] - apply(out[j + 1], behind_ref[j], modes)
    return out


def push_kernel(modes, hub, pprev_ref, front_ref, load_ref, front_out, prev_ref, push_ref, prev_buf, sems):
    elem = lax.axis_index("elem")

    @pl.when((elem > 0) & (elem <= hub))
    def _():
        for copy in start_copies([(pprev_ref, prev_buf), (front_ref, front_out)], sems):
            copy.wait()
        weight = previous_weight(prev_buf, modes)
        prev_ref[...] = weight
        push_ref[...] = apply_nt(load_ref[1], weight, modes)


def forward_kernel(modes, at, got_ref, push_ref, y_ref, front_ref, old_ref, state_ref, send_ref):
    @pl.when(lax.axis_index("elem") == at)
    def _():
        before = got_ref[...] - push_ref[...]
        state_ref[0] = before
        send_ref[...] = y_ref[y_ref.shape[0] - 1] + apply(before, front_ref[...], modes)


def backward_map_kernel(modes, mode_total, hub, hub_call, *refs):
    inputs, outputs = refs[:9], refs[-(12 if hub_call else 13) :]

    @pl.when((lax.axis_index("elem") == hub) == hub_call)
    def _():
        backward_maps(modes, mode_total, hub, hub_call, *inputs, *outputs)


def backward_maps(
    modes, mode_total, hub, hub_call, band_ref, radial_ref, map_ref, state_ref, load_ref, reduced_ref, y_ref, panel_ref, bands_ref,
    ahead_ref, behind_ref, radt_ref, solved_ref, back_ref, base_ref, *rest,
):
    *rest, band_buf, radial_buf, map_buf, sems = rest
    elem = lax.axis_index("elem")
    slabs, rows, size = reduced_ref.shape
    lam = wave(mode_total, (rows, size), modes)
    waves = [wave_of(k, mode_total, modes) for k in range(modes)]
    pairs = [(band_ref, band_buf), (radial_ref, radial_buf)]
    copies = start_copies(pairs + [(map_ref, map_buf)] if hub_call else pairs, sems)

    def part(k):
        return pl.ds(k * size, size)

    for j in range(slabs):
        solved_ref[j] = apply(reduced_ref[j], panel_ref[pl.ds(j * modes * size, modes * size)], modes)
    for copy in copies[:2]:
        copy.wait()
    for j in range(slabs):
        radt_ref[j] = wide(radial_buf[j].T)
    for j in range(slabs):
        first, second = band_buf[0, j].T, band_buf[1, j].T
        for k in range(modes):
            ahead_ref[j, part(k)] = wide(product(first + waves[k] * second, panel_ref[part(j * modes + k)]))
    for j in range(slabs - 1):
        for k in range(modes):
            behind_ref[j, part(k)] = wide(
                product(band_buf[0, j + 1] + waves[k] * band_buf[1, j + 1], panel_ref[part(j * modes + k)])
            )

    def entry(k):
        return wide(band_buf[0, 0] + waves[k] * band_buf[1, 0])

    def back_maps(outs):
        current = [-whole(panel_ref[part((slabs - 1) * modes + k)]) for k in range(modes)]
        for j in range(slabs - 2, -1, -1):
            current = [-product(current[k], behind_ref[j, part(k)]) for k in range(modes)]
            for k in range(modes):
                if outs:
                    outs[j][part(k)] = wide(current[k])

        @pl.when(elem > 0)
        def _():
            for k in range(modes):
                back_ref[part(k)] = wide(product(current[k], entry(k)))

    def base(values, found_ref):
        found = backward_values(values, None, None, behind_ref, modes)
        if found_ref is not None:
            for j in range(slabs):
                found_ref[j] = found[j]
        base_ref[...] = load_ref[1] + face_lift(found[0], band_of(bands_ref, 0), lam)

    if hub_call:
        cross_ref, far_weight_ref = rest
        base([y_ref[j] for j in range(slabs)], None)
        back_maps(None)
        forward = [[-whole(ahead_ref[0, part(k)]) for k in range(modes)]]
        for j in range(1, slabs):
            forward.append([-product(forward[-1][k], ahead_ref[j, part(k)]) for k in range(modes)])
        current = forward[-1]
        for j in range(slabs - 2, -1, -1):
            current = [forward[j][k] - product(current[k], behind_ref[j, part(k)]) for k in range(modes)]
        for k in range(modes):
            cross_ref[part(k)] = wide(product(current[k], entry(k)))
        copies[2].wait()
        for k in range(modes):
            far_weight_ref[part(k)] = wide(map_buf[k])
        return
    near_ref, mid_ref, found_ref = rest

    @pl.when(elem < hub)
    def _():
        back_maps({0: near_ref, 1: mid_ref})

    @pl.when(elem == 0)
    def _():
        base([y_ref[j] for j in range(slabs)], found_ref)

    @pl.when((elem > 0) & (elem < hub))
    def _():
        base(forward_values(state_ref[0], solved_ref, ahead_ref, modes), found_ref)


def hub_kernel(
    modes, at, place, got_ref, push_ref, far_ref, far_weight_ref, y_ref, front_ref, back_ref, cross_ref, base_ref, w_ref, old_ref,
    state_ref, send_ref, last_ref,
):
    slabs = y_ref.shape[0]

    @pl.when(lax.axis_index("elem") == at)
    def _():
        panel = w_ref[place.at("panel", slabs - 1)]
        load = apply(far_ref[1], panel, modes)
        value = y_ref[slabs - 1]
        out = base_ref[...]
        if at > 0:
            before = got_ref[...] - push_ref[...]
            state_ref[0] = before
            value = value + apply(before, front_ref[...], modes)
            out = out + apply(before, cross_ref[...], modes)
        final = value - load
        after = far_ref[0] + apply(final, far_weight_ref[...], modes)
        state_ref[1] = after
        send_ref[...] = out + apply(after, back_ref[...], modes)
        last_ref[0] = final
        last_ref[1] = value - apply(after, panel, modes)


def backward_kernel(modes, at, got_ref, base_ref, back_ref, old_ref, state_ref, send_ref):
    @pl.when(lax.axis_index("elem") == at)
    def _():
        after = got_ref[...]
        state_ref[1] = after
        send_ref[...] = base_ref[...] + apply(after, back_ref[...], modes)


def final_kernel(
    modes, mode_total, hub, place, zsrc_ref, inv_ref, state_ref, got_ref, last_ref, found_ref, near_ref, mid_ref, solved_ref, prev_ref, w_ref, bands_ref, ahead_ref,
    behind_ref, radt_ref, axial_ref, weight_ref, out_ref, x_ref,
):
    slabs, inner, rows, size = zsrc_ref.shape
    lam = wave(mode_total, (rows, size), modes)
    elem, last = lax.axis_index("elem"), lax.axis_size("elem") - 1
    maps = {0: near_ref, 1: mid_ref}

    def backward(after):
        for j in range(slabs - 1):
            x_ref[j + 1] = found_ref[j] + apply(after, maps[j][...], modes)
        x_ref[slabs] = found_ref[slabs - 1] - apply(after, w_ref[place.at("panel", slabs - 1)], modes)

    def before_first(before):
        back = face_lift(x_ref[1], band_of(bands_ref, 0), lam)
        x_ref[0] = before - apply_nt(back, prev_ref[...], modes)

    @pl.when(elem == 0)
    def _():
        x_ref[0] = jnp.zeros((rows, size), F32)
        backward(got_ref[...])

    @pl.when((elem > 0) & (elem < hub))
    def _():
        backward(state_ref[1])
        before_first(state_ref[0])

    @pl.when(elem == hub)
    def _():
        values = forward_values(state_ref[0], solved_ref, ahead_ref, modes)
        found = backward_values(values, state_ref[1], w_ref[place.at("panel", slabs - 1)], behind_ref, modes)
        for j in range(slabs):
            x_ref[j + 1] = found[j]
        before_first(state_ref[0])

    @pl.when(elem == last)
    def _():
        values = forward_values(last_ref[0], solved_ref, ahead_ref, modes)
        found = backward_values(values, None, None, behind_ref, modes)
        for j in range(slabs):
            x_ref[j + 1] = found[j]
        x_ref[0] = last_ref[1]

    for j in range(slabs):
        lifted = [face_lift(x_ref[j + side], place.face(w_ref, j, side), lam) for side in range(2)]
        kept = []
        for b in range(inner):
            total = lifted[0] * weight_ref[j, 0, b] + lifted[1] * weight_ref[j, 1, b]
            kept.append(zsrc_ref[j, b] - total * inv_ref[j, b])
        values = []
        for a in range(inner):
            value = kept[0] * axial_ref[j, a, 0]
            for b in range(1, inner):
                value = value + kept[b] * axial_ref[j, a, b]
            values.append(value)
        result = dot(tall(jnp.concatenate(values, axis=0)), radt_ref[j])
        result = folded(result, inner * rows)
        for a in range(inner):
            at = (j * (inner + 1) + a) * size
            out_ref[:, at : at + size] = result[a * rows : (a + 1) * rows]
        at = (j * (inner + 1) + inner) * size
        out_ref[:, at : at + size] = x_ref[j + 1]


def dft_table(planes):
    row, col = np.arange(planes)[:, None], np.arange(planes)[None]
    angle = row // 2 * col % planes * (2.0 * math.pi / planes)
    table = np.where(row % 2 == 0, np.cos(angle), -np.sin(angle)) / math.sqrt(planes)
    table = jnp.asarray(table, F32)
    high, low = split(table)
    return jnp.concatenate([high, low, high], axis=1)


def body(
    rhs_phys, radial_basis, axial_basis, radial_eig, axial_eig, face_stiff, face_mass, axial_coupling, face_numbering,
    band_panels, inverse_panels,
):
    planes, nodes = rhs_phys.shape
    modes, slabs, size, _ = inverse_panels.shape
    inner = axial_basis.shape[1]
    devices = lax.axis_size("mode")
    elems = lax.axis_size("elem")
    mode_total = modes * devices
    rows = 2 * modes
    hub = elems - 2
    last = elems - 1

    def shape(*dims):
        return jax.ShapeDtypeStruct(dims, F32)

    def kept(*dims):
        return pltpu.VMEM(dims, F32)

    def half(*dims):
        return pltpu.VMEM(dims, BF16)

    table = dft_table(planes)
    many = modes * size
    place = Weights(size, ("panel", slabs, many), ("radial", slabs, size), ("face", 4 * slabs, size))
    ship, spectrum = call(
        functools.partial(far_kernel, modes, mode_total),
        [shape(modes, size, size), pltpu.HBM((planes, nodes), F32)],
        [inverse_panels, band_panels, rhs_phys, table],
        anywhere=4,
        scratch=[
            pltpu.VMEM((slabs, modes, size, size), F32),
            pltpu.VMEM(band_panels.shape, F32),
            pltpu.VMEM(rhs_phys.shape, F32),
            pltpu.VMEM(table.shape, BF16),
            pltpu.SemaphoreType.DMA((slabs + 3,)),
        ],
    )
    far_map = lax.ppermute(ship, "elem", [(last, hub)])
    pprev = lax.ppermute(ship, "elem", [(i, i + 1) for i in range(hub)])
    spectrum = call(
        dft_kernel,
        [pltpu.HBM((planes, nodes), F32)],
        [rhs_phys, table, spectrum],
        anywhere=3,
        scratch=[pltpu.VMEM(rhs_phys.shape, F32), pltpu.VMEM(table.shape, BF16), pltpu.SemaphoreType.DMA((2,))],
        aliases={2: 0},
    )[0]
    spectrum = lax.all_to_all(spectrum.reshape(devices, rows, nodes), "mode", 0, 0, tiled=False)
    if nodes % size:
        spectrum = jnp.swapaxes(spectrum, 0, 1).reshape(1, rows, devices * nodes)
    vector = (rows, size)
    matrix = half(many, 2 * size)
    bands, front, w, reig, axial, weight, aeig = call(
        functools.partial(maps_kernel, modes, mode_total, hub, place),
        [
            pltpu.HBM((2 * slabs, size, 2 * size), BF16),
            pltpu.HBM((many, 2 * size), BF16),
            half(place.total, 2 * size),
            kept(*radial_eig.shape),
            pltpu.SMEM(axial_basis.shape, F32),
            pltpu.SMEM((slabs, 2, inner), F32),
            pltpu.SMEM(axial_eig.shape, F32),
        ],
        [
            inverse_panels, band_panels, radial_basis, face_stiff, face_mass, face_numbering,
            radial_eig, axial_basis, axial_eig, axial_coupling,
        ],
        anywhere=10,
        outside=3,
        scratch=[
            pltpu.VMEM((slabs, modes, size, size), F32),
            pltpu.VMEM(band_panels.shape, F32),
            pltpu.VMEM(radial_basis.shape, F32),
            pltpu.VMEM(face_stiff.shape, F32),
            pltpu.VMEM(face_mass.shape, F32),
            pltpu.VMEM(face_numbering.shape, jnp.int32),
            pltpu.SMEM(axial_basis.shape, F32),
            pltpu.SMEM(axial_coupling.shape, F32),
            pltpu.VMEM((2 * slabs, size, 2 * size), BF16),
            pltpu.VMEM((many, 2 * size), BF16),
            pltpu.SemaphoreType.DMA((slabs + 9,)),
        ],
    )
    solves = [
        half(2 * slabs, size, 2 * size), kept(slabs, inner, *vector), kept(slabs, inner, *vector), kept(slabs, *vector),
        kept(slabs, *vector),
    ]
    *solve, send = call(
        functools.partial(inner_kernel, modes, mode_total, place, True),
        solves + [kept(*vector)],
        [bands, spectrum, w, reig, axial, weight, aeig],
        anywhere=1,
        smem=3,
        scratch=[pltpu.SemaphoreType.DMA((1,))],
    )
    got = lax.ppermute(send, "elem", [(0, 1)])
    bands, zsrc, inv, reduced, y, load = call(
        functools.partial(inner_kernel, modes, mode_total, place, False),
        solves + [kept(2, *vector)],
        [bands, spectrum, w, reig, *solve, axial, weight, aeig],
        anywhere=1,
        smem=3,
        scratch=[pltpu.SemaphoreType.DMA((1,))],
        aliases={4 + i: i for i in range(5)},
    )
    far = lax.ppermute(load, "elem", [(last, hub)])
    front, prev, push = call(
        functools.partial(push_kernel, modes, hub),
        [matrix, half(2 * size, many), kept(*vector)],
        [pprev, front, load],
        anywhere=2,
        scratch=[pltpu.VMEM((modes, size, size), F32), pltpu.SemaphoreType.DMA((2,))],
    )
    state = jnp.zeros((2, *vector), F32)
    for at in range(1, hub):
        state, send = call(
            functools.partial(forward_kernel, modes, at),
            [kept(*state.shape), shape(*vector)],
            [got, push, y, front, state],
            aliases={4: 0},
        )
        got = lax.ppermute(send, "elem", [(at, at + 1)])
    maps = [
        half(slabs, many, 2 * size), half(slabs - 1, many, 2 * size), half(slabs, size, 2 * size), kept(slabs, *vector),
        matrix, kept(*vector),
    ]
    scratch = [
        pltpu.VMEM(band_panels.shape, F32),
        pltpu.VMEM(radial_basis.shape, F32),
        pltpu.VMEM((modes, size, size), F32),
        pltpu.SemaphoreType.DMA((3,)),
    ]
    *known, cross, far_weight = call(
        functools.partial(backward_map_kernel, modes, mode_total, hub, True),
        maps + [matrix, matrix],
        [band_panels, radial_basis, far_map, state, load, reduced, y, w, bands],
        anywhere=3,
        scratch=scratch,
    )
    state, send, final = call(
        functools.partial(hub_kernel, modes, hub, place),
        [kept(*state.shape), shape(*vector), shape(2, *vector)],
        [got, push, far, far_weight, y, front, known[4], cross, known[5], w, state],
        aliases={10: 0},
    )
    ahead, behind, radt, solved, back, base, near, mid, found = call(
        functools.partial(backward_map_kernel, modes, mode_total, hub, False),
        maps + [matrix, matrix, kept(slabs, *vector)],
        [band_panels, radial_basis, far_map, state, load, reduced, y, w, bands, *known],
        anywhere=3,
        scratch=scratch,
        aliases={9 + i: i for i in range(6)},
    )
    got = send
    for at in range(hub - 1, -1, -1):
        got = lax.ppermute(send, "elem", [(at + 1, at)])
        if at > 0:
            state, send = call(
                functools.partial(backward_kernel, modes, at),
                [kept(*state.shape), shape(*vector)],
                [got, base, back, state],
                aliases={3: 0},
            )
    final = lax.ppermute(final, "elem", [(hub, last)])
    return call(
        functools.partial(final_kernel, modes, mode_total, hub, place),
        [shape(rows, slabs * (inner + 1) * size)],
        [zsrc, inv, state, got, final, found, near, mid, solved, prev, w, bands, ahead, behind, radt, axial, weight],
        smem=2,
        scratch=[pltpu.VMEM((slabs + 1, *vector), F32)],
    )[0]


def solution(mesh):
    placed = (
        P(None, ("elem", "mode")),
        P("elem", None, None),
        P("elem", None, None),
        P("elem", None),
        P("elem", None),
        P("elem", None, None),
        P("elem", None, None),
        P("elem", None, None),
        P("elem", None, None),
        P(None, "elem", None, None),
        P("mode", "elem", None, None),
    )
    return jax.shard_map(
        body, mesh=mesh, in_specs=placed, out_specs=P("mode", "elem"), check_vma=False
    )
```

time: 77.9 us -> 42.2 us (0.54)
  Pallas kernels: 27.3 us -> 13.9 us
  blocking collectives: 10.3 us -> 0 us
  waiting for transfers between devices: 21.2 us -> 11.9 us
  local copies, waits for them, and re-layouts: 3.65 us -> 0.01 us
  starting transfers between devices: 13 us -> 15.8 us
  other arithmetic: 1.8 us -> 0 us
    pallas_call x7 -> x12, Pallas kernels: 27.3 us -> 13.9 us  [call(): pl.pallas_call(kernel, out_shape=outs, in_specs=[HBM] * anywhere + [VMEM]...]
    ppermute x2, waiting for transfers between devices: 19.8 us -> 8.36 us  [body(): got = lax.ppermute(send, 'elem', [(at + 1, at)])]
    all_to_all x1 -> x0, blocking collectives: 10.3 us -> none  [body(): lax.all_to_all(spectrum.reshape(devices, rows, nodes), 'mode', 0, 0, tile...]
    all_to_all x0 -> x1, starting transfers between devices: none -> 3.74 us  [body(): lax.all_to_all(spectrum.reshape(devices, rows, nodes), 'mode', 0, 0, tile...]
    all_to_all x0 -> x1, waiting for transfers between devices: none -> 2.92 us  [body(): lax.all_to_all(spectrum.reshape(devices, rows, nodes), 'mode', 0, 0, tile...]
    unnamed x22 -> x0, local copies, waits for them, and re-layouts: 2.19 us -> none
    select_n x3 -> x0, other arithmetic: 1.8 us -> none  [the longest x1 0.62 us: body(): values = jnp.where(here == at, values_new, values)]
    slice x2 -> x0, local copies, waits for them, and re-layouts: 1.46 us -> none  [the longest x1 0.76 us: body(): send = out[:1]]
  transfers between devices with their start and end apart: 8 -> 9, of which waited for: 2 -> 3; matrix products, arithmetic and copies ran while one was open for 2% -> 0% of each run, Pallas kernels for 9% -> 24%
where the time goes in v2:
time: 42.2 us; the launch traced here: 41.7 us
  starting transfers between devices  15.8 us (37%)
  Pallas kernels  13.9 us (33%)
  waiting for transfers between devices  11.9 us (28%)
    pallas_call x12, Pallas kernels, call(): pl.pallas_call(kernel, out_shape=outs, in_specs=[HBM] * anywhere + [VMEM]...  13.9 us
    ppermute x2, waiting for transfers between devices, body(): got = lax.ppermute(send, 'elem', [(at + 1, at)])  8.36 us
    ppermute x1, starting transfers between devices, body(): pprev = lax.ppermute(ship, 'elem', [(i, i + 1) for i in range(hub)])  4.78 us
    all_to_all x1, starting transfers between devices, body(): lax.all_to_all(spectrum.reshape(devices, rows, nodes), 'mode', 0, 0, tile...  3.74 us
    all_to_all x1, waiting for transfers between devices, body(): lax.all_to_all(spectrum.reshape(devices, rows, nodes), 'mode', 0, 0, tile...  2.92 us
    ppermute x2, starting transfers between devices, body(): got = lax.ppermute(send, 'elem', [(at + 1, at)])  1.95 us
    ppermute x1, starting transfers between devices, body(): got = lax.ppermute(send, 'elem', [(0, 1)])  1.9 us
    ppermute x1, starting transfers between devices, body(): far_map = lax.ppermute(ship, 'elem', [(last, hub)])  1.46 us
  transfers between devices with their start and end apart: 9, of which 3 were waited for; matrix products, arithmetic and copies ran while one was open for 0% of the time, Pallas kernels for 24%

profile of v2, /device:TPU:0, one launch (start us, length us, event | category | flops | bytes accessed | tf_op | source)
XLA Modules:
  0.0 41.7 jit_solution(18441733757610315668)
XLA Ops:
  0.0 2.1 %shard_map.119 = (f32[8,128,128]{2,1,0:T(8,128)S(1)}, f32[128,384]{1,0:T(8,128)}) custom-call(f32[8,3,128,128]{3,2,1,0:T(8,128)} %panels_ref.3, f32[2,3,128,128]{3,2,1,0:T(8,128)} %refs_0_.3, f32[128,384]{1,0:T(8,128)} %rhs_ref.3, bf16[128,384]{1,0:T(8,128)(2,1)} %constant.19.table_ref), custom_call_target="tpu_custom_call" | custom-call | tf_op jit(solution)/shard_map/pallas_call | solution.py:26
  2.1 4.8 %collective-permute-start.1 = (f32[8,128,128]{2,1,0:T(8,128)S(1)}, f32[8,128,128]{2,1,0:T(8,128)}, u32[]{:S(2)}, u32[]{:S(2)}) collective-permute-start(f32[8,128,128]{2,1,0:T(8,128)S(1)} %get-tuple-element.68), channel_id=1, source_target_pairs={{0,1},{1,2},{4,5},{5,6},{8,9},{9,10},{12,13},{13,14},{16,17},{17,1... | collective-permute-start | bytes 1572872 | tf_op jit(solution)/shard_map/ppermute | solution.py:643
  6.8 1.5 %collective-permute-start.4 = (f32[8,128,128]{2,1,0:T(8,128)S(1)}, f32[8,128,128]{2,1,0:T(8,128)}, u32[]{:S(2)}, u32[]{:S(2)}) collective-permute-start(f32[8,128,128]{2,1,0:T(8,128)S(1)} %get-tuple-element.68), channel_id=1, source_target_pairs={{3,2},{7,6},{11,10},{15,14},{19,18},{23,22},{27,26},{31,30}} | collective-permute-start | bytes 1572872 | tf_op jit(solution)/shard_map/ppermute | solution.py:642
  8.3 3.7 %all-to-all-start = ((f32[8,16,384]{2,1,0:T(8,128)}), f32[8,16,384]{2,1,0:T(8,128)S(1)}, u32[]{:S(2)}, u32[]{:S(2)}) async-start(f32[8,16,384]{2,1,0:T(8,128)} %bitcast.1), calls=%async_computation | async-start | bytes 393216 | tf_op jit(solution)/shard_map/all_to_all | solution.py:652
  12.1 3.3 %shard_map.118 = (bf16[6,128,256]{2,1,0:T(8,128)(2,1)}, bf16[1024,256]{1,0:T(8,128)(2,1)}, bf16[4992,256]{1,0:T(8,128)(2,1)S(1)}, f32[3,128]{1,0:T(4,128)S(1)}, ...) custom-call(f32[8,3,128,128]{3,2,1,0:T(8,128)} %panels_ref.3, f32[2,3,128,128]{3,2,1,0:T(8,128)} %refs_0_.3, ...), custom_call_target="tpu_custom_call" | custom-call | tf_op jit(solution)/shard_map/pallas_call | solution.py:26
  15.4 2.9 %all-to-all-done.spec_ref = f32[8,16,384]{2,1,0:T(8,128)S(1)} async-done(((f32[8,16,384]{2,1,0:T(8,128)}), f32[8,16,384]{2,1,0:T(8,128)S(1)}, u32[]{:S(2)}, u32[]{:S(2)}) %all-to-all-start) | async-done | bytes 196640 | tf_op jit(solution)/shard_map/all_to_all | solution.py:652
  18.3 2.7 %shard_map.121 = (bf16[6,128,256]{2,1,0:T(8,128)(2,1)S(1)}, f32[3,7,16,128]{3,2,1,0:T(8,128)S(1)}, f32[3,7,16,128]{3,2,1,0:T(8,128)S(1)}, f32[3,16,128]{2,1,0:T(...) custom-call(bf16[6,128,256]{2,1,0:T(8,128)(2,1)} %get-tuple-element.53.bands_ref, ...), custom_call_target="tpu_custom_call" | custom-call | tf_op jit(solution)/shard_map/pallas_call | solution.py:26
  21.0 1.9 %collective-permute-start = (f32[16,128]{1,0:T(8,128)S(1)}, f32[16,128]{1,0:T(8,128)S(1)}, u32[]{:S(2)}, u32[]{:S(2)}) collective-permute-start(f32[16,128]{1,0:T(8,128)S(1)} %get-tuple-element.67), channel_id=1, source_target_pairs={{0,1},{4,5},{8,9},{12,13},{16,17},{20,21},{24,25},{28,29}} | collective-permute-start | bytes 24584 | tf_op jit(solution)/shard_map/ppermute | solution.py:700
  22.9 0.7 %collective-permute-start.3 = (f32[2,16,128]{2,1,0:T(8,128)S(1)}, f32[2,16,128]{2,1,0:T(8,128)S(1)}, u32[]{:S(2)}, u32[]{:S(2)}) collective-permute-start(f32[2,16,128]{2,1,0:T(8,128)S(1)} %get-tuple-element.70.load_ref.refs_4_), channel_id=1, source_target_pairs={{3,2},{7,6},{11,10},{15,14},{19,18},{23,22},{27,26},{31,30}} | collective-permute-start | bytes 49160 | tf_op jit(solution)/shard_map/ppermute | solution.py:710
  23.6 0.0 collective-permute-done.1.pprev_ref
  23.6 0.6 %collective-permute-done.got_ref = f32[16,128]{1,0:T(8,128)S(1)} collective-permute-done((f32[16,128]{1,0:T(8,128)S(1)}, f32[16,128]{1,0:T(8,128)S(1)}, u32[]{:S(2)}, u32[]{:S(2)}) %collective-permute-start) | collective-permute-done | bytes 8224 | tf_op jit(solution)/shard_map/ppermute | solution.py:700
  24.2 0.6 %collective-permute-start.2 = (f32[16,128]{1,0:T(8,128)S(1)}, f32[16,128]{1,0:T(8,128)S(1)}, u32[]{:S(2)}, u32[]{:S(2)}) collective-permute-start(f32[16,128]{1,0:T(8,128)S(1)} %get-tuple-element.74), channel_id=1, source_target_pairs={{1,2},{5,6},{9,10},{13,14},{17,18},{21,22},{25,26},{29,30}} | collective-permute-start | bytes 24584 | tf_op jit(solution)/shard_map/ppermute | solution.py:726
  24.9 0.0 collective-permute-done.4.refs_2_
  24.9 0.2 shard_map.125
  25.1 0.0 collective-permute-done.3.far_ref
  25.2 0.0 collective-permute-done.2.got_ref
  25.2 0.7 %collective-permute-start.5 = (f32[16,128]{1,0:T(8,128)S(1)}, f32[16,128]{1,0:T(8,128)S(1)}, u32[]{:S(2)}, u32[]{:S(2)}) collective-permute-start(f32[16,128]{1,0:T(8,128)S(1)} %get-tuple-element.82), channel_id=1, source_target_pairs={{2,1},{6,5},{10,9},{14,13},{18,17},{22,21},{26,25},{30,29}} | collective-permute-start | bytes 24584 | tf_op jit(solution)/shard_map/ppermute | solution.py:760
  25.9 0.7 %collective-permute-start.7 = (f32[2,16,128]{2,1,0:T(8,128)S(1)}, f32[2,16,128]{2,1,0:T(8,128)S(1)}, u32[]{:S(2)}, u32[]{:S(2)}) collective-permute-start(f32[2,16,128]{2,1,0:T(8,128)S(1)} %get-tuple-element.92), channel_id=1, source_target_pairs={{2,3},{6,7},{10,11},{14,15},{18,19},{22,23},{26,27},{30,31}} | collective-permute-start | bytes 49160 | tf_op jit(solution)/shard_map/ppermute | solution.py:768
  26.5 3.7 %shard_map.127 = (bf16[3,1024,256]{2,1,0:T(8,128)(2,1)S(1)}, bf16[2,1024,256]{2,1,0:T(8,128)(2,1)S(1)}, bf16[3,128,256]{2,1,0:T(8,128)(2,1)S(1)}, f32[3,16,128]{...) custom-call(f32[2,3,128,128]{3,2,1,0:T(8,128)} %refs_0_.3, ...), custom_call_target="tpu_custom_call", output_to_operand_aliasing={{0}: (9, {}), {1}: (10, {}), {2}: (11, {}), {3}: (12, {}), ... | custom-call | tf_op jit(solution)/shard_map/pallas_call | solution.py:26
  30.3 0.0 collective-permute-done.5.got_ref
  30.3 1.3 %collective-permute-start.6 = (f32[16,128]{1,0:T(8,128)S(1)}, f32[16,128]{1,0:T(8,128)S(1)}, u32[]{:S(2)}, u32[]{:S(2)}) collective-permute-start(f32[16,128]{1,0:T(8,128)S(1)} %get-tuple-element.91), channel_id=1, source_target_pairs={{1,0},{5,4},{9,8},{13,12},{17,16},{21,20},{25,24},{29,28}} | collective-permute-start | bytes 24584 | tf_op jit(solution)/shard_map/ppermute | solution.py:760
  31.6 0.0 collective-permute-done.7.last_ref
  31.6 8.4 %collective-permute-done.6.got_ref = f32[16,128]{1,0:T(8,128)S(1)} collective-permute-done((f32[16,128]{1,0:T(8,128)S(1)}, f32[16,128]{1,0:T(8,128)S(1)}, u32[]{:S(2)}, u32[]{:S(2)}) %collective-permute-start.6) | collective-permute-done | bytes 8224 | tf_op jit(solution)/shard_map/ppermute | solution.py:760
  40.0 1.8 %shard_map.129 = f32[16,3072]{1,0:T(8,128)} custom-call(f32[3,7,16,128]{3,2,1,0:T(8,128)S(1)} %get-tuple-element.65.zsrc_ref, f32[3,7,16,128]{3,2,1,0:T(8,128)S(1)} %get-tuple-element.66.inv_ref, f32[2,16,128]{2,1,0:T(8,128)S(1)} %get-tuple-element.90.state_ref, f32[16,128]{1,0:T(8,128)S(1)} %collective-permute-done.6.got_ref, ...), custom_call_target="tpu_custom_call" | custom-call | tf_op jit(solution)/shard_map/pallas_call | solution.py:26
  (7 shorter events, 0.1 us)
Async XLA Ops:
  2.1 21.5 %collective-permute-start.1 = (f32[8,128,128]{2,1,0:T(8,128)S(1)}, f32[8,128,128]{2,1,0:T(8,128)}, u32[]{:S(2)}, u32[]{:S(2)}) collective-permute-start(f32[8,128,128]{2,1,0:T(8,128)S(1)} %get-tuple-element.68), channel_id=1, source_target_pairs={{0,1},{1,2},{4,5},{5,6},{8,9},{9,10},{12,13},{13,14},{16,17},{17,1... | collective-permute-start | bytes 1572872 | tf_op jit(solution)/shard_map/ppermute | solution.py:643
  6.8 18.1 %collective-permute-start.4 = (f32[8,128,128]{2,1,0:T(8,128)S(1)}, f32[8,128,128]{2,1,0:T(8,128)}, u32[]{:S(2)}, u32[]{:S(2)}) collective-permute-start(f32[8,128,128]{2,1,0:T(8,128)S(1)} %get-tuple-element.68), channel_id=1, source_target_pairs={{3,2},{7,6},{11,10},{15,14},{19,18},{23,22},{27,26},{31,30}} | collective-permute-start | bytes 1572872 | tf_op jit(solution)/shard_map/ppermute | solution.py:642
  8.3 10.0 %all-to-all-start = ((f32[8,16,384]{2,1,0:T(8,128)}), f32[8,16,384]{2,1,0:T(8,128)S(1)}, u32[]{:S(2)}, u32[]{:S(2)}) async-start(f32[8,16,384]{2,1,0:T(8,128)} %bitcast.1), calls=%async_computation | async-start | bytes 393216 | tf_op jit(solution)/shard_map/all_to_all | solution.py:652
  21.0 3.3 %collective-permute-start = (f32[16,128]{1,0:T(8,128)S(1)}, f32[16,128]{1,0:T(8,128)S(1)}, u32[]{:S(2)}, u32[]{:S(2)}) collective-permute-start(f32[16,128]{1,0:T(8,128)S(1)} %get-tuple-element.67), channel_id=1, source_target_pairs={{0,1},{4,5},{8,9},{12,13},{16,17},{20,21},{24,25},{28,29}} | collective-permute-start | bytes 24584 | tf_op jit(solution)/shard_map/ppermute | solution.py:700
  22.9 2.2 %collective-permute-start.3 = (f32[2,16,128]{2,1,0:T(8,128)S(1)}, f32[2,16,128]{2,1,0:T(8,128)S(1)}, u32[]{:S(2)}, u32[]{:S(2)}) collective-permute-start(f32[2,16,128]{2,1,0:T(8,128)S(1)} %get-tuple-element.70.load_ref.refs_4_), channel_id=1, source_target_pairs={{3,2},{7,6},{11,10},{15,14},{19,18},{23,22},{27,26},{31,30}} | collective-permute-start | bytes 49160 | tf_op jit(solution)/shard_map/ppermute | solution.py:710
  24.2 0.9 %collective-permute-start.2 = (f32[16,128]{1,0:T(8,128)S(1)}, f32[16,128]{1,0:T(8,128)S(1)}, u32[]{:S(2)}, u32[]{:S(2)}) collective-permute-start(f32[16,128]{1,0:T(8,128)S(1)} %get-tuple-element.74), channel_id=1, source_target_pairs={{1,2},{5,6},{9,10},{13,14},{17,18},{21,22},{25,26},{29,30}} | collective-permute-start | bytes 24584 | tf_op jit(solution)/shard_map/ppermute | solution.py:726
  25.2 5.1 %collective-permute-start.5 = (f32[16,128]{1,0:T(8,128)S(1)}, f32[16,128]{1,0:T(8,128)S(1)}, u32[]{:S(2)}, u32[]{:S(2)}) collective-permute-start(f32[16,128]{1,0:T(8,128)S(1)} %get-tuple-element.82), channel_id=1, source_target_pairs={{2,1},{6,5},{10,9},{14,13},{18,17},{22,21},{26,25},{30,29}} | collective-permute-start | bytes 24584 | tf_op jit(solution)/shard_map/ppermute | solution.py:760
  25.9 5.8 %collective-permute-start.7 = (f32[2,16,128]{2,1,0:T(8,128)S(1)}, f32[2,16,128]{2,1,0:T(8,128)S(1)}, u32[]{:S(2)}, u32[]{:S(2)}) collective-permute-start(f32[2,16,128]{2,1,0:T(8,128)S(1)} %get-tuple-element.92), channel_id=1, source_target_pairs={{2,3},{6,7},{10,11},{14,15},{18,19},{22,23},{26,27},{30,31}} | collective-permute-start | bytes 49160 | tf_op jit(solution)/shard_map/ppermute | solution.py:768
  30.3 9.7 %collective-permute-start.6 = (f32[16,128]{1,0:T(8,128)S(1)}, f32[16,128]{1,0:T(8,128)S(1)}, u32[]{:S(2)}, u32[]{:S(2)}) collective-permute-start(f32[16,128]{1,0:T(8,128)S(1)} %get-tuple-element.91), channel_id=1, source_target_pairs={{1,0},{5,4},{9,8},{13,12},{17,16},{21,20},{25,24},{29,28}} | collective-permute-start | bytes 24584 | tf_op jit(solution)/shard_map/ppermute | solution.py:760

commit v3 on v2

v3 whole, which is shorter than its diff:
```python
import functools
import math

import jax
import jax.numpy as jnp
import numpy as np
from jax import lax
from jax.experimental import pallas as pl
from jax.experimental.pallas import tpu as pltpu
from jax.sharding import PartitionSpec as P

F32 = jnp.float32
BF16 = jnp.bfloat16
VMEM = pl.BlockSpec(memory_space=pltpu.VMEM)
SMEM = pl.BlockSpec(memory_space=pltpu.SMEM)
HBM = pl.BlockSpec(memory_space=pltpu.HBM)
ANY = pl.BlockSpec(memory_space=pl.ANY)
NN = (((1,), (0,)), ((), ()))
NT = (((1,), (1,)), ((), ()))


def call(kernel, outs, args, smem=0, anywhere=0, free=0, outside=0, scratch=(), aliases=None):
    inside = len(args) - smem - anywhere - free
    spaces = [None] * free + [pltpu.HBM] * anywhere + [pltpu.VMEM] * inside + [pltpu.SMEM] * smem
    args = [arg if space is None else pltpu.with_memory_space_constraint(arg, space) for arg, space in zip(args, spaces)]
    return pl.pallas_call(
        kernel,
        out_shape=outs,
        in_specs=[ANY] * free + [HBM] * anywhere + [VMEM] * inside + [SMEM] * smem,
        out_specs=[HBM if getattr(out, "memory_space", None) is pltpu.HBM else VMEM for out in outs[: len(outs) - outside]]
        + [SMEM] * outside,
        scratch_shapes=scratch,
        input_output_aliases=aliases or {},
        compiler_params=pltpu.CompilerParams(vmem_limit_bytes=16 * 2**20),
    )(*args)


def split(x):
    high = x.astype(BF16)
    return high, (x - high.astype(F32)).astype(BF16)


def dot(a, b, dims=NN):
    return lax.dot_general(a, b, dims, preferred_element_type=F32)


def wide(x):
    return jnp.concatenate(split(x), axis=1)


def tall(x):
    return jnp.concatenate(split(x), axis=0)


def product(left, right):
    size = right.shape[1] // 2
    out = dot(wide(left), jnp.concatenate([right, right], axis=0))
    return out[:, :size] + out[:, size:]


def by_mode(x, modes):
    mode_of = lax.broadcasted_iota(jnp.int32, x.shape, 0) // 2
    spread = jnp.concatenate([jnp.where(mode_of == k, x, 0.0) for k in range(modes)], axis=1)
    return tall(spread)


def folded(out, rows):
    size = out.shape[1] // 2
    return out[:rows, :size] + out[:rows, size:] + out[rows:, :size]


def apply(x, weight, modes):
    return folded(dot(by_mode(x, modes), weight), x.shape[0])


def wave(mode_total, shape, modes, axis=0):
    first = lax.axis_index("mode") * modes
    index = first + lax.broadcasted_iota(jnp.int32, shape, axis) // 2
    number = index.astype(F32) / mode_total
    return 4.0 * number * number


def wave_of(k, mode_total, modes):
    number = (jnp.full((1, 1), lax.axis_index("mode") * modes + k, jnp.int32)).astype(F32) / mode_total
    return 4.0 * number * number


class Weights:
    def __init__(self, size, *entries):
        self.size, self.rows = size, {}
        self.total = 0
        for name, count, rows in entries:
            self.rows[name] = (self.total, rows)
            self.total += count * rows

    def at(self, name, index, mode=None):
        start, rows = self.rows[name]
        if mode is None:
            return pl.ds(start + index * rows, rows)
        return pl.ds(start + index * rows + mode * self.size, self.size)

    def pair(self, ref, name, index):
        return jnp.concatenate([ref[self.at(name, index)], ref[self.at(name, index + 1)]], axis=1)

    def band(self, ref, slab):
        return self.pair(ref, "band", 2 * (slab - 1))

    def face(self, ref, slab, side):
        return self.pair(ref, "face", 4 * slab + 2 * side)


def band_wide(stiff, mass):
    return wide(jnp.concatenate([stiff, mass], axis=1))


def whole(weight):
    size = weight.shape[1] // 2
    value = weight.astype(F32)
    return value[:, :size] + value[:, size:]


def start_copies(pairs, sems):
    copies = [pltpu.make_async_copy(src, dst, sems.at[i]) for i, (src, dst) in enumerate(pairs)]
    for copy in copies:
        copy.start()
    return copies


def transform(rhs_ref, table_ref, out_ref, rhs_buf, table_buf, sems):
    for copy in start_copies([(rhs_ref, rhs_buf), (table_ref, table_buf)], sems):
        copy.wait()
    high, low = split(rhs_buf[...])
    rhs_buf[...] = dot(table_buf[...], jnp.concatenate([high, high, low], axis=0))
    for copy in start_copies([(rhs_buf, out_ref)], sems):
        copy.wait()


def copy_panels(panels_ref, ship_buf, ship_ref, sems, meanwhile):
    fetch = start_copies([(panels_ref.at[:, panels_ref.shape[1] - 1], ship_buf)], sems.at[pl.ds(2, 1)])
    meanwhile()
    fetch[0].wait()
    for copy in start_copies([(ship_buf, ship_ref)], sems.at[pl.ds(2, 1)]):
        copy.wait()


def ends_kernel(
    modes, mode_total, panels_ref, band_ref, rhs_ref, table_ref, ship_ref, out_ref,
    panels_buf, band_buf, ship_buf, rhs_buf, table_buf, sems,
):
    slabs, size = panels_ref.shape[1:3]
    elem, last = lax.axis_index("elem"), lax.axis_size("elem") - 1

    @pl.when(elem == 0)
    def _():
        copy_panels(panels_ref, ship_buf, ship_ref, sems, lambda: transform(rhs_ref, table_ref, out_ref, rhs_buf, table_buf, sems))

    @pl.when(elem == last)
    def _():
        copies = start_copies(
            [(band_ref, band_buf)] + [(panels_ref.at[:, j], panels_buf.at[j]) for j in range(slabs)],
            sems.at[pl.ds(2, slabs + 1)],
        )
        transform(rhs_ref, table_ref, out_ref, rhs_buf, table_buf, sems)
        copies[0].wait()
        band_t = [(band_buf[0, j].T, band_buf[1, j].T) for j in range(slabs)]
        lam = [wave_of(k, mode_total, modes) for k in range(modes)]
        forward = []
        for j in range(slabs):
            copies[1 + j].wait()
            steps = [
                product(panels_buf[j, k], wide(band_buf[0, j] + lam[k] * band_buf[1, j])) for k in range(modes)
            ]
            if j == 0:
                forward.append([-step for step in steps])
            else:
                forward.append([-product(steps[k], wide(forward[-1][k])) for k in range(modes)])
        current = forward[-1]
        for j in range(slabs - 2, -1, -1):
            steps = [
                product(panels_buf[j, k], wide(band_t[j + 1][0] + lam[k] * band_t[j + 1][1])) for k in range(modes)
            ]
            current = [forward[j][k] - product(steps[k], wide(current[k])) for k in range(modes)]
        for k in range(modes):
            ship_buf[k] = product(band_t[0][0] + lam[k] * band_t[0][1], wide(current[k]))
        for copy in start_copies([(ship_buf, ship_ref)], sems):
            copy.wait()


def between_kernel(hub, panels_ref, rhs_ref, table_ref, old_ref, ship_ref, out_ref, ship_buf, rhs_buf, table_buf, sems):
    elem = lax.axis_index("elem")

    @pl.when((elem > 0) & (elem < hub))
    def _():
        copy_panels(panels_ref, ship_buf, ship_ref, sems, lambda: transform(rhs_ref, table_ref, out_ref, rhs_buf, table_buf, sems))


def late_kernel(hub, rhs_ref, table_ref, old_ref, out_ref, rhs_buf, table_buf, sems):
    @pl.when(lax.axis_index("elem") == hub)
    def _():
        transform(rhs_ref, table_ref, out_ref, rhs_buf, table_buf, sems)


def maps_kernel(
    modes, mode_total, hub, place, panels_ref, band_ref, radial_ref, stiff_ref, mass_ref, number_ref, reig_ref, axial_ref, aeig_ref,
    coup_ref, front_ref, back_ref, w_ref, reig_out, axial_out, weight_out, aeig_out,
    panels_buf, band_buf, radial_buf, stiff_buf, mass_buf, number_buf, axial_buf, coup_buf, front_buf, back_buf, sems,
):
    slabs, size = panels_ref.shape[1:3]
    inner = aeig_ref.shape[1]
    copies = start_copies(
        [(radial_ref, radial_buf), (stiff_ref, stiff_buf), (mass_ref, mass_buf), (number_ref, number_buf), (band_ref, band_buf)]
        + [(panels_ref.at[:, j], panels_buf.at[j]) for j in range(slabs)]
        + [(axial_ref, axial_buf), (coup_ref, coup_buf), (aeig_ref, aeig_out), (reig_ref, reig_out)],
        sems,
    )
    for copy in copies[:4]:
        copy.wait()
    for j in range(slabs):
        radial = wide(radial_buf[j])
        w_ref[place.at("radial", j)] = radial
        parts = [wide(product(ref[j].T, radial)) for ref in (stiff_buf, mass_buf)]
        for side in range(2):
            spot = lax.broadcasted_iota(jnp.int32, (size, size), 0)
            onehot = jnp.where(number_buf[j, side : side + 1] == spot, 1.0, 0.0).astype(BF16)
            for i in range(2):
                both = jnp.concatenate([p[:, i * size : (i + 1) * size] for p in parts], axis=1)
                w_ref[place.at("face", 4 * j + 2 * side + i)] = dot(onehot, both).astype(BF16)
    copies[4].wait()
    for j in range(1, slabs):
        bands = band_wide(band_buf[0, j], band_buf[1, j])
        for i in range(2):
            w_ref[place.at("band", 2 * (j - 1) + i)] = bands[:, 2 * i * size : 2 * (i + 1) * size]
    for j in range(slabs):
        copies[5 + j].wait()
        for k in range(modes):
            w_ref[place.at("panel", j, k)] = wide(panels_buf[j, k].T)
    for copy in copies[5 + slabs :]:
        copy.wait()
    for j in range(slabs):
        for b in range(inner):
            for a in range(inner):
                axial_out[j, a, b] = axial_buf[j, a, b]
            for side in range(2):
                weight = coup_buf[j, side, 0] * axial_buf[j, 0, b]
                for a in range(1, inner):
                    weight = weight + coup_buf[j, side, a] * axial_buf[j, a, b]
                weight_out[j, side, b] = weight

    @pl.when((lax.axis_index("elem") > 0) & (lax.axis_index("elem") <= hub))
    def _():
        lam = [wave_of(k, mode_total, modes) for k in range(modes)]
        current = None
        for j in range(slabs):
            first, second = band_buf[0, j].T, band_buf[1, j].T
            steps = [product(first + lam[k] * second, w_ref[place.at("panel", j, k)]) for k in range(modes)]
            if current is None:
                current = [-step for step in steps]
            else:
                current = [-product(current[k], wide(steps[k])) for k in range(modes)]
        for k in range(modes):
            front_buf[pl.ds(k * size, size)] = wide(current[k])
        start_copies([(front_buf, front_ref)], sems.at[pl.ds(1, 1)])

        @pl.when(lax.axis_index("elem") <= hub)
        def _():
            current = [-whole(w_ref[place.at("panel", slabs - 1, k)]) for k in range(modes)]
            for j in range(slabs - 2, -1, -1):
                steps = [
                    product(band_buf[0, j + 1] + lam[k] * band_buf[1, j + 1], w_ref[place.at("panel", j, k)]) for k in range(modes)
                ]
                current = [-product(current[k], wide(steps[k])) for k in range(modes)]
            for k in range(modes):
                back_buf[pl.ds(k * size, size)] = wide(product(current[k], wide(band_buf[0, 0] + lam[k] * band_buf[1, 0])))
            for copy in start_copies([(back_buf, back_ref)], sems):
                copy.wait()

        pltpu.make_async_copy(front_buf, front_ref, sems.at[1]).wait()


def face_push(values, weight, lam):
    rows, size = values.shape
    high, low = split(values)
    blocks = [weight[:, i * size : (i + 1) * size] for i in range(4)]
    out = dot(
        jnp.concatenate([high, low], axis=0), jnp.concatenate(blocks, axis=0), NT
    )
    out = out[:rows, : 2 * size] + out[:rows, 2 * size :] + out[rows:, : 2 * size]
    return out[:, :size] + lam * out[:, size:]


def face_lift(values, weight, lam):
    rows, size = values.shape
    out = folded(dot(tall(values), weight), rows)
    return out[:, :size] + lam * out[:, size:]


def block_of(spec_ref, index, size):
    per = spec_ref.shape[2] // size
    at = index % per * size
    return spec_ref[index // per, :, at : at + size]


def band_step(values, weight, lam):
    return face_push(values, weight, lam)


def inner_kernel(modes, mode_total, place, hub, first_call, band_ref, front_ref, *refs):
    elem = lax.axis_index("elem")
    if first_call:
        spec_ref, w_ref, reig_ref, axial_ref, weight_ref, aeig_ref, zsrc_ref, inv_ref, reduced_ref, y_ref, send_ref = refs
    else:
        spec_ref, w_ref, reig_ref = refs[:3]
        axial_ref, weight_ref, aeig_ref, zsrc_ref, inv_ref, reduced_ref, y_ref, load_ref, front_out, band_buf, sems = refs[7:]
        inside = (elem > 0) & (elem <= hub)
        early = (front_ref, front_out)
        late = (band_ref.at[:, 0], band_buf)

        @pl.when(inside)
        def _():
            start_copies([early], sems.at[pl.ds(1, 1)])

        @pl.when(elem == lax.axis_size("elem") - 1)
        def _():
            start_copies([late], sems)

    @pl.when((elem == 0) == first_call)
    def _():
        load, values = inner_part(
            modes, mode_total, place, spec_ref, w_ref, reig_ref, axial_ref, weight_ref, aeig_ref, zsrc_ref, inv_ref, reduced_ref, y_ref
        )
        if first_call:
            send_ref[...] = values[-1]
            return
        load_ref[1] = load

        @pl.when(inside)
        def _():
            pltpu.make_async_copy(*early, sems.at[1]).wait()

        @pl.when(elem == lax.axis_size("elem") - 1)
        def _():
            lam = wave(mode_total, load.shape, modes)
            current = values[-1]
            for j in range(len(values) - 2, -1, -1):
                step = face_lift(current, place.band(w_ref, j + 1), lam)
                current = values[j] - apply(step, w_ref[place.at("panel", j)], modes)
            pltpu.make_async_copy(*late, sems.at[0]).wait()
            load_ref[0] = load + face_lift(current, band_wide(band_buf[0], band_buf[1]), lam)


def inner_part(
    modes, mode_total, place, spec_ref, w_ref, reig_ref, axial_ref, weight_ref, aeig_ref, zsrc_ref, inv_ref, solved_ref, y_ref
):
    slabs, inner, rows, size = zsrc_ref.shape
    lam = wave(mode_total, (rows, size), modes)
    pushed = []
    for j in range(slabs):
        source = jnp.concatenate(
            [block_of(spec_ref, j * (inner + 1) + a, size) for a in range(inner)], axis=0
        )
        first = product(source, w_ref[place.at("radial", j)])
        first = [first[a * rows : (a + 1) * rows] for a in range(inner)]
        sums = [None, None]
        for b in range(inner):
            value = first[0] * axial_ref[j, 0, b]
            for a in range(1, inner):
                value = value + first[a] * axial_ref[j, a, b]
            inverse = 1.0 / (aeig_ref[j, b] + reig_ref[j : j + 1] + lam)
            inv_ref[j, b] = inverse
            value = value * inverse
            zsrc_ref[j, b] = value
            for side in range(2):
                term = value * weight_ref[j, side, b]
                sums[side] = term if sums[side] is None else sums[side] + term
        pushed.append([face_push(sums[side], place.face(w_ref, j, side), lam) for side in range(2)])
    load = pushed[0][0]
    values = []
    for j in range(slabs):
        reduced = block_of(spec_ref, j * (inner + 1) + inner, size) - pushed[j][1]
        if j + 1 < slabs:
            reduced = reduced - pushed[j + 1][0]
        panel = w_ref[place.at("panel", j)]
        solved_ref[j] = reduced
        if j > 0:
            reduced = reduced - band_step(values[-1], place.band(w_ref, j), lam)
        values.append(apply(reduced, panel, modes))
        y_ref[j] = values[j]
    return load, values


def previous_weight(panel_ref, modes):
    parts = [split(panel_ref[k]) for k in range(modes)]
    return jnp.concatenate(
        [jnp.concatenate([p[i] for p in parts], axis=1) for i in range(2)], axis=0
    )


def apply_nt(x, weight, modes):
    return folded(dot(by_mode(x, modes), weight, NT), x.shape[0])


def backward_values(values, after, panel, behind_ref, modes):
    slabs = len(values)
    out = [None] * slabs
    out[-1] = values[-1]
    if after is not None:
        out[-1] = out[-1] - apply(after, panel, modes)
    for j in range(slabs - 2, -1, -1):
        out[j] = values[j] - apply(out[j + 1], behind_ref[j], modes)
    return out


def push_kernel(modes, first_ref, load_ref, prev_ref, push_ref, prev_buf, sems):
    @pl.when(lax.axis_index("elem") == 1)
    def _():
        for copy in start_copies([(first_ref, prev_buf)], sems):
            copy.wait()
        weight = previous_weight(prev_buf, modes)
        prev_ref[...] = weight
        push_ref[...] = apply_nt(load_ref[1], weight, modes)


def forward_kernel(modes, at, got_ref, push_ref, y_ref, front_ref, old_ref, state_ref, send_ref):
    @pl.when(lax.axis_index("elem") == at)
    def _():
        before = got_ref[...] - push_ref[...]
        state_ref[0] = before
        send_ref[...] = y_ref[y_ref.shape[0] - 1] + apply(before, front_ref[...], modes)


def base_kernel(
    modes, mode_total, hub, place, band_ref, map_ref, state_ref, load_ref, reduced_ref, y_ref, w_ref,
    base_ref, found_ref, back_ref, band_buf, sems,
):
    elem = lax.axis_index("elem")
    slabs, rows, size = reduced_ref.shape
    lam = wave(mode_total, (rows, size), modes)

    @pl.when((elem > 0) & (elem < hub))
    def _():
        copies = start_copies([(band_ref.at[:, 0], band_buf), (map_ref, back_ref)], sems)
        copies[0].wait()
        first = band_wide(band_buf[0], band_buf[1])
        bands = [first] + [place.band(w_ref, j) for j in range(1, slabs)]
        panels = [w_ref[place.at("panel", j)] for j in range(slabs)]
        values = []
        for j in range(slabs):
            step = face_push(values[-1] if j > 0 else state_ref[0], bands[j], lam)
            values.append(apply(reduced_ref[j] - step, panels[j], modes))
        found = values[-1]
        found_ref[slabs - 1] = found
        for j in range(slabs - 2, -1, -1):
            found = values[j] - apply(face_lift(found, bands[j + 1], lam), panels[j], modes)
            found_ref[j] = found
        base_ref[...] = load_ref[1] + face_lift(found, first, lam)
        copies[1].wait()


def ahead_maps(ahead_ref, band_buf, waves, w_ref, place):
    slabs, many, _ = ahead_ref.shape
    for j in range(slabs):
        first, second = band_buf[0, j].T, band_buf[1, j].T
        for k, lam in enumerate(waves):
            ahead_ref[j, pl.ds(k * place.size, place.size)] = wide(product(first + lam * second, w_ref[place.at("panel", j, k)]))


def behind_maps(behind_ref, band_buf, waves, w_ref, place):
    for j in range(behind_ref.shape[0]):
        for k, lam in enumerate(waves):
            step = product(band_buf[0, j + 1] + lam * band_buf[1, j + 1], w_ref[place.at("panel", j, k)])
            behind_ref[j, pl.ds(k * place.size, place.size)] = wide(step)


def hub_map_kernel(
    modes, mode_total, hub, place, map_ref, pprev_ref, band_ref, given_ref, load_ref, y_ref, w_ref, front_ref, old_prev_ref, old_push_ref,
    prev_ref, push_ref, ahead_ref, behind_ref, back_ref, base_ref, cross_ref, far_ref, band_buf, map_buf, prev_buf, sems,
):
    slabs, rows, size = y_ref.shape
    lam = wave(mode_total, (rows, size), modes)
    inside = (lax.axis_index("elem") > 1) & (lax.axis_index("elem") <= hub)

    @pl.when(inside)
    def _():
        start_copies([(pprev_ref, prev_buf)], sems.at[pl.ds(2, 1)])

    @pl.when(lax.axis_index("elem") == hub)
    def _():
        copies = start_copies([(band_ref, band_buf), (map_ref, map_buf)], sems)
        given = start_copies([(given_ref, back_ref)], sems.at[pl.ds(3, 1)])[0]
        waves = [wave_of(k, mode_total, modes) for k in range(modes)]

        def part(k):
            return pl.ds(k * size, size)

        copies[0].wait()
        ahead_maps(ahead_ref, band_buf, waves, w_ref, place)
        behind_maps(behind_ref, band_buf, waves, w_ref, place)
        entry = [wide(band_buf[0, 0] + waves[k] * band_buf[1, 0]) for k in range(modes)]
        forward = [[-whole(ahead_ref[0, part(k)]) for k in range(modes)]]
        for j in range(1, slabs - 1):
            forward.append([-product(forward[-1][k], ahead_ref[j, part(k)]) for k in range(modes)])
        cross = [whole(front_ref[part(k)]) for k in range(modes)]
        for j in range(slabs - 2, -1, -1):
            cross = [forward[j][k] - product(cross[k], behind_ref[j, part(k)]) for k in range(modes)]
        for k in range(modes):
            cross_ref[part(k)] = wide(product(cross[k], entry[k]))
        found = backward_values([y_ref[j] for j in range(slabs)], None, None, behind_ref, modes)
        base_ref[...] = load_ref[1] + face_lift(found[0], band_wide(band_buf[0, 0], band_buf[1, 0]), lam)
        copies[1].wait()
        far_ref[...] = previous_weight(map_buf, modes)
        given.wait()

    @pl.when(inside)
    def _():
        pltpu.make_async_copy(pprev_ref, prev_buf, sems.at[2]).wait()
        weight = previous_weight(prev_buf, modes)
        prev_ref[...] = weight
        push_ref[...] = apply_nt(load_ref[1], weight, modes)


def hub_kernel(
    modes, at, place, got_ref, push_ref, far_ref, far_weight_ref, y_ref, front_ref, back_ref, cross_ref, base_ref, w_ref, old_ref,
    state_ref, send_ref, last_ref,
):
    slabs = y_ref.shape[0]

    @pl.when(lax.axis_index("elem") == at)
    def _():
        panel = w_ref[place.at("panel", slabs - 1)]
        load = apply(far_ref[1], panel, modes)
        before = got_ref[...] - push_ref[...]
        state_ref[0] = before
        value = y_ref[slabs - 1] + apply(before, front_ref[...], modes)
        out = base_ref[...] + apply(before, cross_ref[...], modes)
        final = value - load
        after = far_ref[0] + apply_nt(final, far_weight_ref[...], modes)
        state_ref[1] = after
        send_ref[...] = out + apply(after, back_ref[...], modes)
        last_ref[0] = final
        last_ref[1] = value - apply(after, panel, modes)


def own_map_kernel(
    modes, mode_total, hub, place, band_ref, radial_ref, state_ref, reduced_ref, y_ref, w_ref, prev_ref, ahead_ref, behind_ref, old_ref,
    found_ref, own_ref, before_ref, radt_ref, ahead_buf, behind_buf, band_buf, radial_buf, sems,
):
    slabs, rows, size = reduced_ref.shape
    elem, last = lax.axis_index("elem"), lax.axis_size("elem") - 1
    lam = wave(mode_total, (rows, size), modes)
    waves = [wave_of(k, mode_total, modes) for k in range(modes)]
    copies = start_copies([(band_ref, band_buf), (radial_ref, radial_buf)], sems)

    def part(k):
        return pl.ds(k * size, size)

    copies[0].wait()

    @pl.when(elem == hub)
    def _():
        panels = [w_ref[place.at("panel", j)] for j in range(slabs)]
        before, values = state_ref[0], []
        for j in range(slabs):
            solved = apply(reduced_ref[j], panels[j], modes)
            values.append(solved - apply(values[-1] if j > 0 else before, ahead_ref[j], modes))
        found = backward_values(values, state_ref[1], panels[-1], behind_ref, modes)
        for j in range(slabs):
            found_ref[j] = found[j]
        back = face_lift(found[0], band_wide(band_buf[0, 0], band_buf[1, 0]), lam)
        before_ref[...] = before - apply_nt(back, prev_ref[...], modes)

    @pl.when(elem != hub)
    def _():
        behind_maps(behind_buf, band_buf, waves, w_ref, place)

    @pl.when(elem < hub)
    def _():
        current = [-whole(w_ref[place.at("panel", slabs - 1, k)]) for k in range(modes)]
        for k in range(modes):
            own_ref[slabs - 1, part(k)] = -w_ref[place.at("panel", slabs - 1, k)]
        for j in range(slabs - 2, -1, -1):
            current = [-product(current[k], behind_buf[j, part(k)]) for k in range(modes)]
            for k in range(modes):
                own_ref[j, part(k)] = wide(current[k])

    @pl.when(elem == last)
    def _():
        ahead_maps(ahead_buf, band_buf, waves, w_ref, place)
        forward = [[-whole(ahead_buf[0, part(k)]) for k in range(modes)]]
        for j in range(1, slabs):
            forward.append([-product(forward[-1][k], ahead_buf[j, part(k)]) for k in range(modes)])
        current = forward[-1]
        for k in range(modes):
            own_ref[slabs - 1, part(k)] = wide(current[k])
        for j in range(slabs - 2, -1, -1):
            current = [forward[j][k] - product(current[k], behind_buf[j, part(k)]) for k in range(modes)]
            for k in range(modes):
                own_ref[j, part(k)] = wide(current[k])

    @pl.when((elem == 0) | (elem == last))
    def _():
        found = backward_values([y_ref[j] for j in range(slabs)], None, None, behind_buf, modes)
        for j in range(slabs):
            found_ref[j] = found[j]

    copies[1].wait()
    for j in range(slabs):
        radt_ref[j] = wide(radial_buf[j].T)


def backward_kernel(modes, at, got_ref, base_ref, back_ref, old_ref, state_ref, send_ref):
    @pl.when(lax.axis_index("elem") == at)
    def _():
        after = got_ref[...]
        state_ref[1] = after
        send_ref[...] = base_ref[...] + apply(after, back_ref[...], modes)


def final_kernel(
    modes, mode_total, hub, place, zsrc_ref, inv_ref, state_ref, got_ref, base_ref, last_ref, load_ref, found_ref, own_ref, back_ref, before_ref, prev_ref, w_ref, radt_ref, axial_ref, weight_ref,
    out_ref, x_ref, out_buf, sems,
):
    slabs, inner, rows, size = zsrc_ref.shape
    lam = wave(mode_total, (rows, size), modes)
    elem, last = lax.axis_index("elem"), lax.axis_size("elem") - 1

    def values(given):
        for j in range(slabs):
            x_ref[j + 1] = found_ref[j] + apply(given, own_ref[j], modes)

    @pl.when(elem == 0)
    def _():
        x_ref[0] = jnp.zeros((rows, size), F32)
        values(got_ref[...])

    @pl.when((elem > 0) & (elem < hub))
    def _():
        after = state_ref[1]
        values(after)
        back = base_ref[...] - load_ref[1] + apply(after, back_ref[...], modes)
        x_ref[0] = state_ref[0] - apply_nt(back, prev_ref[...], modes)

    @pl.when(elem == hub)
    def _():
        for j in range(slabs):
            x_ref[j + 1] = found_ref[j]
        x_ref[0] = before_ref[...]

    @pl.when(elem == last)
    def _():
        values(last_ref[0])
        x_ref[0] = last_ref[1]

    copies = []
    for j in range(slabs):
        lifted = [face_lift(x_ref[j + side], place.face(w_ref, j, side), lam) for side in range(2)]
        kept = []
        for b in range(inner):
            total = lifted[0] * weight_ref[j, 0, b] + lifted[1] * weight_ref[j, 1, b]
            kept.append(zsrc_ref[j, b] - total * inv_ref[j, b])
        values = []
        for a in range(inner):
            value = kept[0] * axial_ref[j, a, 0]
            for b in range(1, inner):
                value = value + kept[b] * axial_ref[j, a, b]
            values.append(value)
        result = product(jnp.concatenate(values, axis=0), radt_ref[j])
        for a in range(inner):
            out_buf[j, :, a * size : (a + 1) * size] = result[a * rows : (a + 1) * rows]
        out_buf[j, :, inner * size :] = x_ref[j + 1]
        width = (inner + 1) * size
        copies += start_copies([(out_buf.at[j], out_ref.at[:, pl.ds(j * width, width)])], sems.at[pl.ds(j, 1)])
    for copy in copies:
        copy.wait()


def dft_table(planes):
    row, col = np.arange(planes)[:, None], np.arange(planes)[None]
    angle = row // 2 * col % planes * (2.0 * math.pi / planes)
    table = np.where(row % 2 == 0, np.cos(angle), -np.sin(angle)) / math.sqrt(planes)
    table = jnp.asarray(table, F32)
    high, low = split(table)
    return jnp.concatenate([high, low, high], axis=1)


def body(
    rhs_phys, radial_basis, axial_basis, radial_eig, axial_eig, face_stiff, face_mass, axial_coupling, face_numbering,
    band_panels, inverse_panels,
):
    planes, nodes = rhs_phys.shape
    modes, slabs, size, _ = inverse_panels.shape
    inner = axial_basis.shape[1]
    devices = lax.axis_size("mode")
    elems = lax.axis_size("elem")
    mode_total = modes * devices
    rows = 2 * modes
    hub = elems - 2
    last = elems - 1

    def shape(*dims):
        return jax.ShapeDtypeStruct(dims, F32)

    def kept(*dims):
        return pltpu.VMEM(dims, F32)

    def half(*dims):
        return pltpu.VMEM(dims, BF16)

    table = dft_table(planes)
    many = modes * size
    place = Weights(size, ("panel", slabs, many), ("radial", slabs, size), ("face", 4 * slabs, size), ("band", 2 * (slabs - 1), size))
    buffers = [pltpu.VMEM((planes, nodes), F32), pltpu.VMEM(table.shape, BF16), pltpu.SemaphoreType.DMA((slabs + 3,))]
    whole_spectrum = pltpu.HBM((planes, nodes), F32)
    whole_panels = pltpu.HBM((modes, size, size), F32)
    panels_buffer = pltpu.VMEM((modes, size, size), F32)
    ship, spectrum = call(
        functools.partial(ends_kernel, modes, mode_total),
        [whole_panels, whole_spectrum],
        [inverse_panels, band_panels, rhs_phys, table],
        anywhere=4,
        scratch=[pltpu.VMEM((slabs, modes, size, size), F32), pltpu.VMEM(band_panels.shape, F32), panels_buffer] + buffers,
    )
    if hub > 1:
        first = far_map = lax.ppermute(ship, "elem", [(0, 1), (last, hub)])
    else:
        first, far_map = lax.ppermute(ship, "elem", [(0, 1)]), lax.ppermute(ship, "elem", [(last, hub)])
    ship, spectrum = call(
        functools.partial(between_kernel, hub),
        [whole_panels, whole_spectrum],
        [inverse_panels, rhs_phys, table, spectrum],
        anywhere=4,
        scratch=[panels_buffer] + buffers,
        aliases={3: 1},
    )
    pprev = lax.ppermute(ship, "elem", [(i, i + 1) for i in range(1, hub)]) if hub > 1 else first
    spectrum = call(
        functools.partial(late_kernel, hub),
        [whole_spectrum],
        [rhs_phys, table, spectrum],
        anywhere=3,
        scratch=buffers,
        aliases={2: 0},
    )[0]
    spectrum = lax.all_to_all(spectrum.reshape(devices, rows, nodes), "mode", 0, 0, tiled=False)
    if nodes % size:
        spectrum = jnp.swapaxes(spectrum, 0, 1).reshape(1, rows, devices * nodes)
    vector = (rows, size)
    matrix = half(many, 2 * size)
    front, back_map, w, reig, axial, weight, aeig = call(
        functools.partial(maps_kernel, modes, mode_total, hub, place),
        [
            pltpu.HBM((many, 2 * size), BF16),
            pltpu.HBM((many, 2 * size), BF16),
            half(place.total, 2 * size),
            kept(*radial_eig.shape),
            pltpu.SMEM(axial_basis.shape, F32),
            pltpu.SMEM((slabs, 2, inner), F32),
            pltpu.SMEM(axial_eig.shape, F32),
        ],
        [
            inverse_panels, band_panels, radial_basis, face_stiff, face_mass, face_numbering,
            radial_eig, axial_basis, axial_eig, axial_coupling,
        ],
        anywhere=10,
        outside=3,
        scratch=[
            pltpu.VMEM((slabs, modes, size, size), F32),
            pltpu.VMEM(band_panels.shape, F32),
            pltpu.VMEM(radial_basis.shape, F32),
            pltpu.VMEM(face_stiff.shape, F32),
            pltpu.VMEM(face_mass.shape, F32),
            pltpu.VMEM(face_numbering.shape, jnp.int32),
            pltpu.SMEM(axial_basis.shape, F32),
            pltpu.SMEM(axial_coupling.shape, F32),
            pltpu.VMEM((many, 2 * size), BF16),
            pltpu.VMEM((many, 2 * size), BF16),
            pltpu.SemaphoreType.DMA((slabs + 9,)),
        ],
    )
    solves = [kept(slabs, inner, *vector), kept(slabs, inner, *vector), kept(slabs, *vector), kept(slabs, *vector)]
    *solve, send = call(
        functools.partial(inner_kernel, modes, mode_total, place, hub, True),
        solves + [kept(*vector)],
        [band_panels, front, spectrum, w, reig, axial, weight, aeig],
        anywhere=2,
        smem=3,
    )
    got = lax.ppermute(send, "elem", [(0, 1)])
    zsrc, inv, reduced, y, load, front = call(
        functools.partial(inner_kernel, modes, mode_total, place, hub, False),
        solves + [kept(2, *vector), matrix],
        [band_panels, front, spectrum, w, reig, *solve, axial, weight, aeig],
        anywhere=2,
        smem=3,
        scratch=[
            pltpu.VMEM((2, size, size), F32),
            pltpu.SemaphoreType.DMA((2,)),
        ],
        aliases={5 + i: i for i in range(4)},
    )
    far = lax.ppermute(load, "elem", [(last, hub)])
    prev, push = call(
        functools.partial(push_kernel, modes),
        [half(2 * size, many), kept(*vector)],
        [first, load],
        free=1,
        scratch=[panels_buffer, pltpu.SemaphoreType.DMA((1,))],
    )
    prev, later_push, ahead, behind, hub_back, hub_base, cross, far_weight = call(
        functools.partial(hub_map_kernel, modes, mode_total, hub, place),
        [
            half(2 * size, many), kept(*vector), half(slabs, many, 2 * size), half(slabs - 1, many, 2 * size), matrix,
            kept(*vector), matrix, half(2 * size, many),
        ],
        [far_map, pprev, band_panels, back_map, load, y, w, front, prev, push],
        free=2,
        anywhere=2,
        scratch=[pltpu.VMEM(band_panels.shape, F32), panels_buffer, panels_buffer, pltpu.SemaphoreType.DMA((4,))],
        aliases={8: 0, 9: 1},
    )
    state = jnp.zeros((2, *vector), F32)
    for at in range(1, hub):
        state, send = call(
            functools.partial(forward_kernel, modes, at),
            [kept(*state.shape), shape(*vector)],
            [got, push if at == 1 else later_push, y, front, state],
            aliases={4: 0},
        )
        got = lax.ppermute(send, "elem", [(at, at + 1)])
    state, send, final = call(
        functools.partial(hub_kernel, modes, hub, place),
        [kept(*state.shape), shape(*vector), shape(2, *vector)],
        [got, push if hub == 1 else later_push, far, far_weight, y, front, hub_back, cross, hub_base, w, state],
        aliases={10: 0},
    )
    base, found, back = call(
        functools.partial(base_kernel, modes, mode_total, hub, place),
        [kept(*vector), kept(slabs, *vector), matrix],
        [band_panels, back_map, state, load, reduced, y, w],
        anywhere=2,
        scratch=[pltpu.VMEM((2, size, size), F32), pltpu.SemaphoreType.DMA((2,))],
    )
    for at in range(hub - 1, 0, -1):
        got = lax.ppermute(send, "elem", [(at + 1, at)])
        state, send = call(
            functools.partial(backward_kernel, modes, at),
            [kept(*state.shape), shape(*vector)],
            [got, base, back, state],
            aliases={3: 0},
        )
    got = lax.ppermute(send, "elem", [(1, 0)])
    found, own, before, radt = call(
        functools.partial(own_map_kernel, modes, mode_total, hub, place),
        [kept(slabs, *vector), half(slabs, many, 2 * size), kept(*vector), half(slabs, size, 2 * size)],
        [band_panels, radial_basis, state, reduced, y, w, prev, ahead, behind, found],
        anywhere=2,
        scratch=[
            pltpu.VMEM((slabs, many, 2 * size), BF16),
            pltpu.VMEM((slabs - 1, many, 2 * size), BF16),
            pltpu.VMEM(band_panels.shape, F32),
            pltpu.VMEM(radial_basis.shape, F32),
            pltpu.SemaphoreType.DMA((2,)),
        ],
        aliases={9: 0},
    )
    final = lax.ppermute(final, "elem", [(hub, last)])
    return call(
        functools.partial(final_kernel, modes, mode_total, hub, place),
        [pltpu.HBM((rows, slabs * (inner + 1) * size), F32)],
        [
            zsrc, inv, state, got, base, final, load, found, own, back, before, prev, w, radt, axial, weight,
        ],
        smem=2,
        scratch=[
            pltpu.VMEM((slabs + 1, *vector), F32),
            pltpu.VMEM((slabs, rows, (inner + 1) * size), F32),
            pltpu.SemaphoreType.DMA((slabs,)),
        ],
    )[0]


def solution(mesh):
    placed = (
        P(None, ("elem", "mode")),
        P("elem", None, None),
        P("elem", None, None),
        P("elem", None),
        P("elem", None),
        P("elem", None, None),
        P("elem", None, None),
        P("elem", None, None),
        P("elem", None, None),
        P(None, "elem", None, None),
        P("mode", "elem", None, None),
    )
    return jax.shard_map(
        body, mesh=mesh, in_specs=placed, out_specs=P("mode", "elem"), check_vma=False
    )
```

time: 42.2 us -> 40.2 us (0.953)
  starting transfers between devices: 15.8 us -> 14.3 us
  Pallas kernels: 13.9 us -> 12.5 us
  waiting for transfers between devices: 11.9 us -> 12.7 us
    ppermute x2 -> x3, waiting for transfers between devices: 0.01 us -> 9.09 us  [the longest x1 9.08 us: body(): got = lax.ppermute(send, 'elem', [(1, 0)])]
    ppermute x2 -> x1, waiting for transfers between devices: 8.36 us -> 0.01 us  [body(): got = lax.ppermute(send, 'elem', [(at + 1, at)])]
    pallas_call x12 -> x14, Pallas kernels: 13.9 us -> 12.5 us  [call(): pl.pallas_call(kernel, out_shape=outs, in_specs=[ANY] * free + [HBM] * an...]
    ppermute x2 -> x3, starting transfers between devices: 6.23 us -> 4.92 us  [the longest x1 2.16 us: body(): first = far_map = lax.ppermute(ship, 'elem', [(0, 1), (last, hub)])]
    ppermute x2 -> x1, starting transfers between devices: 1.95 us -> 0.66 us  [body(): got = lax.ppermute(send, 'elem', [(at + 1, at)])]
    all_to_all x1, starting transfers between devices: 3.74 us -> 4.34 us  [body(): lax.all_to_all(spectrum.reshape(devices, rows, nodes), 'mode', 0, 0, tile...]
    ppermute x1, starting transfers between devices: 1.9 us -> 2.42 us  [body(): got = lax.ppermute(send, 'elem', [(0, 1)])]
  transfers between devices with their start and end apart: 9 -> 9, of which waited for: 3 -> 3; matrix products, arithmetic and copies ran while one was open for 0% -> 0% of each run, Pallas kernels for 24% -> 20%
where the time goes in v3:
time: 40.2 us; the launch traced here: 39.8 us
  starting transfers between devices  14.3 us (36%)
  waiting for transfers between devices  12.7 us (32%)
  Pallas kernels  12.5 us (31%)
    pallas_call x14, Pallas kernels, call(): pl.pallas_call(kernel, out_shape=outs, in_specs=[ANY] * free + [HBM] * an...  12.5 us
    ppermute x1, waiting for transfers between devices, body(): got = lax.ppermute(send, 'elem', [(1, 0)])  9.08 us
    all_to_all x1, starting transfers between devices, body(): lax.all_to_all(spectrum.reshape(devices, rows, nodes), 'mode', 0, 0, tile...  4.34 us
    all_to_all x1, waiting for transfers between devices, body(): lax.all_to_all(spectrum.reshape(devices, rows, nodes), 'mode', 0, 0, tile...  3 us
    ppermute x1, starting transfers between devices, body(): got = lax.ppermute(send, 'elem', [(0, 1)])  2.42 us
    ppermute x1, starting transfers between devices, body(): first = far_map = lax.ppermute(ship, 'elem', [(0, 1), (last, hub)])  2.16 us
    ppermute x1, starting transfers between devices, body(): lax.ppermute(ship, 'elem', [(i, i + 1) for i in range(1, hub)])  1.47 us
    ppermute x1, starting transfers between devices, body(): got = lax.ppermute(send, 'elem', [(1, 0)])  1.29 us
  transfers between devices with their start and end apart: 9, of which 3 were waited for; matrix products, arithmetic and copies ran while one was open for 0% of the time, Pallas kernels for 20%

profile of v3, /device:TPU:0, one launch (start us, length us, event | category | flops | bytes accessed | tf_op | source)
XLA Modules:
  0.0 39.8 jit_solution(1230309115513857691)
XLA Ops:
  0.0 2.9 %shard_map.119 = (f32[8,128,128]{2,1,0:T(8,128)}, f32[128,384]{1,0:T(8,128)}) custom-call(f32[8,3,128,128]{3,2,1,0:T(8,128)} %panels_ref.5, f32[2,3,128,128]{3,2,1,0:T(8,128)} %band_ref.13, f32[128,384]{1,0:T(8,128)} %rhs_ref.5, bf16[128,384]{1,0:T(8,128)(2,1)} %constant.19.table_ref), custom_call_target="tpu_custom_call" | custom-call | tf_op jit(solution)/shard_map/pallas_call | solution.py:26
  2.9 2.2 %collective-permute-start.1 = (f32[8,128,128]{2,1,0:T(8,128)}, f32[8,128,128]{2,1,0:T(8,128)S(1)}, u32[]{:S(2)}, u32[]{:S(2)}) collective-permute-start(f32[8,128,128]{2,1,0:T(8,128)} %get-tuple-element.66), channel_id=1, source_target_pairs={{0,1},{3,2},{4,5},{7,6},{8,9},{11,10},{12,13},{15,14},{16,17},{19,... | collective-permute-start | bytes 1572872 | tf_op jit(solution)/shard_map/ppermute | solution.py:723
  5.0 0.1 shard_map.120
  5.1 1.5 %collective-permute-start.3 = (f32[8,128,128]{2,1,0:T(8,128)}, f32[8,128,128]{2,1,0:T(8,128)}, u32[]{:S(2)}, u32[]{:S(2)}) collective-permute-start(f32[8,128,128]{2,1,0:T(8,128)} %get-tuple-element.72), channel_id=1, source_target_pairs={{1,2},{5,6},{9,10},{13,14},{17,18},{21,22},{25,26},{29,30}} | collective-permute-start | bytes 1572872 | tf_op jit(solution)/shard_map/ppermute | solution.py:734
  6.6 0.1 shard_map.121
  6.6 4.3 %all-to-all-start = ((f32[8,16,384]{2,1,0:T(8,128)}), f32[8,16,384]{2,1,0:T(8,128)S(1)}, u32[]{:S(2)}, u32[]{:S(2)}) async-start(f32[8,16,384]{2,1,0:T(8,128)} %bitcast.1), calls=%async_computation | async-start | bytes 393216 | tf_op jit(solution)/shard_map/all_to_all | solution.py:743
  11.0 3.2 %shard_map.118 = (bf16[1024,256]{1,0:T(8,128)(2,1)}, bf16[1024,256]{1,0:T(8,128)(2,1)}, bf16[5504,256]{1,0:T(8,128)(2,1)S(1)}, f32[3,128]{1,0:T(4,128)S(1)}, f32...) custom-call(f32[8,3,128,128]{3,2,1,0:T(8,128)} %panels_ref.5, f32[2,3,128,128]{3,2,1,0:T(8,128)} %band_ref.13, ...), custom_call_target="tpu_custom_call" | custom-call | tf_op jit(solution)/shard_map/pallas_call | solution.py:26
  14.2 3.0 %all-to-all-done.refs_0_ = f32[8,16,384]{2,1,0:T(8,128)S(1)} async-done(((f32[8,16,384]{2,1,0:T(8,128)}), f32[8,16,384]{2,1,0:T(8,128)S(1)}, u32[]{:S(2)}, u32[]{:S(2)}) %all-to-all-start) | async-done | bytes 196640 | tf_op jit(solution)/shard_map/all_to_all | solution.py:743
  17.2 1.7 %shard_map.122 = (f32[3,7,16,128]{3,2,1,0:T(8,128)S(1)}, f32[3,7,16,128]{3,2,1,0:T(8,128)S(1)}, f32[3,16,128]{2,1,0:T(8,128)S(1)}, f32[3,16,128]{2,1,0:T(8,128)S(1)}, f32[16,128]{1,0:T(8,128)S(1)}) custom-call(f32[2,3,128,128]{3,2,1,0:T(8,128)} %band_ref.13, bf16[1024,256]{1,0:T(8,128)(2,1)} %get-tuple-element.51.front_ref, ...), custom_call_target="tpu_custom_call" | custom-call | tf_op jit(solution)/shard_map/pallas_call | solution.py:26
  18.9 2.4 %collective-permute-start = (f32[16,128]{1,0:T(8,128)S(1)}, f32[16,128]{1,0:T(8,128)S(1)}, u32[]{:S(2)}, u32[]{:S(2)}) collective-permute-start(f32[16,128]{1,0:T(8,128)S(1)} %get-tuple-element.65), channel_id=1, source_target_pairs={{0,1},{4,5},{8,9},{12,13},{16,17},{20,21},{24,25},{28,29}} | collective-permute-start | bytes 24584 | tf_op jit(solution)/shard_map/ppermute | solution.py:787
  21.4 0.7 %collective-permute-start.4 = (f32[2,16,128]{2,1,0:T(8,128)S(1)}, f32[2,16,128]{2,1,0:T(8,128)S(1)}, u32[]{:S(2)}, u32[]{:S(2)}) collective-permute-start(f32[2,16,128]{2,1,0:T(8,128)S(1)} %get-tuple-element.67.load_ref), channel_id=1, source_target_pairs={{3,2},{7,6},{11,10},{15,14},{19,18},{23,22},{27,26},{31,30}} | collective-permute-start | bytes 49160 | tf_op jit(solution)/shard_map/ppermute | solution.py:800
  22.0 0.0 collective-permute-done.1.first_ref.map_ref
  22.1 0.6 %collective-permute-done.got_ref = f32[16,128]{1,0:T(8,128)S(1)} collective-permute-done((f32[16,128]{1,0:T(8,128)S(1)}, f32[16,128]{1,0:T(8,128)S(1)}, u32[]{:S(2)}, u32[]{:S(2)}) %collective-permute-start) | collective-permute-done | bytes 8224 | tf_op jit(solution)/shard_map/ppermute | solution.py:787
  22.7 0.6 %collective-permute-start.2 = (f32[16,128]{1,0:T(8,128)S(1)}, f32[16,128]{1,0:T(8,128)S(1)}, u32[]{:S(2)}, u32[]{:S(2)}) collective-permute-start(f32[16,128]{1,0:T(8,128)S(1)} %get-tuple-element.71), channel_id=1, source_target_pairs={{1,2},{5,6},{9,10},{13,14},{17,18},{21,22},{25,26},{29,30}} | collective-permute-start | bytes 24584 | tf_op jit(solution)/shard_map/ppermute | solution.py:828
  23.3 0.0 collective-permute-done.3.pprev_ref
  23.3 0.1 shard_map.126
  23.4 0.0 collective-permute-done.4.far_ref
  23.4 0.2 shard_map.127
  23.6 0.7 %collective-permute-start.5 = (f32[16,128]{1,0:T(8,128)S(1)}, f32[16,128]{1,0:T(8,128)S(1)}, u32[]{:S(2)}, u32[]{:S(2)}) collective-permute-start(f32[16,128]{1,0:T(8,128)S(1)} %get-tuple-element.81), channel_id=1, source_target_pairs={{2,1},{6,5},{10,9},{14,13},{18,17},{22,21},{26,25},{30,29}} | collective-permute-start | bytes 24584 | tf_op jit(solution)/shard_map/ppermute | solution.py:843
  24.3 0.7 %collective-permute-start.7 = (f32[2,16,128]{2,1,0:T(8,128)S(1)}, f32[2,16,128]{2,1,0:T(8,128)S(1)}, u32[]{:S(2)}, u32[]{:S(2)}) collective-permute-start(f32[2,16,128]{2,1,0:T(8,128)S(1)} %get-tuple-element.88), channel_id=1, source_target_pairs={{2,3},{6,7},{10,11},{14,15},{18,19},{22,23},{26,27},{30,31}} | collective-permute-start | bytes 49160 | tf_op jit(solution)/shard_map/ppermute | solution.py:865
  25.0 1.3 %collective-permute-start.6 = (f32[16,128]{1,0:T(8,128)S(1)}, f32[16,128]{1,0:T(8,128)S(1)}, u32[]{:S(2)}, u32[]{:S(2)}) collective-permute-start(f32[16,128]{1,0:T(8,128)S(1)} %get-tuple-element.87), channel_id=1, source_target_pairs={{1,0},{5,4},{9,8},{13,12},{17,16},{21,20},{25,24},{29,28}} | collective-permute-start | bytes 24584 | tf_op jit(solution)/shard_map/ppermute | solution.py:850
  26.3 2.6 %shard_map.130 = (f32[3,16,128]{2,1,0:T(8,128)S(1)}, bf16[3,1024,256]{2,1,0:T(8,128)(2,1)S(1)}, f32[16,128]{1,0:T(8,128)S(1)}, bf16[3,128,256]{2,1,0:T(8,128)(2,1)S(1)}) custom-call(f32[2,3,128,128]{3,2,1,0:T(8,128)} %band_ref.13, f32[3,128,128]{2,1,0:T(8,128)} %radial_ref.3, ...), custom_call_target="tpu_custom_call", output_to_operand_aliasing={{0}: (9, {})} | custom-call | tf_op jit(solution)/shard_map/pallas_call | solution.py:26
  28.9 9.1 %collective-permute-done.6.got_ref = f32[16,128]{1,0:T(8,128)S(1)} collective-permute-done((f32[16,128]{1,0:T(8,128)S(1)}, f32[16,128]{1,0:T(8,128)S(1)}, u32[]{:S(2)}, u32[]{:S(2)}) %collective-permute-start.6) | collective-permute-done | bytes 8224 | tf_op jit(solution)/shard_map/ppermute | solution.py:850
  38.0 1.6 %shard_map.131 = f32[16,3072]{1,0:T(8,128)} custom-call(f32[3,7,16,128]{3,2,1,0:T(8,128)S(1)} %get-tuple-element.63.zsrc_ref, f32[3,7,16,128]{3,2,1,0:T(8,128)S(1)} %get-tuple-element.64.inv_ref, f32[2,16,128]{2,1,0:T(8,128)S(1)} %get-tuple-element.86.state_ref, f32[16,128]{1,0:T(8,128)S(1)} %collective-permute-done.6.got_ref, ...), custom_call_target="tpu_custom_call" | custom-call | tf_op jit(solution)/shard_map/pallas_call | solution.py:26
  (9 shorter events, 0.1 us)
Async XLA Ops:
  2.9 19.2 %collective-permute-start.1 = (f32[8,128,128]{2,1,0:T(8,128)}, f32[8,128,128]{2,1,0:T(8,128)S(1)}, u32[]{:S(2)}, u32[]{:S(2)}) collective-permute-start(f32[8,128,128]{2,1,0:T(8,128)} %get-tuple-element.66), channel_id=1, source_target_pairs={{0,1},{3,2},{4,5},{7,6},{8,9},{11,10},{12,13},{15,14},{16,17},{19,... | collective-permute-start | bytes 1572872 | tf_op jit(solution)/shard_map/ppermute | solution.py:723
  5.1 18.2 %collective-permute-start.3 = (f32[8,128,128]{2,1,0:T(8,128)}, f32[8,128,128]{2,1,0:T(8,128)}, u32[]{:S(2)}, u32[]{:S(2)}) collective-permute-start(f32[8,128,128]{2,1,0:T(8,128)} %get-tuple-element.72), channel_id=1, source_target_pairs={{1,2},{5,6},{9,10},{13,14},{17,18},{21,22},{25,26},{29,30}} | collective-permute-start | bytes 1572872 | tf_op jit(solution)/shard_map/ppermute | solution.py:734
  6.6 10.6 %all-to-all-start = ((f32[8,16,384]{2,1,0:T(8,128)}), f32[8,16,384]{2,1,0:T(8,128)S(1)}, u32[]{:S(2)}, u32[]{:S(2)}) async-start(f32[8,16,384]{2,1,0:T(8,128)} %bitcast.1), calls=%async_computation | async-start | bytes 393216 | tf_op jit(solution)/shard_map/all_to_all | solution.py:743
  18.9 3.8 %collective-permute-start = (f32[16,128]{1,0:T(8,128)S(1)}, f32[16,128]{1,0:T(8,128)S(1)}, u32[]{:S(2)}, u32[]{:S(2)}) collective-permute-start(f32[16,128]{1,0:T(8,128)S(1)} %get-tuple-element.65), channel_id=1, source_target_pairs={{0,1},{4,5},{8,9},{12,13},{16,17},{20,21},{24,25},{28,29}} | collective-permute-start | bytes 24584 | tf_op jit(solution)/shard_map/ppermute | solution.py:787
  21.4 2.0 %collective-permute-start.4 = (f32[2,16,128]{2,1,0:T(8,128)S(1)}, f32[2,16,128]{2,1,0:T(8,128)S(1)}, u32[]{:S(2)}, u32[]{:S(2)}) collective-permute-start(f32[2,16,128]{2,1,0:T(8,128)S(1)} %get-tuple-element.67.load_ref), channel_id=1, source_target_pairs={{3,2},{7,6},{11,10},{15,14},{19,18},{23,22},{27,26},{31,30}} | collective-permute-start | bytes 49160 | tf_op jit(solution)/shard_map/ppermute | solution.py:800
  22.7 0.7 %collective-permute-start.2 = (f32[16,128]{1,0:T(8,128)S(1)}, f32[16,128]{1,0:T(8,128)S(1)}, u32[]{:S(2)}, u32[]{:S(2)}) collective-permute-start(f32[16,128]{1,0:T(8,128)S(1)} %get-tuple-element.71), channel_id=1, source_target_pairs={{1,2},{5,6},{9,10},{13,14},{17,18},{21,22},{25,26},{29,30}} | collective-permute-start | bytes 24584 | tf_op jit(solution)/shard_map/ppermute | solution.py:828
  23.6 1.4 %collective-permute-start.5 = (f32[16,128]{1,0:T(8,128)S(1)}, f32[16,128]{1,0:T(8,128)S(1)}, u32[]{:S(2)}, u32[]{:S(2)}) collective-permute-start(f32[16,128]{1,0:T(8,128)S(1)} %get-tuple-element.81), channel_id=1, source_target_pairs={{2,1},{6,5},{10,9},{14,13},{18,17},{22,21},{26,25},{30,29}} | collective-permute-start | bytes 24584 | tf_op jit(solution)/shard_map/ppermute | solution.py:843
  24.3 13.7 %collective-permute-start.7 = (f32[2,16,128]{2,1,0:T(8,128)S(1)}, f32[2,16,128]{2,1,0:T(8,128)S(1)}, u32[]{:S(2)}, u32[]{:S(2)}) collective-permute-start(f32[2,16,128]{2,1,0:T(8,128)S(1)} %get-tuple-element.88), channel_id=1, source_target_pairs={{2,3},{6,7},{10,11},{14,15},{18,19},{22,23},{26,27},{30,31}} | collective-permute-start | bytes 49160 | tf_op jit(solution)/shard_map/ppermute | solution.py:865
  25.0 13.0 %collective-permute-start.6 = (f32[16,128]{1,0:T(8,128)S(1)}, f32[16,128]{1,0:T(8,128)S(1)}, u32[]{:S(2)}, u32[]{:S(2)}) collective-permute-start(f32[16,128]{1,0:T(8,128)S(1)} %get-tuple-element.87), channel_id=1, source_target_pairs={{1,0},{5,4},{9,8},{13,12},{17,16},{21,20},{25,24},{29,28}} | collective-permute-start | bytes 24584 | tf_op jit(solution)/shard_map/ppermute | solution.py:850

commit v4 on v3

--- a/solution.py
+++ b/solution.py
@@ -131,16 +131,16 @@
         copy.wait()
     high, low = split(rhs_buf[...])
     rhs_buf[...] = dot(table_buf[...], jnp.concatenate([high, high, low], axis=0))
-    for copy in start_copies([(rhs_buf, out_ref)], sems):
-        copy.wait()
-
-
-def copy_panels(panels_ref, ship_buf, ship_ref, sems, meanwhile):
-    fetch = start_copies([(panels_ref.at[:, panels_ref.shape[1] - 1], ship_buf)], sems.at[pl.ds(2, 1)])
-    meanwhile()
-    fetch[0].wait()
-    for copy in start_copies([(ship_buf, ship_ref)], sems.at[pl.ds(2, 1)]):
-        copy.wait()
+    return start_copies([(rhs_buf, out_ref)], sems)[0]
+
+
+def panels_and_transform(panels_ref, ship_ref, rhs_ref, table_ref, out_ref, ship_buf, rhs_buf, table_buf, sems):
+    fetch = start_copies([(panels_ref.at[:, panels_ref.shape[1] - 1], ship_buf)], sems.at[pl.ds(2, 1)])[0]
+    result = transform(rhs_ref, table_ref, out_ref, rhs_buf, table_buf, sems)
+    fetch.wait()
+    ship = start_copies([(ship_buf, ship_ref)], sems.at[pl.ds(2, 1)])[0]
+    result.wait()
+    ship.wait()
 
 
 def ends_kernel(
@@ -152,7 +152,7 @@
 
     @pl.when(elem == 0)
     def _():
-        copy_panels(panels_ref, ship_buf, ship_ref, sems, lambda: transform(rhs_ref, table_ref, out_ref, rhs_buf, table_buf, sems))
+        panels_and_transform(panels_ref, ship_ref, rhs_ref, table_ref, out_ref, ship_buf, rhs_buf, table_buf, sems)
 
     @pl.when(elem == last)
     def _():
@@ -160,7 +160,7 @@
             [(band_ref, band_buf)] + [(panels_ref.at[:, j], panels_buf.at[j]) for j in range(slabs)],
             sems.at[pl.ds(2, slabs + 1)],
         )
-        transform(rhs_ref, table_ref, out_ref, rhs_buf, table_buf, sems)
+        result = transform(rhs_ref, table_ref, out_ref, rhs_buf, table_buf, sems)
         copies[0].wait()
         band_t = [(band_buf[0, j].T, band_buf[1, j].T) for j in range(slabs)]
         lam = [wave_of(k, mode_total, modes) for k in range(modes)]
@@ -182,8 +182,9 @@
             current = [forward[j][k] - product(steps[k], wide(current[k])) for k in range(modes)]
         for k in range(modes):
             ship_buf[k] = product(band_t[0][0] + lam[k] * band_t[0][1], wide(current[k]))
-        for copy in start_copies([(ship_buf, ship_ref)], sems):
+        for copy in start_copies([(ship_buf, ship_ref)], sems.at[pl.ds(1, 1)]):
             copy.wait()
+        result.wait()
 
 
 def between_kernel(hub, panels_ref, rhs_ref, table_ref, old_ref, ship_ref, out_ref, ship_buf, rhs_buf, table_buf, sems):
@@ -191,19 +192,19 @@
 
     @pl.when((elem > 0) & (elem < hub))
     def _():
-        copy_panels(panels_ref, ship_buf, ship_ref, sems, lambda: transform(rhs_ref, table_ref, out_ref, rhs_buf, table_buf, sems))
+        panels_and_transform(panels_ref, ship_ref, rhs_ref, table_ref, out_ref, ship_buf, rhs_buf, table_buf, sems)
 
 
 def late_kernel(hub, rhs_ref, table_ref, old_ref, out_ref, rhs_buf, table_buf, sems):
     @pl.when(lax.axis_index("elem") == hub)
     def _():
-        transform(rhs_ref, table_ref, out_ref, rhs_buf, table_buf, sems)
+        transform(rhs_ref, table_ref, out_ref, rhs_buf, table_buf, sems).wait()
 
 
 def maps_kernel(
     modes, mode_total, hub, place, panels_ref, band_ref, radial_ref, stiff_ref, mass_ref, number_ref, reig_ref, axial_ref, aeig_ref,
-    coup_ref, front_ref, back_ref, w_ref, reig_out, axial_out, weight_out, aeig_out,
-    panels_buf, band_buf, radial_buf, stiff_buf, mass_buf, number_buf, axial_buf, coup_buf, front_buf, back_buf, sems,
+    coup_ref, front_ref, back_ref, behind_ref, w_ref, reig_out, axial_out, weight_out, aeig_out,
+    panels_buf, band_buf, radial_buf, stiff_buf, mass_buf, number_buf, axial_buf, coup_buf, front_buf, back_buf, behind_buf, sems,
 ):
     slabs, size = panels_ref.shape[1:3]
     inner = aeig_ref.shape[1]
@@ -276,6 +277,12 @@
 
         pltpu.make_async_copy(front_buf, front_ref, sems.at[1]).wait()
 
+    @pl.when(lax.axis_index("elem") == lax.axis_size("elem") - 1)
+    def _():
+        behind_maps(behind_buf, band_buf, [wave_of(k, mode_total, modes) for k in range(modes)], w_ref, place)
+        for copy in start_copies([(behind_buf, behind_ref)], sems):
+            copy.wait()
+
 
 def face_push(values, weight, lam):
     rows, size = values.shape
@@ -304,16 +311,16 @@
     return face_push(values, weight, lam)
 
 
-def inner_kernel(modes, mode_total, place, hub, first_call, band_ref, front_ref, *refs):
+def inner_kernel(modes, mode_total, place, hub, first_call, band_ref, front_ref, behind_ref, *refs):
     elem = lax.axis_index("elem")
     if first_call:
         spec_ref, w_ref, reig_ref, axial_ref, weight_ref, aeig_ref, zsrc_ref, inv_ref, reduced_ref, y_ref, send_ref = refs
     else:
         spec_ref, w_ref, reig_ref = refs[:3]
-        axial_ref, weight_ref, aeig_ref, zsrc_ref, inv_ref, reduced_ref, y_ref, load_ref, front_out, band_buf, sems = refs[7:]
+        axial_ref, weight_ref, aeig_ref, zsrc_ref, inv_ref, reduced_ref, y_ref, load_ref, front_out, band_buf, behind_buf, sems = refs[7:]
         inside = (elem > 0) & (elem <= hub)
         early = (front_ref, front_out)
-        late = (band_ref.at[:, 0], band_buf)
+        late = [(band_ref.at[:, 0], band_buf), (behind_ref, behind_buf)]
 
         @pl.when(inside)
         def _():
@@ -321,7 +328,7 @@
 
         @pl.when(elem == lax.axis_size("elem") - 1)
         def _():
-            start_copies([late], sems)
+            start_copies(late, sems)
 
     @pl.when((elem == 0) == first_call)
     def _():
@@ -341,10 +348,10 @@
         def _():
             lam = wave(mode_total, load.shape, modes)
             current = values[-1]
+            for i, pair in enumerate(late):
+                pltpu.make_async_copy(*pair, sems.at[i]).wait()
             for j in range(len(values) - 2, -1, -1):
-                step = face_lift(current, place.band(w_ref, j + 1), lam)
-                current = values[j] - apply(step, w_ref[place.at("panel", j)], modes)
-            pltpu.make_async_copy(*late, sems.at[0]).wait()
+                current = values[j] - apply(current, behind_buf[j], modes)
             load_ref[0] = load + face_lift(current, band_wide(band_buf[0], band_buf[1]), lam)
 
 
@@ -745,11 +752,12 @@
         spectrum = jnp.swapaxes(spectrum, 0, 1).reshape(1, rows, devices * nodes)
     vector = (rows, size)
     matrix = half(many, 2 * size)
-    front, back_map, w, reig, axial, weight, aeig = call(
+    front, back_map, later, w, reig, axial, weight, aeig = call(
         functools.partial(maps_kernel, modes, mode_total, hub, place),
         [
             pltpu.HBM((many, 2 * size), BF16),
             pltpu.HBM((many, 2 * size), BF16),
+            pltpu.HBM((slabs - 1, many, 2 * size), BF16),
             half(place.total, 2 * size),
             kept(*radial_eig.shape),
             pltpu.SMEM(axial_basis.shape, F32),
@@ -773,6 +781,7 @@
             pltpu.SMEM(axial_coupling.shape, F32),
             pltpu.VMEM((many, 2 * size), BF16),
             pltpu.VMEM((many, 2 * size), BF16),
+            pltpu.VMEM((slabs - 1, many, 2 * size), BF16),
             pltpu.SemaphoreType.DMA((slabs + 9,)),
         ],
     )
@@ -780,22 +789,23 @@
     *solve, send = call(
         functools.partial(inner_kernel, modes, mode_total, place, hub, True),
         solves + [kept(*vector)],
-        [band_panels, front, spectrum, w, reig, axial, weight, aeig],
-        anywhere=2,
+        [band_panels, front, later, spectrum, w, reig, axial, weight, aeig],
+        anywhere=3,
         smem=3,
     )
     got = lax.ppermute(send, "elem", [(0, 1)])
     zsrc, inv, reduced, y, load, front = call(
         functools.partial(inner_kernel, modes, mode_total, place, hub, False),
         solves + [kept(2, *vector), matrix],
-        [band_panels, front, spectrum, w, reig, *solve, axial, weight, aeig],
-        anywhere=2,
+        [band_panels, front, later, spectrum, w, reig, *solve, axial, weight, aeig],
+        anywhere=3,
         smem=3,
         scratch=[
             pltpu.VMEM((2, size, size), F32),
+            pltpu.VMEM((slabs - 1, many, 2 * size), BF16),
             pltpu.SemaphoreType.DMA((2,)),
         ],
-        aliases={5 + i: i for i in range(4)},
+        aliases={6 + i: i for i in range(4)},
     )
     far = lax.ppermute(load, "elem", [(last, hub)])
     prev, push = call(

time: 40.2 us -> 39.3 us (0.978)
  Pallas kernels: 12.5 us -> 11.9 us
    ppermute x1, starting transfers between devices: 2.16 us -> 2.78 us  [body(): first = far_map = lax.ppermute(ship, 'elem', [(0, 1), (last, hub)])]
    pallas_call x14, Pallas kernels: 12.5 us -> 11.9 us  [call(): pl.pallas_call(kernel, out_shape=outs, in_specs=[ANY] * free + [HBM] * an...]
    all_to_all x1, starting transfers between devices: 4.34 us -> 3.74 us  [body(): lax.all_to_all(spectrum.reshape(devices, rows, nodes), 'mode', 0, 0, tile...]
where the time goes in v4:
time: 39.3 us; the launch traced here: 39 us
  starting transfers between devices  14.3 us (36%)
  waiting for transfers between devices  12.5 us (32%)
  Pallas kernels  11.9 us (30%)
    pallas_call x14, Pallas kernels, call(): pl.pallas_call(kernel, out_shape=outs, in_specs=[ANY] * free + [HBM] * an...  11.9 us
    ppermute x1, waiting for transfers between devices, body(): got = lax.ppermute(send, 'elem', [(1, 0)])  8.84 us
    all_to_all x1, starting transfers between devices, body(): lax.all_to_all(spectrum.reshape(devices, rows, nodes), 'mode', 0, 0, tile...  3.74 us
    all_to_all x1, waiting for transfers between devices, body(): lax.all_to_all(spectrum.reshape(devices, rows, nodes), 'mode', 0, 0, tile...  3 us
    ppermute x1, starting transfers between devices, body(): first = far_map = lax.ppermute(ship, 'elem', [(0, 1), (last, hub)])  2.78 us
    ppermute x1, starting transfers between devices, body(): got = lax.ppermute(send, 'elem', [(0, 1)])  2.41 us
    ppermute x1, starting transfers between devices, body(): lax.ppermute(ship, 'elem', [(i, i + 1) for i in range(1, hub)])  1.46 us
    ppermute x1, starting transfers between devices, body(): got = lax.ppermute(send, 'elem', [(1, 0)])  1.29 us
  transfers between devices with their start and end apart: 9, of which 3 were waited for; matrix products, arithmetic and copies ran while one was open for 0% of the time, Pallas kernels for 20%

profile of v4, /device:TPU:0, one launch (start us, length us, event | category | flops | bytes accessed | tf_op | source)
XLA Modules:
  0.0 39.0 jit_solution(1253554138889572414)
XLA Ops:
  0.0 2.2 %shard_map.119 = (f32[8,128,128]{2,1,0:T(8,128)}, f32[128,384]{1,0:T(8,128)}) custom-call(f32[8,3,128,128]{3,2,1,0:T(8,128)} %panels_ref.5, f32[2,3,128,128]{3,2,1,0:T(8,128)} %band_ref.13, f32[128,384]{1,0:T(8,128)} %rhs_ref.5, bf16[128,384]{1,0:T(8,128)(2,1)} %constant.19.table_ref), custom_call_target="tpu_custom_call" | custom-call | tf_op jit(solution)/shard_map/pallas_call | solution.py:26
  2.2 2.8 %collective-permute-start.1 = (f32[8,128,128]{2,1,0:T(8,128)}, f32[8,128,128]{2,1,0:T(8,128)S(1)}, u32[]{:S(2)}, u32[]{:S(2)}) collective-permute-start(f32[8,128,128]{2,1,0:T(8,128)} %get-tuple-element.68), channel_id=1, source_target_pairs={{0,1},{3,2},{4,5},{7,6},{8,9},{11,10},{12,13},{15,14},{16,17},{19,... | collective-permute-start | bytes 1572872 | tf_op jit(solution)/shard_map/ppermute | solution.py:730
  5.0 0.1 shard_map.120
  5.1 1.5 %collective-permute-start.3 = (f32[8,128,128]{2,1,0:T(8,128)}, f32[8,128,128]{2,1,0:T(8,128)}, u32[]{:S(2)}, u32[]{:S(2)}) collective-permute-start(f32[8,128,128]{2,1,0:T(8,128)} %get-tuple-element.74), channel_id=1, source_target_pairs={{1,2},{5,6},{9,10},{13,14},{17,18},{21,22},{25,26},{29,30}} | collective-permute-start | bytes 1572872 | tf_op jit(solution)/shard_map/ppermute | solution.py:741
  6.6 0.1 shard_map.121
  6.6 3.7 %all-to-all-start = ((f32[8,16,384]{2,1,0:T(8,128)}), f32[8,16,384]{2,1,0:T(8,128)S(1)}, u32[]{:S(2)}, u32[]{:S(2)}) async-start(f32[8,16,384]{2,1,0:T(8,128)} %bitcast.1), calls=%async_computation | async-start | bytes 393216 | tf_op jit(solution)/shard_map/all_to_all | solution.py:750
  10.4 3.2 %shard_map.118 = (bf16[1024,256]{1,0:T(8,128)(2,1)}, bf16[1024,256]{1,0:T(8,128)(2,1)}, bf16[2,1024,256]{2,1,0:T(8,128)(2,1)}, bf16[5504,256]{1,0:T(8,128)(2,1)S...) custom-call(f32[8,3,128,128]{3,2,1,0:T(8,128)} %panels_ref.5, ...), custom_call_target="tpu_custom_call" | custom-call | tf_op jit(solution)/shard_map/pallas_call | solution.py:26
  13.6 3.0 %all-to-all-done.refs_0_ = f32[8,16,384]{2,1,0:T(8,128)S(1)} async-done(((f32[8,16,384]{2,1,0:T(8,128)}), f32[8,16,384]{2,1,0:T(8,128)S(1)}, u32[]{:S(2)}, u32[]{:S(2)}) %all-to-all-start) | async-done | bytes 196640 | tf_op jit(solution)/shard_map/all_to_all | solution.py:750
  16.6 1.7 %shard_map.122 = (f32[3,7,16,128]{3,2,1,0:T(8,128)S(1)}, f32[3,7,16,128]{3,2,1,0:T(8,128)S(1)}, f32[3,16,128]{2,1,0:T(8,128)S(1)}, f32[3,16,128]{2,1,0:T(8,128)S(1)}, f32[16,128]{1,0:T(8,128)S(1)}) custom-call(f32[2,3,128,128]{3,2,1,0:T(8,128)} %band_ref.13, bf16[1024,256]{1,0:T(8,128)(2,1)} %get-tuple-element.52.front_ref, ...), custom_call_target="tpu_custom_call" | custom-call | tf_op jit(solution)/shard_map/pallas_call | solution.py:26
  18.3 2.4 %collective-permute-start = (f32[16,128]{1,0:T(8,128)S(1)}, f32[16,128]{1,0:T(8,128)S(1)}, u32[]{:S(2)}, u32[]{:S(2)}) collective-permute-start(f32[16,128]{1,0:T(8,128)S(1)} %get-tuple-element.67), channel_id=1, source_target_pairs={{0,1},{4,5},{8,9},{12,13},{16,17},{20,21},{24,25},{28,29}} | collective-permute-start | bytes 24584 | tf_op jit(solution)/shard_map/ppermute | solution.py:796
  20.7 0.7 %collective-permute-start.4 = (f32[2,16,128]{2,1,0:T(8,128)S(1)}, f32[2,16,128]{2,1,0:T(8,128)S(1)}, u32[]{:S(2)}, u32[]{:S(2)}) collective-permute-start(f32[2,16,128]{2,1,0:T(8,128)S(1)} %get-tuple-element.69.load_ref), channel_id=1, source_target_pairs={{3,2},{7,6},{11,10},{15,14},{19,18},{23,22},{27,26},{31,30}} | collective-permute-start | bytes 49160 | tf_op jit(solution)/shard_map/ppermute | solution.py:810
  21.4 0.0 collective-permute-done.1.first_ref.map_ref
  21.4 0.6 %collective-permute-done.got_ref = f32[16,128]{1,0:T(8,128)S(1)} collective-permute-done((f32[16,128]{1,0:T(8,128)S(1)}, f32[16,128]{1,0:T(8,128)S(1)}, u32[]{:S(2)}, u32[]{:S(2)}) %collective-permute-start) | collective-permute-done | bytes 8224 | tf_op jit(solution)/shard_map/ppermute | solution.py:796
  22.0 0.6 %collective-permute-start.2 = (f32[16,128]{1,0:T(8,128)S(1)}, f32[16,128]{1,0:T(8,128)S(1)}, u32[]{:S(2)}, u32[]{:S(2)}) collective-permute-start(f32[16,128]{1,0:T(8,128)S(1)} %get-tuple-element.73), channel_id=1, source_target_pairs={{1,2},{5,6},{9,10},{13,14},{17,18},{21,22},{25,26},{29,30}} | collective-permute-start | bytes 24584 | tf_op jit(solution)/shard_map/ppermute | solution.py:838
  22.7 0.2 shard_map.126
  23.0 0.0 collective-permute-done.4.far_ref
  23.0 0.7 %collective-permute-start.5 = (f32[16,128]{1,0:T(8,128)S(1)}, f32[16,128]{1,0:T(8,128)S(1)}, u32[]{:S(2)}, u32[]{:S(2)}) collective-permute-start(f32[16,128]{1,0:T(8,128)S(1)} %get-tuple-element.83), channel_id=1, source_target_pairs={{2,1},{6,5},{10,9},{14,13},{18,17},{22,21},{26,25},{30,29}} | collective-permute-start | bytes 24584 | tf_op jit(solution)/shard_map/ppermute | solution.py:853
  23.7 0.7 %collective-permute-start.7 = (f32[2,16,128]{2,1,0:T(8,128)S(1)}, f32[2,16,128]{2,1,0:T(8,128)S(1)}, u32[]{:S(2)}, u32[]{:S(2)}) collective-permute-start(f32[2,16,128]{2,1,0:T(8,128)S(1)} %get-tuple-element.90), channel_id=1, source_target_pairs={{2,3},{6,7},{10,11},{14,15},{18,19},{22,23},{26,27},{30,31}} | collective-permute-start | bytes 49160 | tf_op jit(solution)/shard_map/ppermute | solution.py:875
  24.4 0.0 collective-permute-done.5.got_ref
  24.4 1.3 %collective-permute-start.6 = (f32[16,128]{1,0:T(8,128)S(1)}, f32[16,128]{1,0:T(8,128)S(1)}, u32[]{:S(2)}, u32[]{:S(2)}) collective-permute-start(f32[16,128]{1,0:T(8,128)S(1)} %get-tuple-element.89), channel_id=1, source_target_pairs={{1,0},{5,4},{9,8},{13,12},{17,16},{21,20},{25,24},{29,28}} | collective-permute-start | bytes 24584 | tf_op jit(solution)/shard_map/ppermute | solution.py:860
  25.7 2.6 %shard_map.130 = (f32[3,16,128]{2,1,0:T(8,128)S(1)}, bf16[3,1024,256]{2,1,0:T(8,128)(2,1)S(1)}, f32[16,128]{1,0:T(8,128)S(1)}, bf16[3,128,256]{2,1,0:T(8,128)(2,1)S(1)}) custom-call(f32[2,3,128,128]{3,2,1,0:T(8,128)} %band_ref.13, f32[3,128,128]{2,1,0:T(8,128)} %radial_ref.3, ...), custom_call_target="tpu_custom_call", output_to_operand_aliasing={{0}: (9, {})} | custom-call | tf_op jit(solution)/shard_map/pallas_call | solution.py:26
  28.3 8.8 %collective-permute-done.6.got_ref = f32[16,128]{1,0:T(8,128)S(1)} collective-permute-done((f32[16,128]{1,0:T(8,128)S(1)}, f32[16,128]{1,0:T(8,128)S(1)}, u32[]{:S(2)}, u32[]{:S(2)}) %collective-permute-start.6) | collective-permute-done | bytes 8224 | tf_op jit(solution)/shard_map/ppermute | solution.py:860
  37.2 0.0 collective-permute-done.7.last_ref
  37.2 1.6 %shard_map.131 = f32[16,3072]{1,0:T(8,128)} custom-call(f32[3,7,16,128]{3,2,1,0:T(8,128)S(1)} %get-tuple-element.65.zsrc_ref, f32[3,7,16,128]{3,2,1,0:T(8,128)S(1)} %get-tuple-element.66.inv_ref, f32[2,16,128]{2,1,0:T(8,128)S(1)} %get-tuple-element.88.state_ref, f32[16,128]{1,0:T(8,128)S(1)} %collective-permute-done.6.got_ref, ...), custom_call_target="tpu_custom_call" | custom-call | tf_op jit(solution)/shard_map/pallas_call | solution.py:26
  (9 shorter events, 0.1 us)
Async XLA Ops:
  2.2 19.2 %collective-permute-start.1 = (f32[8,128,128]{2,1,0:T(8,128)}, f32[8,128,128]{2,1,0:T(8,128)S(1)}, u32[]{:S(2)}, u32[]{:S(2)}) collective-permute-start(f32[8,128,128]{2,1,0:T(8,128)} %get-tuple-element.68), channel_id=1, source_target_pairs={{0,1},{3,2},{4,5},{7,6},{8,9},{11,10},{12,13},{15,14},{16,17},{19,... | collective-permute-start | bytes 1572872 | tf_op jit(solution)/shard_map/ppermute | solution.py:730
  5.1 17.6 %collective-permute-start.3 = (f32[8,128,128]{2,1,0:T(8,128)}, f32[8,128,128]{2,1,0:T(8,128)}, u32[]{:S(2)}, u32[]{:S(2)}) collective-permute-start(f32[8,128,128]{2,1,0:T(8,128)} %get-tuple-element.74), channel_id=1, source_target_pairs={{1,2},{5,6},{9,10},{13,14},{17,18},{21,22},{25,26},{29,30}} | collective-permute-start | bytes 1572872 | tf_op jit(solution)/shard_map/ppermute | solution.py:741
  6.6 10.0 %all-to-all-start = ((f32[8,16,384]{2,1,0:T(8,128)}), f32[8,16,384]{2,1,0:T(8,128)S(1)}, u32[]{:S(2)}, u32[]{:S(2)}) async-start(f32[8,16,384]{2,1,0:T(8,128)} %bitcast.1), calls=%async_computation | async-start | bytes 393216 | tf_op jit(solution)/shard_map/all_to_all | solution.py:750
  18.3 3.8 %collective-permute-start = (f32[16,128]{1,0:T(8,128)S(1)}, f32[16,128]{1,0:T(8,128)S(1)}, u32[]{:S(2)}, u32[]{:S(2)}) collective-permute-start(f32[16,128]{1,0:T(8,128)S(1)} %get-tuple-element.67), channel_id=1, source_target_pairs={{0,1},{4,5},{8,9},{12,13},{16,17},{20,21},{24,25},{28,29}} | collective-permute-start | bytes 24584 | tf_op jit(solution)/shard_map/ppermute | solution.py:796
  20.7 2.2 %collective-permute-start.4 = (f32[2,16,128]{2,1,0:T(8,128)S(1)}, f32[2,16,128]{2,1,0:T(8,128)S(1)}, u32[]{:S(2)}, u32[]{:S(2)}) collective-permute-start(f32[2,16,128]{2,1,0:T(8,128)S(1)} %get-tuple-element.69.load_ref), channel_id=1, source_target_pairs={{3,2},{7,6},{11,10},{15,14},{19,18},{23,22},{27,26},{31,30}} | collective-permute-start | bytes 49160 | tf_op jit(solution)/shard_map/ppermute | solution.py:810
  22.0 0.9 %collective-permute-start.2 = (f32[16,128]{1,0:T(8,128)S(1)}, f32[16,128]{1,0:T(8,128)S(1)}, u32[]{:S(2)}, u32[]{:S(2)}) collective-permute-start(f32[16,128]{1,0:T(8,128)S(1)} %get-tuple-element.73), channel_id=1, source_target_pairs={{1,2},{5,6},{9,10},{13,14},{17,18},{21,22},{25,26},{29,30}} | collective-permute-start | bytes 24584 | tf_op jit(solution)/shard_map/ppermute | solution.py:838
  23.0 1.4 %collective-permute-start.5 = (f32[16,128]{1,0:T(8,128)S(1)}, f32[16,128]{1,0:T(8,128)S(1)}, u32[]{:S(2)}, u32[]{:S(2)}) collective-permute-start(f32[16,128]{1,0:T(8,128)S(1)} %get-tuple-element.83), channel_id=1, source_target_pairs={{2,1},{6,5},{10,9},{14,13},{18,17},{22,21},{26,25},{30,29}} | collective-permute-start | bytes 24584 | tf_op jit(solution)/shard_map/ppermute | solution.py:853
  23.7 13.5 %collective-permute-start.7 = (f32[2,16,128]{2,1,0:T(8,128)S(1)}, f32[2,16,128]{2,1,0:T(8,128)S(1)}, u32[]{:S(2)}, u32[]{:S(2)}) collective-permute-start(f32[2,16,128]{2,1,0:T(8,128)S(1)} %get-tuple-element.90), channel_id=1, source_target_pairs={{2,3},{6,7},{10,11},{14,15},{18,19},{22,23},{26,27},{30,31}} | collective-permute-start | bytes 49160 | tf_op jit(solution)/shard_map/ppermute | solution.py:875
  24.4 12.7 %collective-permute-start.6 = (f32[16,128]{1,0:T(8,128)S(1)}, f32[16,128]{1,0:T(8,128)S(1)}, u32[]{:S(2)}, u32[]{:S(2)}) collective-permute-start(f32[16,128]{1,0:T(8,128)S(1)} %get-tuple-element.89), channel_id=1, source_target_pairs={{1,0},{5,4},{9,8},{13,12},{17,16},{21,20},{25,24},{29,28}} | collective-permute-start | bytes 24584 | tf_op jit(solution)/shard_map/ppermute | solution.py:860

commit v5 on v4

--- a/solution.py
+++ b/solution.py
@@ -126,8 +126,8 @@
     return copies
 
 
-def transform(rhs_ref, table_ref, out_ref, rhs_buf, table_buf, sems):
-    for copy in start_copies([(rhs_ref, rhs_buf), (table_ref, table_buf)], sems):
+def transform(rhs_ref, table_ref, out_ref, rhs_buf, table_buf, sems, started=None):
+    for copy in started or start_copies([(rhs_ref, rhs_buf), (table_ref, table_buf)], sems):
         copy.wait()
     high, low = split(rhs_buf[...])
     rhs_buf[...] = dot(table_buf[...], jnp.concatenate([high, high, low], axis=0))
@@ -135,12 +135,16 @@
 
 
 def panels_and_transform(panels_ref, ship_ref, rhs_ref, table_ref, out_ref, ship_buf, rhs_buf, table_buf, sems):
-    fetch = start_copies([(panels_ref.at[:, panels_ref.shape[1] - 1], ship_buf)], sems.at[pl.ds(2, 1)])[0]
+    half = ship_buf.shape[0] // 2
+    parts = [pl.ds(0, half), pl.ds(half, ship_buf.shape[0] - half)]
+    fetch = start_copies([(panels_ref.at[part, panels_ref.shape[1] - 1], ship_buf.at[part]) for part in parts], sems.at[pl.ds(2, 2)])
     result = transform(rhs_ref, table_ref, out_ref, rhs_buf, table_buf, sems)
-    fetch.wait()
-    ship = start_copies([(ship_buf, ship_ref)], sems.at[pl.ds(2, 1)])[0]
-    result.wait()
-    ship.wait()
+    ship = []
+    for i, part in enumerate(parts):
+        fetch[i].wait()
+        ship += start_copies([(ship_buf.at[part], ship_ref.at[part])], sems.at[pl.ds(2 + i, 1)])
+    for copy in [result] + ship:
+        copy.wait()
 
 
 def ends_kernel(
@@ -160,7 +164,7 @@
             [(band_ref, band_buf)] + [(panels_ref.at[:, j], panels_buf.at[j]) for j in range(slabs)],
             sems.at[pl.ds(2, slabs + 1)],
         )
-        result = transform(rhs_ref, table_ref, out_ref, rhs_buf, table_buf, sems)
+        started = start_copies([(rhs_ref, rhs_buf), (table_ref, table_buf)], sems)
         copies[0].wait()
         band_t = [(band_buf[0, j].T, band_buf[1, j].T) for j in range(slabs)]
         lam = [wave_of(k, mode_total, modes) for k in range(modes)]
@@ -180,11 +184,15 @@
                 product(panels_buf[j, k], wide(band_t[j + 1][0] + lam[k] * band_t[j + 1][1])) for k in range(modes)
             ]
             current = [forward[j][k] - product(steps[k], wide(current[k])) for k in range(modes)]
-        for k in range(modes):
-            ship_buf[k] = product(band_t[0][0] + lam[k] * band_t[0][1], wide(current[k]))
-        for copy in start_copies([(ship_buf, ship_ref)], sems.at[pl.ds(1, 1)]):
+        ship = [transform(rhs_ref, table_ref, out_ref, rhs_buf, table_buf, sems, started)]
+        half = modes // 2
+        for i, part in enumerate((range(half), range(half, modes))):
+            for k in part:
+                ship_buf[k] = product(band_t[0][0] + lam[k] * band_t[0][1], wide(current[k]))
+            rows = pl.ds(part.start, len(part))
+            ship += start_copies([(ship_buf.at[rows], ship_ref.at[rows])], sems.at[pl.ds(2 + i, 1)])
+        for copy in ship:
             copy.wait()
-        result.wait()
 
 
 def between_kernel(hub, panels_ref, rhs_ref, table_ref, old_ref, ship_ref, out_ref, ship_buf, rhs_buf, table_buf, sems):
@@ -548,7 +556,7 @@
 
 
 def own_map_kernel(
-    modes, mode_total, hub, place, band_ref, radial_ref, state_ref, reduced_ref, y_ref, w_ref, prev_ref, ahead_ref, behind_ref, old_ref,
+    modes, mode_total, hub, place, band_ref, radial_ref, state_ref, reduced_ref, y_ref, w_ref, front_ref, prev_ref, ahead_ref, behind_ref, old_ref,
     found_ref, own_ref, before_ref, radt_ref, ahead_buf, behind_buf, band_buf, radial_buf, sems,
 ):
     slabs, rows, size = reduced_ref.shape
@@ -567,6 +575,9 @@
         panels = [w_ref[place.at("panel", j)] for j in range(slabs)]
         before, values = state_ref[0], []
         for j in range(slabs):
+            if j == slabs - 1:
+                values.append(y_ref[j] + apply(before, front_ref[...], modes))
+                continue
             solved = apply(reduced_ref[j], panels[j], modes)
             values.append(solved - apply(values[-1] if j > 0 else before, ahead_ref[j], modes))
         found = backward_values(values, state_ref[1], panels[-1], behind_ref, modes)
@@ -818,7 +829,7 @@
     prev, later_push, ahead, behind, hub_back, hub_base, cross, far_weight = call(
         functools.partial(hub_map_kernel, modes, mode_total, hub, place),
         [
-            half(2 * size, many), kept(*vector), half(slabs, many, 2 * size), half(slabs - 1, many, 2 * size), matrix,
+            half(2 * size, many), kept(*vector), half(slabs - 1, many, 2 * size), half(slabs - 1, many, 2 * size), matrix,
             kept(*vector), matrix, half(2 * size, many),
         ],
         [far_map, pprev, band_panels, back_map, load, y, w, front, prev, push],
@@ -861,7 +872,7 @@
     found, own, before, radt = call(
         functools.partial(own_map_kernel, modes, mode_total, hub, place),
         [kept(slabs, *vector), half(slabs, many, 2 * size), kept(*vector), half(slabs, size, 2 * size)],
-        [band_panels, radial_basis, state, reduced, y, w, prev, ahead, behind, found],
+        [band_panels, radial_basis, state, reduced, y, w, front, prev, ahead, behind, found],
         anywhere=2,
         scratch=[
             pltpu.VMEM((slabs, many, 2 * size), BF16),
@@ -870,7 +881,7 @@
             pltpu.VMEM(radial_basis.shape, F32),
             pltpu.SemaphoreType.DMA((2,)),
         ],
-        aliases={9: 0},
+        aliases={10: 0},
     )
     final = lax.ppermute(final, "elem", [(hub, last)])
     return call(

time: 39.3 us -> 38.7 us (0.985)
  waiting for transfers between devices: 12.5 us -> 11.8 us
    ppermute x1, waiting for transfers between devices: 8.84 us -> 8.17 us  [body(): got = lax.ppermute(send, 'elem', [(1, 0)])]
where the time goes in v5:
time: 38.7 us; the launch traced here: 38.3 us
  starting transfers between devices  14.3 us (37%)
  Pallas kernels  11.8 us (30%)
  waiting for transfers between devices  11.8 us (30%)
    pallas_call x14, Pallas kernels, call(): pl.pallas_call(kernel, out_shape=outs, in_specs=[ANY] * free + [HBM] * an...  11.8 us
    ppermute x1, waiting for transfers between devices, body(): got = lax.ppermute(send, 'elem', [(1, 0)])  8.17 us
    all_to_all x1, starting transfers between devices, body(): lax.all_to_all(spectrum.reshape(devices, rows, nodes), 'mode', 0, 0, tile...  3.74 us
    all_to_all x1, waiting for transfers between devices, body(): lax.all_to_all(spectrum.reshape(devices, rows, nodes), 'mode', 0, 0, tile...  3 us
    ppermute x1, starting transfers between devices, body(): first = far_map = lax.ppermute(ship, 'elem', [(0, 1), (last, hub)])  2.8 us
    ppermute x1, starting transfers between devices, body(): got = lax.ppermute(send, 'elem', [(0, 1)])  2.4 us
    ppermute x1, starting transfers between devices, body(): lax.ppermute(ship, 'elem', [(i, i + 1) for i in range(1, hub)])  1.46 us
    ppermute x1, starting transfers between devices, body(): got = lax.ppermute(send, 'elem', [(1, 0)])  1.29 us
  transfers between devices with their start and end apart: 9, of which 3 were waited for; matrix products, arithmetic and copies ran while one was open for 0% of the time, Pallas kernels for 20%

profile of v5, /device:TPU:0, one launch (start us, length us, event | category | flops | bytes accessed | tf_op | source)
XLA Modules:
  0.0 38.3 jit_solution(14002449168138581347)
XLA Ops:
  0.0 2.2 %shard_map.119 = (f32[8,128,128]{2,1,0:T(8,128)}, f32[128,384]{1,0:T(8,128)}) custom-call(f32[8,3,128,128]{3,2,1,0:T(8,128)} %panels_ref.5, f32[2,3,128,128]{3,2,1,0:T(8,128)} %band_ref.13, f32[128,384]{1,0:T(8,128)} %rhs_ref.5, bf16[128,384]{1,0:T(8,128)(2,1)} %constant.19.table_ref), custom_call_target="tpu_custom_call" | custom-call | tf_op jit(solution)/shard_map/pallas_call | solution.py:26
  2.2 2.8 %collective-permute-start.1 = (f32[8,128,128]{2,1,0:T(8,128)}, f32[8,128,128]{2,1,0:T(8,128)S(1)}, u32[]{:S(2)}, u32[]{:S(2)}) collective-permute-start(f32[8,128,128]{2,1,0:T(8,128)} %get-tuple-element.68), channel_id=1, source_target_pairs={{0,1},{3,2},{4,5},{7,6},{8,9},{11,10},{12,13},{15,14},{16,17},{19,... | collective-permute-start | bytes 1572872 | tf_op jit(solution)/shard_map/ppermute | solution.py:741
  5.0 0.1 shard_map.120
  5.1 1.5 %collective-permute-start.3 = (f32[8,128,128]{2,1,0:T(8,128)}, f32[8,128,128]{2,1,0:T(8,128)}, u32[]{:S(2)}, u32[]{:S(2)}) collective-permute-start(f32[8,128,128]{2,1,0:T(8,128)} %get-tuple-element.74), channel_id=1, source_target_pairs={{1,2},{5,6},{9,10},{13,14},{17,18},{21,22},{25,26},{29,30}} | collective-permute-start | bytes 1572872 | tf_op jit(solution)/shard_map/ppermute | solution.py:752
  6.6 0.1 shard_map.121
  6.6 3.7 %all-to-all-start = ((f32[8,16,384]{2,1,0:T(8,128)}), f32[8,16,384]{2,1,0:T(8,128)S(1)}, u32[]{:S(2)}, u32[]{:S(2)}) async-start(f32[8,16,384]{2,1,0:T(8,128)} %bitcast.1), calls=%async_computation | async-start | bytes 393216 | tf_op jit(solution)/shard_map/all_to_all | solution.py:761
  10.4 3.2 %shard_map.118 = (bf16[1024,256]{1,0:T(8,128)(2,1)}, bf16[1024,256]{1,0:T(8,128)(2,1)}, bf16[2,1024,256]{2,1,0:T(8,128)(2,1)}, bf16[5504,256]{1,0:T(8,128)(2,1)S...) custom-call(f32[8,3,128,128]{3,2,1,0:T(8,128)} %panels_ref.5, ...), custom_call_target="tpu_custom_call" | custom-call | tf_op jit(solution)/shard_map/pallas_call | solution.py:26
  13.6 3.0 %all-to-all-done.refs_0_ = f32[8,16,384]{2,1,0:T(8,128)S(1)} async-done(((f32[8,16,384]{2,1,0:T(8,128)}), f32[8,16,384]{2,1,0:T(8,128)S(1)}, u32[]{:S(2)}, u32[]{:S(2)}) %all-to-all-start) | async-done | bytes 196640 | tf_op jit(solution)/shard_map/all_to_all | solution.py:761
  16.6 1.7 %shard_map.122 = (f32[3,7,16,128]{3,2,1,0:T(8,128)S(1)}, f32[3,7,16,128]{3,2,1,0:T(8,128)S(1)}, f32[3,16,128]{2,1,0:T(8,128)S(1)}, f32[3,16,128]{2,1,0:T(8,128)S(1)}, f32[16,128]{1,0:T(8,128)S(1)}) custom-call(f32[2,3,128,128]{3,2,1,0:T(8,128)} %band_ref.13, bf16[1024,256]{1,0:T(8,128)(2,1)} %get-tuple-element.52.front_ref, ...), custom_call_target="tpu_custom_call" | custom-call | tf_op jit(solution)/shard_map/pallas_call | solution.py:26
  18.3 2.4 %collective-permute-start = (f32[16,128]{1,0:T(8,128)S(1)}, f32[16,128]{1,0:T(8,128)S(1)}, u32[]{:S(2)}, u32[]{:S(2)}) collective-permute-start(f32[16,128]{1,0:T(8,128)S(1)} %get-tuple-element.67), channel_id=1, source_target_pairs={{0,1},{4,5},{8,9},{12,13},{16,17},{20,21},{24,25},{28,29}} | collective-permute-start | bytes 24584 | tf_op jit(solution)/shard_map/ppermute | solution.py:807
  20.7 0.7 %collective-permute-start.4 = (f32[2,16,128]{2,1,0:T(8,128)S(1)}, f32[2,16,128]{2,1,0:T(8,128)S(1)}, u32[]{:S(2)}, u32[]{:S(2)}) collective-permute-start(f32[2,16,128]{2,1,0:T(8,128)S(1)} %get-tuple-element.69.load_ref), channel_id=1, source_target_pairs={{3,2},{7,6},{11,10},{15,14},{19,18},{23,22},{27,26},{31,30}} | collective-permute-start | bytes 49160 | tf_op jit(solution)/shard_map/ppermute | solution.py:821
  21.4 0.0 collective-permute-done.1.first_ref.map_ref
  21.4 0.6 %collective-permute-done.got_ref = f32[16,128]{1,0:T(8,128)S(1)} collective-permute-done((f32[16,128]{1,0:T(8,128)S(1)}, f32[16,128]{1,0:T(8,128)S(1)}, u32[]{:S(2)}, u32[]{:S(2)}) %collective-permute-start) | collective-permute-done | bytes 8224 | tf_op jit(solution)/shard_map/ppermute | solution.py:807
  22.0 0.6 %collective-permute-start.2 = (f32[16,128]{1,0:T(8,128)S(1)}, f32[16,128]{1,0:T(8,128)S(1)}, u32[]{:S(2)}, u32[]{:S(2)}) collective-permute-start(f32[16,128]{1,0:T(8,128)S(1)} %get-tuple-element.73), channel_id=1, source_target_pairs={{1,2},{5,6},{9,10},{13,14},{17,18},{21,22},{25,26},{29,30}} | collective-permute-start | bytes 24584 | tf_op jit(solution)/shard_map/ppermute | solution.py:849
  22.7 0.0 collective-permute-done.3.pprev_ref
  22.7 0.1 shard_map.126
  22.8 0.2 shard_map.127
  23.0 0.7 %collective-permute-start.5 = (f32[16,128]{1,0:T(8,128)S(1)}, f32[16,128]{1,0:T(8,128)S(1)}, u32[]{:S(2)}, u32[]{:S(2)}) collective-permute-start(f32[16,128]{1,0:T(8,128)S(1)} %get-tuple-element.83), channel_id=1, source_target_pairs={{2,1},{6,5},{10,9},{14,13},{18,17},{22,21},{26,25},{30,29}} | collective-permute-start | bytes 24584 | tf_op jit(solution)/shard_map/ppermute | solution.py:864
  23.7 0.7 %collective-permute-start.7 = (f32[2,16,128]{2,1,0:T(8,128)S(1)}, f32[2,16,128]{2,1,0:T(8,128)S(1)}, u32[]{:S(2)}, u32[]{:S(2)}) collective-permute-start(f32[2,16,128]{2,1,0:T(8,128)S(1)} %get-tuple-element.90), channel_id=1, source_target_pairs={{2,3},{6,7},{10,11},{14,15},{18,19},{22,23},{26,27},{30,31}} | collective-permute-start | bytes 49160 | tf_op jit(solution)/shard_map/ppermute | solution.py:886
  24.4 1.3 %collective-permute-start.6 = (f32[16,128]{1,0:T(8,128)S(1)}, f32[16,128]{1,0:T(8,128)S(1)}, u32[]{:S(2)}, u32[]{:S(2)}) collective-permute-start(f32[16,128]{1,0:T(8,128)S(1)} %get-tuple-element.89), channel_id=1, source_target_pairs={{1,0},{5,4},{9,8},{13,12},{17,16},{21,20},{25,24},{29,28}} | collective-permute-start | bytes 24584 | tf_op jit(solution)/shard_map/ppermute | solution.py:871
  25.7 2.6 %shard_map.130 = (f32[3,16,128]{2,1,0:T(8,128)S(1)}, bf16[3,1024,256]{2,1,0:T(8,128)(2,1)S(1)}, f32[16,128]{1,0:T(8,128)S(1)}, bf16[3,128,256]{2,1,0:T(8,128)(2,1)S(1)}) custom-call(f32[2,3,128,128]{3,2,1,0:T(8,128)} %band_ref.13, f32[3,128,128]{2,1,0:T(8,128)} %radial_ref.3, ...), custom_call_target="tpu_custom_call", output_to_operand_aliasing={{0}: (10, {})} | custom-call | tf_op jit(solution)/shard_map/pallas_call | solution.py:26
  28.3 8.2 %collective-permute-done.6.got_ref = f32[16,128]{1,0:T(8,128)S(1)} collective-permute-done((f32[16,128]{1,0:T(8,128)S(1)}, f32[16,128]{1,0:T(8,128)S(1)}, u32[]{:S(2)}, u32[]{:S(2)}) %collective-permute-start.6) | collective-permute-done | bytes 8224 | tf_op jit(solution)/shard_map/ppermute | solution.py:871
  36.5 0.0 collective-permute-done.7.last_ref
  36.5 1.6 %shard_map.131 = f32[16,3072]{1,0:T(8,128)} custom-call(f32[3,7,16,128]{3,2,1,0:T(8,128)S(1)} %get-tuple-element.65.zsrc_ref, f32[3,7,16,128]{3,2,1,0:T(8,128)S(1)} %get-tuple-element.66.inv_ref, f32[2,16,128]{2,1,0:T(8,128)S(1)} %get-tuple-element.88.state_ref, f32[16,128]{1,0:T(8,128)S(1)} %collective-permute-done.6.got_ref, ...), custom_call_target="tpu_custom_call" | custom-call | tf_op jit(solution)/shard_map/pallas_call | solution.py:26
  (9 shorter events, 0.1 us)
Async XLA Ops:
  2.2 19.2 %collective-permute-start.1 = (f32[8,128,128]{2,1,0:T(8,128)}, f32[8,128,128]{2,1,0:T(8,128)S(1)}, u32[]{:S(2)}, u32[]{:S(2)}) collective-permute-start(f32[8,128,128]{2,1,0:T(8,128)} %get-tuple-element.68), channel_id=1, source_target_pairs={{0,1},{3,2},{4,5},{7,6},{8,9},{11,10},{12,13},{15,14},{16,17},{19,... | collective-permute-start | bytes 1572872 | tf_op jit(solution)/shard_map/ppermute | solution.py:741
  5.1 17.6 %collective-permute-start.3 = (f32[8,128,128]{2,1,0:T(8,128)}, f32[8,128,128]{2,1,0:T(8,128)}, u32[]{:S(2)}, u32[]{:S(2)}) collective-permute-start(f32[8,128,128]{2,1,0:T(8,128)} %get-tuple-element.74), channel_id=1, source_target_pairs={{1,2},{5,6},{9,10},{13,14},{17,18},{21,22},{25,26},{29,30}} | collective-permute-start | bytes 1572872 | tf_op jit(solution)/shard_map/ppermute | solution.py:752
  6.6 10.0 %all-to-all-start = ((f32[8,16,384]{2,1,0:T(8,128)}), f32[8,16,384]{2,1,0:T(8,128)S(1)}, u32[]{:S(2)}, u32[]{:S(2)}) async-start(f32[8,16,384]{2,1,0:T(8,128)} %bitcast.1), calls=%async_computation | async-start | bytes 393216 | tf_op jit(solution)/shard_map/all_to_all | solution.py:761
  18.3 3.8 %collective-permute-start = (f32[16,128]{1,0:T(8,128)S(1)}, f32[16,128]{1,0:T(8,128)S(1)}, u32[]{:S(2)}, u32[]{:S(2)}) collective-permute-start(f32[16,128]{1,0:T(8,128)S(1)} %get-tuple-element.67), channel_id=1, source_target_pairs={{0,1},{4,5},{8,9},{12,13},{16,17},{20,21},{24,25},{28,29}} | collective-permute-start | bytes 24584 | tf_op jit(solution)/shard_map/ppermute | solution.py:807
  20.7 2.0 %collective-permute-start.4 = (f32[2,16,128]{2,1,0:T(8,128)S(1)}, f32[2,16,128]{2,1,0:T(8,128)S(1)}, u32[]{:S(2)}, u32[]{:S(2)}) collective-permute-start(f32[2,16,128]{2,1,0:T(8,128)S(1)} %get-tuple-element.69.load_ref), channel_id=1, source_target_pairs={{3,2},{7,6},{11,10},{15,14},{19,18},{23,22},{27,26},{31,30}} | collective-permute-start | bytes 49160 | tf_op jit(solution)/shard_map/ppermute | solution.py:821
  22.0 0.7 %collective-permute-start.2 = (f32[16,128]{1,0:T(8,128)S(1)}, f32[16,128]{1,0:T(8,128)S(1)}, u32[]{:S(2)}, u32[]{:S(2)}) collective-permute-start(f32[16,128]{1,0:T(8,128)S(1)} %get-tuple-element.73), channel_id=1, source_target_pairs={{1,2},{5,6},{9,10},{13,14},{17,18},{21,22},{25,26},{29,30}} | collective-permute-start | bytes 24584 | tf_op jit(solution)/shard_map/ppermute | solution.py:849
  23.0 1.4 %collective-permute-start.5 = (f32[16,128]{1,0:T(8,128)S(1)}, f32[16,128]{1,0:T(8,128)S(1)}, u32[]{:S(2)}, u32[]{:S(2)}) collective-permute-start(f32[16,128]{1,0:T(8,128)S(1)} %get-tuple-element.83), channel_id=1, source_target_pairs={{2,1},{6,5},{10,9},{14,13},{18,17},{22,21},{26,25},{30,29}} | collective-permute-start | bytes 24584 | tf_op jit(solution)/shard_map/ppermute | solution.py:864
  23.7 12.8 %collective-permute-start.7 = (f32[2,16,128]{2,1,0:T(8,128)S(1)}, f32[2,16,128]{2,1,0:T(8,128)S(1)}, u32[]{:S(2)}, u32[]{:S(2)}) collective-permute-start(f32[2,16,128]{2,1,0:T(8,128)S(1)} %get-tuple-element.90), channel_id=1, source_target_pairs={{2,3},{6,7},{10,11},{14,15},{18,19},{22,23},{26,27},{30,31}} | collective-permute-start | bytes 49160 | tf_op jit(solution)/shard_map/ppermute | solution.py:886
  24.4 12.1 %collective-permute-start.6 = (f32[16,128]{1,0:T(8,128)S(1)}, f32[16,128]{1,0:T(8,128)S(1)}, u32[]{:S(2)}, u32[]{:S(2)}) collective-permute-start(f32[16,128]{1,0:T(8,128)S(1)} %get-tuple-element.89), channel_id=1, source_target_pairs={{1,0},{5,4},{9,8},{13,12},{17,16},{21,20},{25,24},{29,28}} | collective-permute-start | bytes 24584 | tf_op jit(solution)/shard_map/ppermute | solution.py:871

commit v6 on v5

--- a/solution.py
+++ b/solution.py
@@ -87,10 +87,10 @@
 
 class Weights:
     def __init__(self, size, *entries):
-        self.size, self.rows = size, {}
+        self.size, self.rows, self.counts = size, {}, {}
         self.total = 0
         for name, count, rows in entries:
-            self.rows[name] = (self.total, rows)
+            self.rows[name], self.counts[name] = (self.total, rows), count
             self.total += count * rows
 
     def at(self, name, index, mode=None):
@@ -488,7 +488,7 @@
 
 def hub_map_kernel(
     modes, mode_total, hub, place, map_ref, pprev_ref, band_ref, given_ref, load_ref, y_ref, w_ref, front_ref, old_prev_ref, old_push_ref,
-    prev_ref, push_ref, ahead_ref, behind_ref, back_ref, base_ref, cross_ref, far_ref, band_buf, map_buf, prev_buf, sems,
+    prev_ref, push_ref, ahead_ref, behind_ref, back_ref, base_ref, cross_ref, through_ref, band_buf, map_buf, prev_buf, sems,
 ):
     slabs, rows, size = y_ref.shape
     lam = wave(mode_total, (rows, size), modes)
@@ -522,8 +522,9 @@
         found = backward_values([y_ref[j] for j in range(slabs)], None, None, behind_ref, modes)
         base_ref[...] = load_ref[1] + face_lift(found[0], band_wide(band_buf[0, 0], band_buf[1, 0]), lam)
         copies[1].wait()
-        far_ref[...] = previous_weight(map_buf, modes)
         given.wait()
+        for k in range(modes):
+            through_ref[part(k)] = wide(product(map_buf[k].T, back_ref[part(k)]))
 
     @pl.when(inside)
     def _():
@@ -534,25 +535,33 @@
 
 
 def hub_kernel(
-    modes, at, place, got_ref, push_ref, far_ref, far_weight_ref, y_ref, front_ref, back_ref, cross_ref, base_ref, w_ref, old_ref,
-    state_ref, send_ref, last_ref,
+    modes, at, place, got_ref, push_ref, far_ref, through_ref, y_ref, front_ref, back_ref, cross_ref, base_ref, w_ref,
+    send_ref, values_ref,
 ):
     slabs = y_ref.shape[0]
 
     @pl.when(lax.axis_index("elem") == at)
     def _():
-        panel = w_ref[place.at("panel", slabs - 1)]
-        load = apply(far_ref[1], panel, modes)
         before = got_ref[...] - push_ref[...]
-        state_ref[0] = before
+        load = apply(far_ref[1], w_ref[place.at("panel", slabs - 1)], modes)
         value = y_ref[slabs - 1] + apply(before, front_ref[...], modes)
-        out = base_ref[...] + apply(before, cross_ref[...], modes)
+        out = base_ref[...] + apply(before, cross_ref[...], modes) + apply(far_ref[0], back_ref[...], modes)
         final = value - load
-        after = far_ref[0] + apply_nt(final, far_weight_ref[...], modes)
+        send_ref[...] = out + apply(final, through_ref[...], modes)
+        values_ref[0] = before
+        values_ref[1] = value
+        values_ref[2] = final
+
+
+def hub_values_kernel(modes, at, place, map_ref, far_ref, values_ref, w_ref, old_ref, state_ref, last_ref):
+    @pl.when(lax.axis_index("elem") == at)
+    def _():
+        final = values_ref[2]
+        after = far_ref[0] + apply_nt(final, previous_weight(map_ref, modes), modes)
+        state_ref[0] = values_ref[0]
         state_ref[1] = after
-        send_ref[...] = out + apply(after, back_ref[...], modes)
         last_ref[0] = final
-        last_ref[1] = value - apply(after, panel, modes)
+        last_ref[1] = values_ref[1] - apply(after, w_ref[place.at("panel", place.counts["panel"] - 1)], modes)
 
 
 def own_map_kernel(
@@ -826,11 +835,11 @@
         free=1,
         scratch=[panels_buffer, pltpu.SemaphoreType.DMA((1,))],
     )
-    prev, later_push, ahead, behind, hub_back, hub_base, cross, far_weight = call(
+    prev, later_push, ahead, behind, hub_back, hub_base, cross, through = call(
         functools.partial(hub_map_kernel, modes, mode_total, hub, place),
         [
             half(2 * size, many), kept(*vector), half(slabs - 1, many, 2 * size), half(slabs - 1, many, 2 * size), matrix,
-            kept(*vector), matrix, half(2 * size, many),
+            kept(*vector), matrix, matrix,
         ],
         [far_map, pprev, band_panels, back_map, load, y, w, front, prev, push],
         free=2,
@@ -847,11 +856,16 @@
             aliases={4: 0},
         )
         got = lax.ppermute(send, "elem", [(at, at + 1)])
-    state, send, final = call(
+    send, values = call(
         functools.partial(hub_kernel, modes, hub, place),
-        [kept(*state.shape), shape(*vector), shape(2, *vector)],
-        [got, push if hub == 1 else later_push, far, far_weight, y, front, hub_back, cross, hub_base, w, state],
-        aliases={10: 0},
+        [shape(*vector), kept(3, *vector)],
+        [got, push if hub == 1 else later_push, far, through, y, front, hub_back, cross, hub_base, w],
+    )
+    state, final = call(
+        functools.partial(hub_values_kernel, modes, hub, place),
+        [kept(*state.shape), shape(2, *vector)],
+        [far_map, far, values, w, state],
+        aliases={4: 0},
     )
     base, found, back = call(
         functools.partial(base_kernel, modes, mode_total, hub, place),

time: 38.7 us -> 38.3 us (0.990)
  waiting for transfers between devices: 11.8 us -> 11.4 us
    ppermute x1, waiting for transfers between devices: 8.17 us -> 7.74 us  [body(): got = lax.ppermute(send, 'elem', [(1, 0)])]
    pallas_call x14 -> x15, Pallas kernels: 11.8 us -> 11.8 us  [call(): pl.pallas_call(kernel, out_shape=outs, in_specs=[ANY] * free + [HBM] * an...]
  transfers between devices with their start and end apart: 9 -> 9, of which waited for: 3 -> 3; matrix products, arithmetic and copies ran while one was open for 0% -> 0% of each run, Pallas kernels for 20% -> 21%
where the time goes in v6:
time: 38.3 us; the launch traced here: 37.9 us
  starting transfers between devices  14.3 us (37%)
  Pallas kernels  11.8 us (31%)
  waiting for transfers between devices  11.4 us (30%)
    pallas_call x15, Pallas kernels, call(): pl.pallas_call(kernel, out_shape=outs, in_specs=[ANY] * free + [HBM] * an...  11.8 us
    ppermute x1, waiting for transfers between devices, body(): got = lax.ppermute(send, 'elem', [(1, 0)])  7.74 us
    all_to_all x1, starting transfers between devices, body(): lax.all_to_all(spectrum.reshape(devices, rows, nodes), 'mode', 0, 0, tile...  3.74 us
    all_to_all x1, waiting for transfers between devices, body(): lax.all_to_all(spectrum.reshape(devices, rows, nodes), 'mode', 0, 0, tile...  3 us
    ppermute x1, starting transfers between devices, body(): first = far_map = lax.ppermute(ship, 'elem', [(0, 1), (last, hub)])  2.8 us
    ppermute x1, starting transfers between devices, body(): got = lax.ppermute(send, 'elem', [(0, 1)])  2.41 us
    ppermute x1, starting transfers between devices, body(): lax.ppermute(ship, 'elem', [(i, i + 1) for i in range(1, hub)])  1.46 us
    ppermute x1, starting transfers between devices, body(): got = lax.ppermute(send, 'elem', [(1, 0)])  1.29 us
  transfers between devices with their start and end apart: 9, of which 3 were waited for; matrix products, arithmetic and copies ran while one was open for 0% of the time, Pallas kernels for 21%

profile of v6, /device:TPU:0, one launch (start us, length us, event | category | flops | bytes accessed | tf_op | source)
XLA Modules:
  0.0 37.9 jit_solution(10417575829630434241)
XLA Ops:
  0.0 2.2 %shard_map.119 = (f32[8,128,128]{2,1,0:T(8,128)}, f32[128,384]{1,0:T(8,128)}) custom-call(f32[8,3,128,128]{3,2,1,0:T(8,128)} %panels_ref.5, f32[2,3,128,128]{3,2,1,0:T(8,128)} %band_ref.13, f32[128,384]{1,0:T(8,128)} %rhs_ref.5, bf16[128,384]{1,0:T(8,128)(2,1)} %constant.19.table_ref), custom_call_target="tpu_custom_call" | custom-call | tf_op jit(solution)/shard_map/pallas_call | solution.py:26
  2.2 2.8 %collective-permute-start.1 = (f32[8,128,128]{2,1,0:T(8,128)}, f32[8,128,128]{2,1,0:T(8,128)S(1)}, u32[]{:S(2)}, u32[]{:S(2)}) collective-permute-start(f32[8,128,128]{2,1,0:T(8,128)} %get-tuple-element.69), channel_id=1, source_target_pairs={{0,1},{3,2},{4,5},{7,6},{8,9},{11,10},{12,13},{15,14},{16,17},{19,... | collective-permute-start | bytes 1572872 | tf_op jit(solution)/shard_map/ppermute | solution.py:750
  5.0 0.1 shard_map.120
  5.1 1.5 %collective-permute-start.3 = (f32[8,128,128]{2,1,0:T(8,128)}, f32[8,128,128]{2,1,0:T(8,128)}, u32[]{:S(2)}, u32[]{:S(2)}) collective-permute-start(f32[8,128,128]{2,1,0:T(8,128)} %get-tuple-element.75), channel_id=1, source_target_pairs={{1,2},{5,6},{9,10},{13,14},{17,18},{21,22},{25,26},{29,30}} | collective-permute-start | bytes 1572872 | tf_op jit(solution)/shard_map/ppermute | solution.py:761
  6.6 0.1 shard_map.121
  6.6 3.7 %all-to-all-start = ((f32[8,16,384]{2,1,0:T(8,128)}), f32[8,16,384]{2,1,0:T(8,128)S(1)}, u32[]{:S(2)}, u32[]{:S(2)}) async-start(f32[8,16,384]{2,1,0:T(8,128)} %bitcast.1), calls=%async_computation | async-start | bytes 393216 | tf_op jit(solution)/shard_map/all_to_all | solution.py:770
  10.4 3.2 %shard_map.118 = (bf16[1024,256]{1,0:T(8,128)(2,1)}, bf16[1024,256]{1,0:T(8,128)(2,1)}, bf16[2,1024,256]{2,1,0:T(8,128)(2,1)}, bf16[5504,256]{1,0:T(8,128)(2,1)S...) custom-call(f32[8,3,128,128]{3,2,1,0:T(8,128)} %panels_ref.5, ...), custom_call_target="tpu_custom_call" | custom-call | tf_op jit(solution)/shard_map/pallas_call | solution.py:26
  13.6 3.0 %all-to-all-done.refs_0_ = f32[8,16,384]{2,1,0:T(8,128)S(1)} async-done(((f32[8,16,384]{2,1,0:T(8,128)}), f32[8,16,384]{2,1,0:T(8,128)S(1)}, u32[]{:S(2)}, u32[]{:S(2)}) %all-to-all-start) | async-done | bytes 196640 | tf_op jit(solution)/shard_map/all_to_all | solution.py:770
  16.6 1.7 %shard_map.122 = (f32[3,7,16,128]{3,2,1,0:T(8,128)S(1)}, f32[3,7,16,128]{3,2,1,0:T(8,128)S(1)}, f32[3,16,128]{2,1,0:T(8,128)S(1)}, f32[3,16,128]{2,1,0:T(8,128)S(1)}, f32[16,128]{1,0:T(8,128)S(1)}) custom-call(f32[2,3,128,128]{3,2,1,0:T(8,128)} %band_ref.13, bf16[1024,256]{1,0:T(8,128)(2,1)} %get-tuple-element.53.front_ref, ...), custom_call_target="tpu_custom_call" | custom-call | tf_op jit(solution)/shard_map/pallas_call | solution.py:26
  18.3 2.4 %collective-permute-start = (f32[16,128]{1,0:T(8,128)S(1)}, f32[16,128]{1,0:T(8,128)S(1)}, u32[]{:S(2)}, u32[]{:S(2)}) collective-permute-start(f32[16,128]{1,0:T(8,128)S(1)} %get-tuple-element.68), channel_id=1, source_target_pairs={{0,1},{4,5},{8,9},{12,13},{16,17},{20,21},{24,25},{28,29}} | collective-permute-start | bytes 24584 | tf_op jit(solution)/shard_map/ppermute | solution.py:816
  20.7 0.7 %collective-permute-start.4 = (f32[2,16,128]{2,1,0:T(8,128)S(1)}, f32[2,16,128]{2,1,0:T(8,128)S(1)}, u32[]{:S(2)}, u32[]{:S(2)}) collective-permute-start(f32[2,16,128]{2,1,0:T(8,128)S(1)} %get-tuple-element.70.load_ref), channel_id=1, source_target_pairs={{3,2},{7,6},{11,10},{15,14},{19,18},{23,22},{27,26},{31,30}} | collective-permute-start | bytes 49160 | tf_op jit(solution)/shard_map/ppermute | solution.py:830
  21.4 0.0 collective-permute-done.1.first_ref.map_ref
  21.4 0.6 %collective-permute-done.got_ref = f32[16,128]{1,0:T(8,128)S(1)} collective-permute-done((f32[16,128]{1,0:T(8,128)S(1)}, f32[16,128]{1,0:T(8,128)S(1)}, u32[]{:S(2)}, u32[]{:S(2)}) %collective-permute-start) | collective-permute-done | bytes 8224 | tf_op jit(solution)/shard_map/ppermute | solution.py:816
  22.0 0.6 %collective-permute-start.2 = (f32[16,128]{1,0:T(8,128)S(1)}, f32[16,128]{1,0:T(8,128)S(1)}, u32[]{:S(2)}, u32[]{:S(2)}) collective-permute-start(f32[16,128]{1,0:T(8,128)S(1)} %get-tuple-element.74), channel_id=1, source_target_pairs={{1,2},{5,6},{9,10},{13,14},{17,18},{21,22},{25,26},{29,30}} | collective-permute-start | bytes 24584 | tf_op jit(solution)/shard_map/ppermute | solution.py:858
  22.7 0.0 collective-permute-done.3.pprev_ref
  22.7 0.2 shard_map.126
  23.0 0.0 collective-permute-done.2.got_ref
  23.0 0.7 %collective-permute-start.5 = (f32[16,128]{1,0:T(8,128)S(1)}, f32[16,128]{1,0:T(8,128)S(1)}, u32[]{:S(2)}, u32[]{:S(2)}) collective-permute-start(f32[16,128]{1,0:T(8,128)S(1)} %get-tuple-element.83), channel_id=1, source_target_pairs={{2,1},{6,5},{10,9},{14,13},{18,17},{22,21},{26,25},{30,29}} | collective-permute-start | bytes 24584 | tf_op jit(solution)/shard_map/ppermute | solution.py:878
  23.7 0.7 %collective-permute-start.7 = (f32[2,16,128]{2,1,0:T(8,128)S(1)}, f32[2,16,128]{2,1,0:T(8,128)S(1)}, u32[]{:S(2)}, u32[]{:S(2)}) collective-permute-start(f32[2,16,128]{2,1,0:T(8,128)S(1)} %get-tuple-element.92), channel_id=1, source_target_pairs={{2,3},{6,7},{10,11},{14,15},{18,19},{22,23},{26,27},{30,31}} | collective-permute-start | bytes 49160 | tf_op jit(solution)/shard_map/ppermute | solution.py:900
  24.4 1.3 %collective-permute-start.6 = (f32[16,128]{1,0:T(8,128)S(1)}, f32[16,128]{1,0:T(8,128)S(1)}, u32[]{:S(2)}, u32[]{:S(2)}) collective-permute-start(f32[16,128]{1,0:T(8,128)S(1)} %get-tuple-element.91), channel_id=1, source_target_pairs={{1,0},{5,4},{9,8},{13,12},{17,16},{21,20},{25,24},{29,28}} | collective-permute-start | bytes 24584 | tf_op jit(solution)/shard_map/ppermute | solution.py:885
  25.7 2.6 %shard_map.131 = (f32[3,16,128]{2,1,0:T(8,128)S(1)}, bf16[3,1024,256]{2,1,0:T(8,128)(2,1)S(1)}, f32[16,128]{1,0:T(8,128)S(1)}, bf16[3,128,256]{2,1,0:T(8,128)(2,1)S(1)}) custom-call(f32[2,3,128,128]{3,2,1,0:T(8,128)} %band_ref.13, f32[3,128,128]{2,1,0:T(8,128)} %radial_ref.3, ...), custom_call_target="tpu_custom_call", output_to_operand_aliasing={{0}: (10, {})} | custom-call | tf_op jit(solution)/shard_map/pallas_call | solution.py:26
  28.3 7.7 %collective-permute-done.6.got_ref = f32[16,128]{1,0:T(8,128)S(1)} collective-permute-done((f32[16,128]{1,0:T(8,128)S(1)}, f32[16,128]{1,0:T(8,128)S(1)}, u32[]{:S(2)}, u32[]{:S(2)}) %collective-permute-start.6) | collective-permute-done | bytes 8224 | tf_op jit(solution)/shard_map/ppermute | solution.py:885
  36.1 0.0 collective-permute-done.7.last_ref
  36.1 1.6 %shard_map.132 = f32[16,3072]{1,0:T(8,128)} custom-call(f32[3,7,16,128]{3,2,1,0:T(8,128)S(1)} %get-tuple-element.66.zsrc_ref, f32[3,7,16,128]{3,2,1,0:T(8,128)S(1)} %get-tuple-element.67.inv_ref, f32[2,16,128]{2,1,0:T(8,128)S(1)} %get-tuple-element.90.state_ref, f32[16,128]{1,0:T(8,128)S(1)} %collective-permute-done.6.got_ref, ...), custom_call_target="tpu_custom_call" | custom-call | tf_op jit(solution)/shard_map/pallas_call | solution.py:26
  (10 shorter events, 0.1 us)
Async XLA Ops:
  2.2 19.2 %collective-permute-start.1 = (f32[8,128,128]{2,1,0:T(8,128)}, f32[8,128,128]{2,1,0:T(8,128)S(1)}, u32[]{:S(2)}, u32[]{:S(2)}) collective-permute-start(f32[8,128,128]{2,1,0:T(8,128)} %get-tuple-element.69), channel_id=1, source_target_pairs={{0,1},{3,2},{4,5},{7,6},{8,9},{11,10},{12,13},{15,14},{16,17},{19,... | collective-permute-start | bytes 1572872 | tf_op jit(solution)/shard_map/ppermute | solution.py:750
  5.1 17.6 %collective-permute-start.3 = (f32[8,128,128]{2,1,0:T(8,128)}, f32[8,128,128]{2,1,0:T(8,128)}, u32[]{:S(2)}, u32[]{:S(2)}) collective-permute-start(f32[8,128,128]{2,1,0:T(8,128)} %get-tuple-element.75), channel_id=1, source_target_pairs={{1,2},{5,6},{9,10},{13,14},{17,18},{21,22},{25,26},{29,30}} | collective-permute-start | bytes 1572872 | tf_op jit(solution)/shard_map/ppermute | solution.py:761
  6.6 10.0 %all-to-all-start = ((f32[8,16,384]{2,1,0:T(8,128)}), f32[8,16,384]{2,1,0:T(8,128)S(1)}, u32[]{:S(2)}, u32[]{:S(2)}) async-start(f32[8,16,384]{2,1,0:T(8,128)} %bitcast.1), calls=%async_computation | async-start | bytes 393216 | tf_op jit(solution)/shard_map/all_to_all | solution.py:770
  18.3 3.8 %collective-permute-start = (f32[16,128]{1,0:T(8,128)S(1)}, f32[16,128]{1,0:T(8,128)S(1)}, u32[]{:S(2)}, u32[]{:S(2)}) collective-permute-start(f32[16,128]{1,0:T(8,128)S(1)} %get-tuple-element.68), channel_id=1, source_target_pairs={{0,1},{4,5},{8,9},{12,13},{16,17},{20,21},{24,25},{28,29}} | collective-permute-start | bytes 24584 | tf_op jit(solution)/shard_map/ppermute | solution.py:816
  20.7 2.2 %collective-permute-start.4 = (f32[2,16,128]{2,1,0:T(8,128)S(1)}, f32[2,16,128]{2,1,0:T(8,128)S(1)}, u32[]{:S(2)}, u32[]{:S(2)}) collective-permute-start(f32[2,16,128]{2,1,0:T(8,128)S(1)} %get-tuple-element.70.load_ref), channel_id=1, source_target_pairs={{3,2},{7,6},{11,10},{15,14},{19,18},{23,22},{27,26},{31,30}} | collective-permute-start | bytes 49160 | tf_op jit(solution)/shard_map/ppermute | solution.py:830
  22.0 0.9 %collective-permute-start.2 = (f32[16,128]{1,0:T(8,128)S(1)}, f32[16,128]{1,0:T(8,128)S(1)}, u32[]{:S(2)}, u32[]{:S(2)}) collective-permute-start(f32[16,128]{1,0:T(8,128)S(1)} %get-tuple-element.74), channel_id=1, source_target_pairs={{1,2},{5,6},{9,10},{13,14},{17,18},{21,22},{25,26},{29,30}} | collective-permute-start | bytes 24584 | tf_op jit(solution)/shard_map/ppermute | solution.py:858
  23.0 1.4 %collective-permute-start.5 = (f32[16,128]{1,0:T(8,128)S(1)}, f32[16,128]{1,0:T(8,128)S(1)}, u32[]{:S(2)}, u32[]{:S(2)}) collective-permute-start(f32[16,128]{1,0:T(8,128)S(1)} %get-tuple-element.83), channel_id=1, source_target_pairs={{2,1},{6,5},{10,9},{14,13},{18,17},{22,21},{26,25},{30,29}} | collective-permute-start | bytes 24584 | tf_op jit(solution)/shard_map/ppermute | solution.py:878
  23.7 12.4 %collective-permute-start.7 = (f32[2,16,128]{2,1,0:T(8,128)S(1)}, f32[2,16,128]{2,1,0:T(8,128)S(1)}, u32[]{:S(2)}, u32[]{:S(2)}) collective-permute-start(f32[2,16,128]{2,1,0:T(8,128)S(1)} %get-tuple-element.92), channel_id=1, source_target_pairs={{2,3},{6,7},{10,11},{14,15},{18,19},{22,23},{26,27},{30,31}} | collective-permute-start | bytes 49160 | tf_op jit(solution)/shard_map/ppermute | solution.py:900
  24.4 11.6 %collective-permute-start.6 = (f32[16,128]{1,0:T(8,128)S(1)}, f32[16,128]{1,0:T(8,128)S(1)}, u32[]{:S(2)}, u32[]{:S(2)}) collective-permute-start(f32[16,128]{1,0:T(8,128)S(1)} %get-tuple-element.91), channel_id=1, source_target_pairs={{1,0},{5,4},{9,8},{13,12},{17,16},{21,20},{25,24},{29,28}} | collective-permute-start | bytes 24584 | tf_op jit(solution)/shard_map/ppermute | solution.py:885

commit v7 on v6

--- a/solution.py
+++ b/solution.py
@@ -59,9 +59,9 @@
 
 
 def by_mode(x, modes):
-    mode_of = lax.broadcasted_iota(jnp.int32, x.shape, 0) // 2
-    spread = jnp.concatenate([jnp.where(mode_of == k, x, 0.0) for k in range(modes)], axis=1)
-    return tall(spread)
+    both = tall(x)
+    mode_of = lax.broadcasted_iota(jnp.int32, both.shape, 0) % x.shape[0] // 2
+    return jnp.concatenate([jnp.where(mode_of == k, both, jnp.zeros_like(both)) for k in range(modes)], axis=1)
 
 
 def folded(out, rows):
@@ -236,7 +236,7 @@
                 w_ref[place.at("face", 4 * j + 2 * side + i)] = dot(onehot, both).astype(BF16)
     copies[4].wait()
     for j in range(1, slabs):
-        bands = band_wide(band_buf[0, j], band_buf[1, j])
+        bands = band_wide(band_buf[0, j].T, band_buf[1, j].T)
         for i in range(2):
             w_ref[place.at("band", 2 * (j - 1) + i)] = bands[:, 2 * i * size : 2 * (i + 1) * size]
     for j in range(slabs):
@@ -313,10 +313,6 @@
     per = spec_ref.shape[2] // size
     at = index % per * size
     return spec_ref[index // per, :, at : at + size]
-
-
-def band_step(values, weight, lam):
-    return face_push(values, weight, lam)
 
 
 def inner_kernel(modes, mode_total, place, hub, first_call, band_ref, front_ref, behind_ref, *refs):
@@ -397,7 +393,7 @@
         panel = w_ref[place.at("panel", j)]
         solved_ref[j] = reduced
         if j > 0:
-            reduced = reduced - band_step(values[-1], place.band(w_ref, j), lam)
+            reduced = reduced - face_lift(values[-1], place.band(w_ref, j), lam)
         values.append(apply(reduced, panel, modes))
         y_ref[j] = values[j]
     return load, values
@@ -460,12 +456,12 @@
         panels = [w_ref[place.at("panel", j)] for j in range(slabs)]
         values = []
         for j in range(slabs):
-            step = face_push(values[-1] if j > 0 else state_ref[0], bands[j], lam)
+            step = face_lift(values[-1], bands[j], lam) if j > 0 else face_push(state_ref[0], first, lam)
             values.append(apply(reduced_ref[j] - step, panels[j], modes))
         found = values[-1]
         found_ref[slabs - 1] = found
         for j in range(slabs - 2, -1, -1):
-            found = values[j] - apply(face_lift(found, bands[j + 1], lam), panels[j], modes)
+            found = values[j] - apply(face_push(found, bands[j + 1], lam), panels[j], modes)
             found_ref[j] = found
         base_ref[...] = load_ref[1] + face_lift(found, first, lam)
         copies[1].wait()

time: 38.3 us -> 38.4 us (level)
  no operation moved by 1% of the time
where the time goes in v7:
time: 38.4 us; the launch traced here: 38 us
  starting transfers between devices  14.5 us (38%)
  Pallas kernels  11.9 us (31%)
  waiting for transfers between devices  11.2 us (29%)
    pallas_call x15, Pallas kernels, call(): pl.pallas_call(kernel, out_shape=outs, in_specs=[ANY] * free + [HBM] * an...  11.9 us
    ppermute x1, waiting for transfers between devices, body(): got = lax.ppermute(send, 'elem', [(1, 0)])  7.72 us
    all_to_all x1, starting transfers between devices, body(): lax.all_to_all(spectrum.reshape(devices, rows, nodes), 'mode', 0, 0, tile...  3.74 us
    all_to_all x1, waiting for transfers between devices, body(): lax.all_to_all(spectrum.reshape(devices, rows, nodes), 'mode', 0, 0, tile...  2.89 us
    ppermute x1, starting transfers between devices, body(): first = far_map = lax.ppermute(ship, 'elem', [(0, 1), (last, hub)])  2.8 us
    ppermute x1, starting transfers between devices, body(): got = lax.ppermute(send, 'elem', [(0, 1)])  2.56 us
    ppermute x1, starting transfers between devices, body(): lax.ppermute(ship, 'elem', [(i, i + 1) for i in range(1, hub)])  1.46 us
    ppermute x1, starting transfers between devices, body(): got = lax.ppermute(send, 'elem', [(1, 0)])  1.29 us
  transfers between devices with their start and end apart: 9, of which 3 were waited for; matrix products, arithmetic and copies ran while one was open for 0% of the time, Pallas kernels for 21%

profile of v7, /device:TPU:0, one launch (start us, length us, event | category | flops | bytes accessed | tf_op | source)
XLA Modules:
  0.0 38.0 jit_solution(6304036769080153262)
XLA Ops:
  0.0 2.2 %shard_map.119 = (f32[8,128,128]{2,1,0:T(8,128)}, f32[128,384]{1,0:T(8,128)}) custom-call(f32[8,3,128,128]{3,2,1,0:T(8,128)} %panels_ref.5, f32[2,3,128,128]{3,2,1,0:T(8,128)} %band_ref.13, f32[128,384]{1,0:T(8,128)} %rhs_ref.5, bf16[128,384]{1,0:T(8,128)(2,1)} %constant.19.table_ref), custom_call_target="tpu_custom_call" | custom-call | tf_op jit(solution)/shard_map/pallas_call | solution.py:26
  2.2 2.8 %collective-permute-start.1 = (f32[8,128,128]{2,1,0:T(8,128)}, f32[8,128,128]{2,1,0:T(8,128)S(1)}, u32[]{:S(2)}, u32[]{:S(2)}) collective-permute-start(f32[8,128,128]{2,1,0:T(8,128)} %get-tuple-element.69), channel_id=1, source_target_pairs={{0,1},{3,2},{4,5},{7,6},{8,9},{11,10},{12,13},{15,14},{16,17},{19,... | collective-permute-start | bytes 1572872 | tf_op jit(solution)/shard_map/ppermute | solution.py:746
  5.0 0.1 shard_map.120
  5.1 1.5 %collective-permute-start.3 = (f32[8,128,128]{2,1,0:T(8,128)}, f32[8,128,128]{2,1,0:T(8,128)}, u32[]{:S(2)}, u32[]{:S(2)}) collective-permute-start(f32[8,128,128]{2,1,0:T(8,128)} %get-tuple-element.75), channel_id=1, source_target_pairs={{1,2},{5,6},{9,10},{13,14},{17,18},{21,22},{25,26},{29,30}} | collective-permute-start | bytes 1572872 | tf_op jit(solution)/shard_map/ppermute | solution.py:757
  6.6 0.1 shard_map.121
  6.6 3.7 %all-to-all-start = ((f32[8,16,384]{2,1,0:T(8,128)}), f32[8,16,384]{2,1,0:T(8,128)S(1)}, u32[]{:S(2)}, u32[]{:S(2)}) async-start(f32[8,16,384]{2,1,0:T(8,128)} %bitcast.1), calls=%async_computation | async-start | bytes 393216 | tf_op jit(solution)/shard_map/all_to_all | solution.py:766
  10.4 3.3 %shard_map.118 = (bf16[1024,256]{1,0:T(8,128)(2,1)}, bf16[1024,256]{1,0:T(8,128)(2,1)}, bf16[2,1024,256]{2,1,0:T(8,128)(2,1)}, bf16[5504,256]{1,0:T(8,128)(2,1)S...) custom-call(f32[8,3,128,128]{3,2,1,0:T(8,128)} %panels_ref.5, ...), custom_call_target="tpu_custom_call" | custom-call | tf_op jit(solution)/shard_map/pallas_call | solution.py:26
  13.7 2.9 %all-to-all-done.refs_0_ = f32[8,16,384]{2,1,0:T(8,128)S(1)} async-done(((f32[8,16,384]{2,1,0:T(8,128)}), f32[8,16,384]{2,1,0:T(8,128)S(1)}, u32[]{:S(2)}, u32[]{:S(2)}) %all-to-all-start) | async-done | bytes 196640 | tf_op jit(solution)/shard_map/all_to_all | solution.py:766
  16.6 1.6 %shard_map.122 = (f32[3,7,16,128]{3,2,1,0:T(8,128)S(1)}, f32[3,7,16,128]{3,2,1,0:T(8,128)S(1)}, f32[3,16,128]{2,1,0:T(8,128)S(1)}, f32[3,16,128]{2,1,0:T(8,128)S(1)}, f32[16,128]{1,0:T(8,128)S(1)}) custom-call(f32[2,3,128,128]{3,2,1,0:T(8,128)} %band_ref.13, bf16[1024,256]{1,0:T(8,128)(2,1)} %get-tuple-element.53.front_ref, ...), custom_call_target="tpu_custom_call" | custom-call | tf_op jit(solution)/shard_map/pallas_call | solution.py:26
  18.2 2.6 %collective-permute-start = (f32[16,128]{1,0:T(8,128)S(1)}, f32[16,128]{1,0:T(8,128)S(1)}, u32[]{:S(2)}, u32[]{:S(2)}) collective-permute-start(f32[16,128]{1,0:T(8,128)S(1)} %get-tuple-element.68), channel_id=1, source_target_pairs={{0,1},{4,5},{8,9},{12,13},{16,17},{20,21},{24,25},{28,29}} | collective-permute-start | bytes 24584 | tf_op jit(solution)/shard_map/ppermute | solution.py:812
  20.8 0.7 %collective-permute-start.4 = (f32[2,16,128]{2,1,0:T(8,128)S(1)}, f32[2,16,128]{2,1,0:T(8,128)S(1)}, u32[]{:S(2)}, u32[]{:S(2)}) collective-permute-start(f32[2,16,128]{2,1,0:T(8,128)S(1)} %get-tuple-element.70.load_ref), channel_id=1, source_target_pairs={{3,2},{7,6},{11,10},{15,14},{19,18},{23,22},{27,26},{31,30}} | collective-permute-start | bytes 49160 | tf_op jit(solution)/shard_map/ppermute | solution.py:826
  21.5 0.0 collective-permute-done.1.first_ref.map_ref
  21.6 0.6 %collective-permute-done.got_ref = f32[16,128]{1,0:T(8,128)S(1)} collective-permute-done((f32[16,128]{1,0:T(8,128)S(1)}, f32[16,128]{1,0:T(8,128)S(1)}, u32[]{:S(2)}, u32[]{:S(2)}) %collective-permute-start) | collective-permute-done | bytes 8224 | tf_op jit(solution)/shard_map/ppermute | solution.py:812
  22.1 0.6 %collective-permute-start.2 = (f32[16,128]{1,0:T(8,128)S(1)}, f32[16,128]{1,0:T(8,128)S(1)}, u32[]{:S(2)}, u32[]{:S(2)}) collective-permute-start(f32[16,128]{1,0:T(8,128)S(1)} %get-tuple-element.74), channel_id=1, source_target_pairs={{1,2},{5,6},{9,10},{13,14},{17,18},{21,22},{25,26},{29,30}} | collective-permute-start | bytes 24584 | tf_op jit(solution)/shard_map/ppermute | solution.py:854
  22.8 0.0 collective-permute-done.3.pprev_ref
  22.8 0.2 shard_map.126
  23.1 0.0 collective-permute-done.2.got_ref
  23.1 0.7 %collective-permute-start.5 = (f32[16,128]{1,0:T(8,128)S(1)}, f32[16,128]{1,0:T(8,128)S(1)}, u32[]{:S(2)}, u32[]{:S(2)}) collective-permute-start(f32[16,128]{1,0:T(8,128)S(1)} %get-tuple-element.83), channel_id=1, source_target_pairs={{2,1},{6,5},{10,9},{14,13},{18,17},{22,21},{26,25},{30,29}} | collective-permute-start | bytes 24584 | tf_op jit(solution)/shard_map/ppermute | solution.py:874
  23.8 0.7 %collective-permute-start.7 = (f32[2,16,128]{2,1,0:T(8,128)S(1)}, f32[2,16,128]{2,1,0:T(8,128)S(1)}, u32[]{:S(2)}, u32[]{:S(2)}) collective-permute-start(f32[2,16,128]{2,1,0:T(8,128)S(1)} %get-tuple-element.92), channel_id=1, source_target_pairs={{2,3},{6,7},{10,11},{14,15},{18,19},{22,23},{26,27},{30,31}} | collective-permute-start | bytes 49160 | tf_op jit(solution)/shard_map/ppermute | solution.py:896
  24.5 1.3 %collective-permute-start.6 = (f32[16,128]{1,0:T(8,128)S(1)}, f32[16,128]{1,0:T(8,128)S(1)}, u32[]{:S(2)}, u32[]{:S(2)}) collective-permute-start(f32[16,128]{1,0:T(8,128)S(1)} %get-tuple-element.91), channel_id=1, source_target_pairs={{1,0},{5,4},{9,8},{13,12},{17,16},{21,20},{25,24},{29,28}} | collective-permute-start | bytes 24584 | tf_op jit(solution)/shard_map/ppermute | solution.py:881
  25.8 2.6 %shard_map.131 = (f32[3,16,128]{2,1,0:T(8,128)S(1)}, bf16[3,1024,256]{2,1,0:T(8,128)(2,1)S(1)}, f32[16,128]{1,0:T(8,128)S(1)}, bf16[3,128,256]{2,1,0:T(8,128)(2,1)S(1)}) custom-call(f32[2,3,128,128]{3,2,1,0:T(8,128)} %band_ref.13, f32[3,128,128]{2,1,0:T(8,128)} %radial_ref.3, ...), custom_call_target="tpu_custom_call", output_to_operand_aliasing={{0}: (10, {})} | custom-call | tf_op jit(solution)/shard_map/pallas_call | solution.py:26
  28.5 7.7 %collective-permute-done.6.got_ref = f32[16,128]{1,0:T(8,128)S(1)} collective-permute-done((f32[16,128]{1,0:T(8,128)S(1)}, f32[16,128]{1,0:T(8,128)S(1)}, u32[]{:S(2)}, u32[]{:S(2)}) %collective-permute-start.6) | collective-permute-done | bytes 8224 | tf_op jit(solution)/shard_map/ppermute | solution.py:881
  36.2 0.0 collective-permute-done.7.last_ref
  36.2 1.6 %shard_map.132 = f32[16,3072]{1,0:T(8,128)} custom-call(f32[3,7,16,128]{3,2,1,0:T(8,128)S(1)} %get-tuple-element.66.zsrc_ref, f32[3,7,16,128]{3,2,1,0:T(8,128)S(1)} %get-tuple-element.67.inv_ref, f32[2,16,128]{2,1,0:T(8,128)S(1)} %get-tuple-element.90.state_ref, f32[16,128]{1,0:T(8,128)S(1)} %collective-permute-done.6.got_ref, ...), custom_call_target="tpu_custom_call" | custom-call | tf_op jit(solution)/shard_map/pallas_call | solution.py:26
  (10 shorter events, 0.1 us)
Async XLA Ops:
  2.2 19.3 %collective-permute-start.1 = (f32[8,128,128]{2,1,0:T(8,128)}, f32[8,128,128]{2,1,0:T(8,128)S(1)}, u32[]{:S(2)}, u32[]{:S(2)}) collective-permute-start(f32[8,128,128]{2,1,0:T(8,128)} %get-tuple-element.69), channel_id=1, source_target_pairs={{0,1},{3,2},{4,5},{7,6},{8,9},{11,10},{12,13},{15,14},{16,17},{19,... | collective-permute-start | bytes 1572872 | tf_op jit(solution)/shard_map/ppermute | solution.py:746
  5.1 17.7 %collective-permute-start.3 = (f32[8,128,128]{2,1,0:T(8,128)}, f32[8,128,128]{2,1,0:T(8,128)}, u32[]{:S(2)}, u32[]{:S(2)}) collective-permute-start(f32[8,128,128]{2,1,0:T(8,128)} %get-tuple-element.75), channel_id=1, source_target_pairs={{1,2},{5,6},{9,10},{13,14},{17,18},{21,22},{25,26},{29,30}} | collective-permute-start | bytes 1572872 | tf_op jit(solution)/shard_map/ppermute | solution.py:757
  6.6 10.0 %all-to-all-start = ((f32[8,16,384]{2,1,0:T(8,128)}), f32[8,16,384]{2,1,0:T(8,128)S(1)}, u32[]{:S(2)}, u32[]{:S(2)}) async-start(f32[8,16,384]{2,1,0:T(8,128)} %bitcast.1), calls=%async_computation | async-start | bytes 393216 | tf_op jit(solution)/shard_map/all_to_all | solution.py:766
  18.2 3.9 %collective-permute-start = (f32[16,128]{1,0:T(8,128)S(1)}, f32[16,128]{1,0:T(8,128)S(1)}, u32[]{:S(2)}, u32[]{:S(2)}) collective-permute-start(f32[16,128]{1,0:T(8,128)S(1)} %get-tuple-element.68), channel_id=1, source_target_pairs={{0,1},{4,5},{8,9},{12,13},{16,17},{20,21},{24,25},{28,29}} | collective-permute-start | bytes 24584 | tf_op jit(solution)/shard_map/ppermute | solution.py:812
  20.8 2.2 %collective-permute-start.4 = (f32[2,16,128]{2,1,0:T(8,128)S(1)}, f32[2,16,128]{2,1,0:T(8,128)S(1)}, u32[]{:S(2)}, u32[]{:S(2)}) collective-permute-start(f32[2,16,128]{2,1,0:T(8,128)S(1)} %get-tuple-element.70.load_ref), channel_id=1, source_target_pairs={{3,2},{7,6},{11,10},{15,14},{19,18},{23,22},{27,26},{31,30}} | collective-permute-start | bytes 49160 | tf_op jit(solution)/shard_map/ppermute | solution.py:826
  22.1 0.9 %collective-permute-start.2 = (f32[16,128]{1,0:T(8,128)S(1)}, f32[16,128]{1,0:T(8,128)S(1)}, u32[]{:S(2)}, u32[]{:S(2)}) collective-permute-start(f32[16,128]{1,0:T(8,128)S(1)} %get-tuple-element.74), channel_id=1, source_target_pairs={{1,2},{5,6},{9,10},{13,14},{17,18},{21,22},{25,26},{29,30}} | collective-permute-start | bytes 24584 | tf_op jit(solution)/shard_map/ppermute | solution.py:854
  23.1 1.4 %collective-permute-start.5 = (f32[16,128]{1,0:T(8,128)S(1)}, f32[16,128]{1,0:T(8,128)S(1)}, u32[]{:S(2)}, u32[]{:S(2)}) collective-permute-start(f32[16,128]{1,0:T(8,128)S(1)} %get-tuple-element.83), channel_id=1, source_target_pairs={{2,1},{6,5},{10,9},{14,13},{18,17},{22,21},{26,25},{30,29}} | collective-permute-start | bytes 24584 | tf_op jit(solution)/shard_map/ppermute | solution.py:874
  23.8 12.4 %collective-permute-start.7 = (f32[2,16,128]{2,1,0:T(8,128)S(1)}, f32[2,16,128]{2,1,0:T(8,128)S(1)}, u32[]{:S(2)}, u32[]{:S(2)}) collective-permute-start(f32[2,16,128]{2,1,0:T(8,128)S(1)} %get-tuple-element.92), channel_id=1, source_target_pairs={{2,3},{6,7},{10,11},{14,15},{18,19},{22,23},{26,27},{30,31}} | collective-permute-start | bytes 49160 | tf_op jit(solution)/shard_map/ppermute | solution.py:896
  24.5 11.6 %collective-permute-start.6 = (f32[16,128]{1,0:T(8,128)S(1)}, f32[16,128]{1,0:T(8,128)S(1)}, u32[]{:S(2)}, u32[]{:S(2)}) collective-permute-start(f32[16,128]{1,0:T(8,128)S(1)} %get-tuple-element.91), channel_id=1, source_target_pairs={{1,0},{5,4},{9,8},{13,12},{17,16},{21,20},{25,24},{29,28}} | collective-permute-start | bytes 24584 | tf_op jit(solution)/shard_map/ppermute | solution.py:881
